TPU v7x, 512 devices: a whole 4x8x8 slice. The times are simulated.
512 devices in a mesh: occ: 8 (over x, core), aux: 16 (over y_lo, z), vir: 4 (over y_hi).
Axes of the slice: x: 4, y: 8 (y_hi: 4, y_lo: 2; y = y_hi * 2 + y_lo), z: 8, core: 2. Of those that a mesh axis runs over, the one named last changes fastest.
Arguments:
- bq: float32 [8, 10112, 3072], P('occ', 'aux', 'vir'), may hold values from -1.5 to 1.5
- eps_occ: float32 [8], replicated, may hold values from -1.5 to -0.3
- eps_vir: float32 [3072], P('vir'), may hold values from 0.2 to 3
- tile_pairs: int32 [8, 8, 4, 2], P('occ', None, 'vir'), may hold values from 0 to 35, as said below
- live_counts: int32 [8, 8], P('occ'), may hold values from 1 to 2, as said below
Outputs:
- gamma: float32 [8, 10112, 3072], P('occ', 'aux', 'vir')
- pair_energy: float32 [8, 8], P('occ')
Inputs may be any that keep to these rules, and one draw needn't show every extreme that they name: `tile_pairs`: the 2 entries of one list are distinct. `live_counts`: every occupied orbital i has some j with all 2 slots live.
All inputs are finite; a program needn't handle non-finite values.
Results may differ from a plain program's by a relative error of at most 0.0003.
Values sent between devices are 32-bit elements; how exact they have to be, the bound alone decides.
No kernel may reach another device: no remote copies, remote signals or barrier semaphores. Data moves between devices by JAX's collectives and lax.ppermute only.
A program may use at most 64 MiB of HBM per device.

v0:
```python
import jax
import jax.numpy as jnp
from jax import lax
from jax.sharding import PartitionSpec as P

TILE = 128


def passed_along(value, axis, by):
    count = lax.axis_size(axis)
    return lax.ppermute(value, axis, [(i, (i + by) % count) for i in range(count)])


def per_device(bq, eps_occ, eps_vir, tile_pairs, live_counts):
    highest = lax.Precision.HIGHEST
    cycle_size = lax.axis_size("occ")
    cycle_index = lax.axis_index("occ")
    aux_rows = bq.shape[1]
    vir_cols = bq.shape[2]
    tile_count = vir_cols // TILE
    slot_total = tile_pairs.shape[3]
    local_block = bq[0]
    local_tiles = local_block.reshape(aux_rows, tile_count, TILE)
    vir_levels = eps_vir.reshape(tile_count, TILE)
    chosen_rows = tile_pairs[0, :, 0, :]
    count_row = live_counts[0]
    occ_level = jnp.take(eps_occ, cycle_index)
    slot_index = jnp.arange(slot_total)
    orbital_index = jnp.arange(cycle_size)

    def block_columns(arrived, partner):
        chosen = jnp.take(chosen_rows, partner, axis=0)
        return jnp.take(arrived.reshape(aux_rows, tile_count, TILE), chosen % tile_count, axis=1)

    def visit_pair(totals, right_cols, partner):
        gamma_sum, energy = totals
        chosen = jnp.take(chosen_rows, partner, axis=0)
        first_tile = chosen // tile_count
        second_tile = chosen % tile_count
        left_cols = jnp.take(local_tiles, first_tile, axis=1)
        coulomb_part = jnp.einsum("pkx,pky->kxy", left_cols, right_cols, precision=highest)
        live_slots = (slot_index < jnp.take(count_row, partner)).astype(jnp.float32)
        pair_level = occ_level + jnp.take(eps_occ, partner)
        vir_first = jnp.take(vir_levels, first_tile, axis=0)
        vir_second = jnp.take(vir_levels, second_tile, axis=0)
        summed = lax.psum(coulomb_part, "aux")
        denominator = pair_level - vir_first[:, :, None] - vir_second[:, None, :]
        amplitude = summed / denominator * live_slots[:, None, None]
        weight = jnp.sum(summed * amplitude)
        contribution = jnp.einsum("kxy,pky->kpx", amplitude, right_cols, precision=highest)
        for slot in range(slot_total):
            start_tile = first_tile[slot]
            current = lax.dynamic_slice_in_dim(gamma_sum, start_tile, 1, 1)
            updated = current + contribution[slot][:, None, :]
            gamma_sum = lax.dynamic_update_slice_in_dim(gamma_sum, updated, start_tile, 1)
        pair_mask = (orbital_index == partner).astype(jnp.float32)
        return (gamma_sum, energy + weight * pair_mask)

    totals = (
        jnp.zeros((aux_rows, tile_count, TILE), jnp.float32),
        jnp.zeros((cycle_size,), jnp.float32),
    )
    totals = visit_pair(totals, block_columns(local_block, cycle_index), cycle_index)
    carried = local_block
    for stride in range(1, cycle_size):
        carried = passed_along(carried, "occ", 1)
        partner = (cycle_index - stride) % cycle_size
        totals = visit_pair(totals, block_columns(carried, partner), partner)
    gamma_sum, energy = totals
    energy = lax.psum(energy, "vir")
    return (gamma_sum.reshape(1, aux_rows, vir_cols), energy.reshape(1, cycle_size))


def solution(mesh):
    return jax.shard_map(
        per_device,
        mesh=mesh,
        in_specs=(
            P("occ", "aux", "vir"),
            P(),
            P("vir"),
            P("occ", None, "vir", None),
            P("occ", None),
        ),
        out_specs=(P("occ", "aux", "vir"), P("occ", None)),
        check_vma=False,
    )
```

profile of v0, /device:TPU:6, one launch (start us, length us, event | category | flops | bytes accessed | tf_op | source)
XLA Modules:
  0.0 443.0 jit_solution(3141516488970205298)
XLA Ops:
  7.3 24.1 %collective-permute-done = f32[632,768]{1,0:T(8,128)} collective-permute-done((f32[632,768]{1,0:T(8,128)}, f32[632,768]{1,0:T(8,128)}, u32[]{:S(2)}, u32[]{:S(2)}) %collective-permute-start) | collective-permute-done | bytes 1941536 | tf_op jit(solution)/shard_map/ppermute | solution.py:11
  31.3 3.5 collective-permute-start.1
  34.8 1.6 constant_dynamic-slice_fusion.3
  37.8 1.3 fusion.166
  39.1 16.2 %collective-permute-done.1 = f32[632,768]{1,0:T(8,128)S(1)} collective-permute-done((f32[632,768]{1,0:T(8,128)}, f32[632,768]{1,0:T(8,128)S(1)}, u32[]{:S(2)}, u32[]{:S(2)}) %collective-permute-start.1) | collective-permute-done | bytes 1941536 | tf_op jit(solution)/shard_map/ppermute | solution.py:11
  55.3 4.8 %collective-permute-start.2 = (f32[632,768]{1,0:T(8,128)S(1)}, f32[632,768]{1,0:T(8,128)S(1)}, u32[]{:S(2)}, u32[]{:S(2)}) collective-permute-start(f32[632,768]{1,0:T(8,128)S(1)} %collective-permute-done.1), channel_id=1, source_target_pairs={{0,64},{64,128},{128,192},{192,256},{256,320},{320,384},{384,448},... | collective-permute-start | bytes 5824520 | tf_op jit(solution)/shard_map/ppermute | solution.py:11
  61.0 18.1 %collective-permute-done.2 = f32[632,768]{1,0:T(8,128)S(1)} collective-permute-done((f32[632,768]{1,0:T(8,128)S(1)}, f32[632,768]{1,0:T(8,128)S(1)}, u32[]{:S(2)}, u32[]{:S(2)}) %collective-permute-start.2) | collective-permute-done | bytes 1941536 | tf_op jit(solution)/shard_map/ppermute | solution.py:11
  80.4 5.9 %collective-permute-start.3 = (f32[632,768]{1,0:T(8,128)S(1)}, f32[632,768]{1,0:T(8,128)}, u32[]{:S(2)}, u32[]{:S(2)}) collective-permute-start(f32[632,768]{1,0:T(8,128)S(1)} %collective-permute-done.2), channel_id=1, source_target_pairs={{0,64},{64,128},{128,192},{192,256},{256,320},{320,384},{384,448},... | collective-permute-start | bytes 5824520 | tf_op jit(solution)/shard_map/ppermute | solution.py:11
  87.1 17.2 %collective-permute-done.3 = f32[632,768]{1,0:T(8,128)} collective-permute-done((f32[632,768]{1,0:T(8,128)S(1)}, f32[632,768]{1,0:T(8,128)}, u32[]{:S(2)}, u32[]{:S(2)}) %collective-permute-start.3) | collective-permute-done | bytes 1941536 | tf_op jit(solution)/shard_map/ppermute | solution.py:11
  104.3 7.0 %collective-permute-start.4 = (f32[632,768]{1,0:T(8,128)}, f32[632,768]{1,0:T(8,128)}, u32[]{:S(2)}, u32[]{:S(2)}) collective-permute-start(f32[632,768]{1,0:T(8,128)} %collective-permute-done.3), channel_id=1, source_target_pairs={{0,64},{64,128},{128,192},{192,256},{256,320},{320,384},{384,448},... | collective-permute-start | bytes 5824520 | tf_op jit(solution)/shard_map/ppermute | solution.py:11
  118.3 10.1 %collective-permute-done.4 = f32[632,768]{1,0:T(8,128)} collective-permute-done((f32[632,768]{1,0:T(8,128)}, f32[632,768]{1,0:T(8,128)}, u32[]{:S(2)}, u32[]{:S(2)}) %collective-permute-start.4) | collective-permute-done | bytes 1941536 | tf_op jit(solution)/shard_map/ppermute | solution.py:11
  128.4 8.3 %collective-permute-start.5 = (f32[632,768]{1,0:T(8,128)}, f32[632,768]{1,0:T(8,128)}, u32[]{:S(2)}, u32[]{:S(2)}) collective-permute-start(f32[632,768]{1,0:T(8,128)} %collective-permute-done.4), channel_id=1, source_target_pairs={{0,64},{64,128},{128,192},{192,256},{256,320},{320,384},{384,448},... | collective-permute-start | bytes 5824520 | tf_op jit(solution)/shard_map/ppermute | solution.py:11
  137.3 1.7 fusion.200
  147.4 5.1 %collective-permute-done.5 = f32[632,768]{1,0:T(8,128)} collective-permute-done((f32[632,768]{1,0:T(8,128)}, f32[632,768]{1,0:T(8,128)}, u32[]{:S(2)}, u32[]{:S(2)}) %collective-permute-start.5) | collective-permute-done | bytes 1941536 | tf_op jit(solution)/shard_map/ppermute | solution.py:11
  152.5 9.5 %collective-permute-start.6 = (f32[632,768]{1,0:T(8,128)}, f32[632,768]{1,0:T(8,128)}, u32[]{:S(2)}, u32[]{:S(2)}) collective-permute-start(f32[632,768]{1,0:T(8,128)} %collective-permute-done.5), channel_id=1, source_target_pairs={{0,64},{64,128},{128,192},{192,256},{256,320},{320,384},{384,448},... | collective-permute-start | bytes 5824520 | tf_op jit(solution)/shard_map/ppermute | solution.py:11
  162.0 2.9 copy.7
  164.9 1.9 copy.8
  167.4 1.4 gather_fusion.1
  169.4 1.4 gather_fusion.9
  170.8 1.4 gather_fusion.13
  172.3 1.4 gather_fusion.17
  173.7 1.4 gather_fusion.21
  175.2 1.4 gather_fusion.25
  176.6 1.4 gather_fusion.29
  179.3 3.0 fusion.35
  182.3 1.9 copy.10
  184.2 1.8 copy.11
  186.0 2.1 gather_fusion.4
  188.1 2.0 fusion.30
  190.1 1.9 copy.13
  192.0 1.8 copy.14
  193.7 2.1 gather_fusion.8
  196.8 3.1 fusion.25
  199.8 1.9 copy.16
  201.7 1.8 copy.17
  203.5 2.1 gather_fusion.12
  206.5 3.1 fusion.20
  209.6 1.9 copy.19
  211.4 1.8 copy.20
  213.2 2.1 gather_fusion.16
  216.2 3.1 fusion.15
  219.3 1.9 copy.22
  221.2 1.8 copy.23
  222.9 2.1 gather_fusion.20
  225.9 3.0 fusion.10
  229.0 1.9 copy.25
  230.8 1.8 copy.26
  232.6 2.1 gather_fusion.24
  234.8 3.3 fusion.5
  238.0 1.9 copy.28
  239.9 1.8 copy.29
  241.7 2.1 gather_fusion.28
  243.8 3.1 fusion
  282.5 111.9 %all-reduce.3.cloned.1.call-done = (f32[2,128,128]{2,1,0:T(8,128)}, f32[2,128,128]{2,1,0:T(8,128)}, f32[2,128,128]{2,1,0:T(8,128)}, f32[2,128,128]{2,1,0:T(8,128...) async-done(((f32[2,128,128]{2,1,0:T(8,128)}, f32[2,128,128]{2,1,0:T(8,128)}, f32[2,128,128]{2,1,0:T(8,128)}, ...) | async-done | bytes 1048592 | tf_op jit(solution)/shard_map/psum | solution.py:46
  394.4 2.2 fusion.2
  396.6 1.7 multiply_reduce_fusion
  398.3 2.2 fusion.7
  401.2 1.3 fusion.12
  403.3 1.3 fusion.17
  405.3 1.3 fusion.22
  414.5 1.8 copy.31
  416.4 5.0 %fusion.182 = f32[1,8]{1,0:T(1,128)S(1)} fusion(f32[]{:T(128)} %multiply_reduce_fusion, s32[]{:T(128)S(6)} %select_n.329, f32[]{:T(128)} %multiply_reduce_fusion.1, s32[]{:T(128)S(6)} %select_n.321, f32[]{:T(128)} %multiply_reduce_fusion.2, s32[]{:T(128)S(6)} %select_n.313, f32[]{:T(128)} %multiply_reduce_fusion.3, s32[]{:T(128)S(6)} %select_n.305, ...), kind=kLoop, calls=%fused_computation.358 | loop fusion | flops 184 | bytes 96 | tf_op jit(solution)/shard_map/reshape | solution.py:71
  421.4 2.8 copy.32
  424.2 11.9 %psum.71 = f32[1,8]{1,0:T(1,128)} all-reduce(f32[1,8]{1,0:T(1,128)S(1)} %fusion.182), channel_id=1, replica_groups=mesh['occ'=8,'aux'=16,'vir'=4] {'vir'}, use_global_device_ids=true, to_apply=%region_16.20 | all-reduce | flops 8 | bytes 64 | tf_op jit(solution)/shard_map/psum | solution.py:70
  (149 shorter events, 31.4 us)
Async XLA Ops:
  7.2 104.1 %copy-start = (f32[768]{0:T(1024)S(1)}, f32[768]{0:T(1024)}, u32[]{:S(2)}) copy-start(f32[768]{0:T(1024)} %param.13) | copy-start | bytes 9220
  7.2 387.2 %all-reduce.3.cloned.1.call-start = ((), (), s32[]{:S(2)}) async-start(), calls=%async_computation | async-start | bytes 2097152 | tf_op jit(solution)/shard_map/psum | solution.py:46
  7.2 24.1 %collective-permute-start = (f32[632,768]{1,0:T(8,128)}, f32[632,768]{1,0:T(8,128)}, u32[]{:S(2)}, u32[]{:S(2)}) collective-permute-start(f32[632,768]{1,0:T(8,128)} %bitcast.245), channel_id=1, source_target_pairs={{0,64},{64,128},{128,192},{192,256},{256,320},{320,384},{384,448},... | collective-permute-start | bytes 5824520 | tf_op jit(solution)/shard_map/ppermute | solution.py:11
  31.3 24.0 %collective-permute-start.1 = (f32[632,768]{1,0:T(8,128)}, f32[632,768]{1,0:T(8,128)S(1)}, u32[]{:S(2)}, u32[]{:S(2)}) collective-permute-start(f32[632,768]{1,0:T(8,128)} %collective-permute-done), channel_id=1, source_target_pairs={{0,64},{64,128},{128,192},{192,256},{256,320},{320,384},{384,448},... | collective-permute-start | bytes 5824520 | tf_op jit(solution)/shard_map/ppermute | solution.py:11
  55.3 109.6 %copy-start.11 = (f32[632,768]{1,0:T(8,128)}, f32[632,768]{1,0:T(8,128)S(1)}, u32[]{:S(2)}) copy-start(f32[632,768]{1,0:T(8,128)S(1)} %collective-permute-done.1) | copy-start | bytes 5824516
  55.3 23.8 %collective-permute-start.2 = (f32[632,768]{1,0:T(8,128)S(1)}, f32[632,768]{1,0:T(8,128)S(1)}, u32[]{:S(2)}, u32[]{:S(2)}) collective-permute-start(f32[632,768]{1,0:T(8,128)S(1)} %collective-permute-done.1), channel_id=1, source_target_pairs={{0,64},{64,128},{128,192},{192,256},{256,320},{320,384},{384,448},... | collective-permute-start | bytes 5824520 | tf_op jit(solution)/shard_map/ppermute | solution.py:11
  79.1 1.2 copy-start.12
  80.4 23.9 %collective-permute-start.3 = (f32[632,768]{1,0:T(8,128)S(1)}, f32[632,768]{1,0:T(8,128)}, u32[]{:S(2)}, u32[]{:S(2)}) collective-permute-start(f32[632,768]{1,0:T(8,128)S(1)} %collective-permute-done.2), channel_id=1, source_target_pairs={{0,64},{64,128},{128,192},{192,256},{256,320},{320,384},{384,448},... | collective-permute-start | bytes 5824520 | tf_op jit(solution)/shard_map/ppermute | solution.py:11
  104.3 24.1 %collective-permute-start.4 = (f32[632,768]{1,0:T(8,128)}, f32[632,768]{1,0:T(8,128)}, u32[]{:S(2)}, u32[]{:S(2)}) collective-permute-start(f32[632,768]{1,0:T(8,128)} %collective-permute-done.3), channel_id=1, source_target_pairs={{0,64},{64,128},{128,192},{192,256},{256,320},{320,384},{384,448},... | collective-permute-start | bytes 5824520 | tf_op jit(solution)/shard_map/ppermute | solution.py:11
  128.4 24.1 %collective-permute-start.5 = (f32[632,768]{1,0:T(8,128)}, f32[632,768]{1,0:T(8,128)}, u32[]{:S(2)}, u32[]{:S(2)}) collective-permute-start(f32[632,768]{1,0:T(8,128)} %collective-permute-done.4), channel_id=1, source_target_pairs={{0,64},{64,128},{128,192},{192,256},{256,320},{320,384},{384,448},... | collective-permute-start | bytes 5824520 | tf_op jit(solution)/shard_map/ppermute | solution.py:11
  152.5 85.5 %collective-permute-start.6 = (f32[632,768]{1,0:T(8,128)}, f32[632,768]{1,0:T(8,128)}, u32[]{:S(2)}, u32[]{:S(2)}) collective-permute-start(f32[632,768]{1,0:T(8,128)} %collective-permute-done.5), channel_id=1, source_target_pairs={{0,64},{64,128},{128,192},{192,256},{256,320},{320,384},{384,448},... | collective-permute-start | bytes 5824520 | tf_op jit(solution)/shard_map/ppermute | solution.py:11
  195.9 0.9 copy-start.1
  205.6 0.9 copy-start.3
  215.3 0.9 copy-start.5
  225.1 0.8 copy-start.7
  234.7 3.3 copy-start.9
  243.8 154.5 %copy-start.10 = (f32[2,632,128]{2,1,0:T(8,128)S(1)}, f32[2,632,128]{2,1,0:T(8,128)}, u32[]{:S(2)}) copy-start(f32[2,632,128]{2,1,0:T(8,128)} %copy-done.9) | copy-start | bytes 1941508
  247.0 154.2 %copy-start.8 = (f32[2,632,128]{2,1,0:T(8,128)S(1)}, f32[2,632,128]{2,1,0:T(8,128)}, u32[]{:S(2)}) copy-start(f32[2,632,128]{2,1,0:T(8,128)} %copy-done.7) | copy-start | bytes 1941508
  394.4 6.1 %copy-start.19 = (f32[2,128,128]{2,1,0:T(8,128)S(1)}, f32[2,128,128]{2,1,0:T(8,128)}, u32[]{:S(2)}) copy-start(f32[2,128,128]{2,1,0:T(8,128)} %get-tuple-element.208) | copy-start | bytes 393220
  394.4 6.8 %copy-start.18 = (f32[2,128,128]{2,1,0:T(8,128)S(1)}, f32[2,128,128]{2,1,0:T(8,128)}, u32[]{:S(2)}) copy-start(f32[2,128,128]{2,1,0:T(8,128)} %get-tuple-element.207) | copy-start | bytes 393220
  396.6 6.7 %copy-start.6 = (f32[2,632,128]{2,1,0:T(8,128)S(1)}, f32[2,632,128]{2,1,0:T(8,128)}, u32[]{:S(2)}) copy-start(f32[2,632,128]{2,1,0:T(8,128)} %copy-done.5) | copy-start | bytes 1941508
  396.6 6.7 %copy-start.17 = (f32[2,128,128]{2,1,0:T(8,128)S(1)}, f32[2,128,128]{2,1,0:T(8,128)}, u32[]{:S(2)}) copy-start(f32[2,128,128]{2,1,0:T(8,128)} %get-tuple-element.206) | copy-start | bytes 393220
  400.5 4.8 %copy-start.4 = (f32[2,632,128]{2,1,0:T(8,128)S(1)}, f32[2,632,128]{2,1,0:T(8,128)}, u32[]{:S(2)}) copy-start(f32[2,632,128]{2,1,0:T(8,128)} %copy-done.3) | copy-start | bytes 1941508
  400.5 4.8 %copy-start.16 = (f32[2,128,128]{2,1,0:T(8,128)S(1)}, f32[2,128,128]{2,1,0:T(8,128)}, u32[]{:S(2)}) copy-start(f32[2,128,128]{2,1,0:T(8,128)} %get-tuple-element.205) | copy-start | bytes 393220
  402.5 4.9 %copy-start.2 = (f32[2,632,128]{2,1,0:T(8,128)S(1)}, f32[2,632,128]{2,1,0:T(8,128)}, u32[]{:S(2)}) copy-start(f32[2,632,128]{2,1,0:T(8,128)} %copy-done.1) | copy-start | bytes 1941508
  402.5 4.9 %copy-start.15 = (f32[2,128,128]{2,1,0:T(8,128)S(1)}, f32[2,128,128]{2,1,0:T(8,128)}, u32[]{:S(2)}) copy-start(f32[2,128,128]{2,1,0:T(8,128)} %get-tuple-element.204) | copy-start | bytes 393220
  404.5 4.8 %copy-start.14 = (f32[2,128,128]{2,1,0:T(8,128)S(1)}, f32[2,128,128]{2,1,0:T(8,128)}, u32[]{:S(2)}) copy-start(f32[2,128,128]{2,1,0:T(8,128)} %get-tuple-element.203) | copy-start | bytes 393220
  406.6 4.8 %copy-start.13 = (f32[2,128,128]{2,1,0:T(8,128)S(1)}, f32[2,128,128]{2,1,0:T(8,128)}, u32[]{:S(2)}) copy-start(f32[2,128,128]{2,1,0:T(8,128)} %get-tuple-element.202) | copy-start | bytes 393220
Sparse Core Ops, SparseCore 0:
  247.1 147.2 all-reduce.2
where the time goes:
time: 445 us; the launch traced here: 443 us
  waiting for transfers between devices  203 us (46%)
  local copies, waits for them, and re-layouts  83.1 us (19%)
  between operations  54.9 us (12%)
  starting transfers between devices  39.1 us (9%)
  matrix products  35.5 us (8%)
  other arithmetic  15.6 us (4%)
  blocking collectives  11.9 us (3%)
    psum x1, waiting for transfers between devices, visit_pair(): summed = lax.psum(coulomb_part, 'aux')  112 us
    ppermute x7, waiting for transfers between devices, passed_along(): lax.ppermute(value, axis, [(i, (i + by) % count) for i in range(count)])  90.9 us
    ppermute x7, starting transfers between devices, passed_along(): lax.ppermute(value, axis, [(i, (i + by) % count) for i in range(count)])  39.1 us
    dot_general x8, matrix products, visit_pair(): jnp.einsum('pkx,pky->kxy', left_cols, right_cols, precision=highest)  23.6 us
    gather x8, local copies, waits for them, and re-layouts, block_columns(): jnp.take(arrived.reshape(aux_rows, tile_count, TILE), chosen % tile_count...  15.4 us
    ppermute x7, local copies, waits for them, and re-layouts, passed_along(): lax.ppermute(value, axis, [(i, (i + by) % count) for i in range(count)])  13.2 us
    reshape x7, local copies, waits for them, and re-layouts, block_columns(): arrived.reshape(aux_rows, tile_count, TILE)  12.4 us
    psum x1, blocking collectives, per_device(): energy = lax.psum(energy, 'vir')  11.9 us
  transfers between devices with their start and end apart: 8, of which 7 were waited for; matrix products, arithmetic and copies ran while one was open for 21% of the time, Pallas kernels for 0%

commit v1 on v0

v1 whole, which is shorter than its diff:
```python
import functools

import jax
import jax.numpy as jnp
from jax import lax
from jax.experimental import pallas as pl
from jax.experimental.pallas import tpu as pltpu
from jax.sharding import PartitionSpec as P

TILE = 128
VMEM = pl.BlockSpec(memory_space=pltpu.VMEM)
SMEM = pl.BlockSpec(memory_space=pltpu.SMEM)
GROUPS = (
    ((0, 0), (0, 1), (1, 0), (3, 0)),
    ((1, 1), (3, 1), (2, 0), (2, 1)),
)


def params():
    return pltpu.CompilerParams(vmem_limit_bytes=48 * 1024 * 1024)


def cost(flops, moved):
    return pl.CostEstimate(flops=flops, bytes_accessed=moved, transcendentals=0)


def split(value):
    high = value.astype(jnp.bfloat16)
    low = (value - high.astype(jnp.float32)).astype(jnp.bfloat16)
    return high, low


def lanes(index):
    return pl.ds(pl.multiple_of(index * TILE, TILE), TILE)


def pick_kernel(index_ref, block_ref, *out_refs):
    rows = block_ref.shape[0]
    for k, out_ref in enumerate(out_refs):
        for s in range(2):
            out_ref[:rows, s * TILE : (s + 1) * TILE] = block_ref[:, lanes(index_ref[2 * k + s])]
        out_ref[rows:, :] = jnp.zeros((out_ref.shape[0] - rows, 2 * TILE), jnp.float32)


def pick(index, block, count, padded):
    return pl.pallas_call(
        pick_kernel,
        out_shape=[jax.ShapeDtypeStruct((padded, 2 * TILE), jnp.float32)] * count,
        in_specs=[SMEM, VMEM],
        out_specs=[VMEM] * count,
        compiler_params=params(),
        cost_estimate=cost(0, count * padded * 4 * TILE * 4),
        name="pick",
    )(index, block)


def left_kernel(block_ref, out_ref):
    rows = block_ref.shape[0]
    padded = out_ref.shape[2]
    for f in range(out_ref.shape[0]):
        tile = block_ref[:, f * TILE : (f + 1) * TILE]
        tile = jnp.concatenate([tile, jnp.zeros((padded - rows, TILE), jnp.float32)], axis=0)
        high, low = split(tile.T)
        out_ref[f, :TILE, :] = high
        out_ref[f, TILE:, :] = low


def left(block, padded):
    tiles = block.shape[1] // TILE
    return pl.pallas_call(
        left_kernel,
        out_shape=jax.ShapeDtypeStruct((tiles, 2 * TILE, padded), jnp.bfloat16),
        in_specs=[VMEM],
        out_specs=VMEM,
        compiler_params=params(),
        cost_estimate=cost(0, block.size * 8),
        name="left",
    )(block)


def coulomb_kernel(first_ref, left_ref, *refs):
    out_ref = refs[-1]
    for k, right_ref in enumerate(refs[:-1]):
        for s in range(2):
            t = 2 * k + s
            high, low = split(right_ref[:, s * TILE : (s + 1) * TILE])
            both = jnp.concatenate([high, low], axis=1)
            part = jnp.dot(left_ref[first_ref[t]], both, preferred_element_type=jnp.float32)
            cross = part[:TILE, TILE:] + part[TILE:, :TILE] + part[TILE:, TILE:]
            total = part[:TILE, :TILE] + cross
            out_ref[:, 8 * t : 8 * t + 8, :] = total.reshape(TILE // 8, 8, TILE)


def coulomb(first, left_split, rights):
    count = 2 * len(rights)
    padded = rights[0].shape[0]
    return pl.pallas_call(
        coulomb_kernel,
        out_shape=jax.ShapeDtypeStruct((TILE // 8, 8 * count, TILE), jnp.float32),
        in_specs=[SMEM, VMEM] + [VMEM] * len(rights),
        out_specs=VMEM,
        compiler_params=params(),
        cost_estimate=cost(count * 8 * TILE * TILE * padded, count * padded * TILE * 8),
        name="coulomb",
    )(first, left_split, *rights)


def amplitude_kernel(parts_ref, denominator_ref, out_ref):
    summed = jnp.sum(parts_ref[...], axis=0)
    amplitude = summed / denominator_ref[...]
    tiles = summed.shape[0] // 8
    energy = jnp.sum((summed * amplitude).reshape(tiles, 8, TILE), axis=1)
    extra = out_ref.shape[1] - summed.shape[0]
    energy = jnp.concatenate([energy, jnp.zeros((extra - tiles, TILE), jnp.float32)], axis=0) if extra > tiles else energy
    for owner in range(out_ref.shape[0]):
        out_ref[owner, : 8 * tiles, :] = amplitude
        out_ref[owner, 8 * tiles :, :] = energy


def amplitude(parts, denominator):
    owners, rows, _ = parts.shape
    extra = -(-(rows // 8) // 8) * 8
    return pl.pallas_call(
        amplitude_kernel,
        out_shape=jax.ShapeDtypeStruct((owners, rows + extra, TILE), jnp.float32),
        in_specs=[VMEM, VMEM],
        out_specs=VMEM,
        compiler_params=params(),
        cost_estimate=cost(owners * rows * TILE, 2 * owners * rows * TILE * 4),
        name="amplitude",
    )(parts, denominator)


def gamma_kernel(carried, first_ref, amplitude_ref, *refs):
    if carried:
        gamma_in, *refs = refs
    *right_refs, gamma_ref, energy_ref = refs
    rows = gamma_ref.shape[0]
    count = 2 * len(right_refs)
    gamma_ref[...] = gamma_in[...] if carried else jnp.zeros_like(gamma_ref)
    for k, right_ref in enumerate(right_refs):
        for s in range(2):
            t = 2 * k + s
            value = amplitude_ref[:, 8 * t : 8 * t + 8, :].reshape(TILE, TILE)
            high, low = split(value)
            weights = jnp.concatenate(
                [
                    jnp.concatenate([high, high], axis=1),
                    jnp.concatenate([low, low], axis=1),
                ],
                axis=0,
            )
            both = jnp.concatenate(split(right_ref[:, s * TILE : (s + 1) * TILE]), axis=1)
            part = lax.dot_general(both, weights, (((1,), (1,)), ((), ())), preferred_element_type=jnp.float32)
            place = lanes(first_ref[t])
            gamma_ref[:, place] += (part[:, :TILE] + part[:, TILE:])[:rows]
    energy_ref[...] = jnp.sum(amplitude_ref[:, 8 * count :, :], axis=0)


def gamma_add(first, amplitudes, rights, rows, cols, carried):
    count = 2 * len(rights)
    padded = rights[0].shape[0]
    extra = amplitudes.shape[1] - 8 * count
    inputs = (first, amplitudes) + ((carried,) if carried is not None else ())
    return pl.pallas_call(
        functools.partial(gamma_kernel, carried is not None),
        out_shape=[
            jax.ShapeDtypeStruct((rows, cols), jnp.float32),
            jax.ShapeDtypeStruct((extra, TILE), jnp.float32),
        ],
        in_specs=[SMEM] + [VMEM] * (len(inputs) - 1 + len(rights)),
        out_specs=[VMEM, VMEM],
        compiler_params=params(),
        cost_estimate=cost(count * 8 * TILE * TILE * padded, count * padded * TILE * 8),
        name="gamma",
    )(*inputs, *rights)


def per_device(bq, eps_occ, eps_vir, tile_pairs, live_counts):
    occ_size = lax.axis_size("occ")
    me = lax.axis_index("occ")
    chip, core = me // 2, me % 2
    chips = occ_size // 2
    owner = lax.axis_index("aux")
    block = bq[0]
    rows, cols = block.shape
    padded = -(-rows // 16) * 16
    tile_count = cols // TILE
    own_pairs = tile_pairs[0, :, 0, :]
    all_pairs = lax.all_gather(own_pairs, "occ")

    shifts = [shift for group in GROUPS for shift in group]
    receivers = jnp.stack([(chip + dx) % chips * 2 + (core + dc) % 2 for dx, dc in shifts])
    partners = jnp.stack([(chip - dx) % chips * 2 + (core - dc) % 2 for dx, dc in shifts])
    wanted = all_pairs[receivers, me] % tile_count
    chosen = own_pairs[partners]
    first = (chosen // tile_count).astype(jnp.int32)
    second = chosen % tile_count

    left_split = left(block, padded)
    picked = pick(wanted.reshape(-1), block, len(shifts), padded)
    held = {}
    for shift, tiles in zip(shifts, picked):
        dx, dc = shift
        if shift == (0, 0):
            held[shift] = tiles
        else:
            route = [(x * 2 + c, (x + dx) % chips * 2 + (c + dc) % 2) for x in range(chips) for c in range(2)]
            held[shift] = lax.ppermute(tiles, "occ", route)

    vir_rows = eps_vir.reshape(tile_count, TILE // 8, 8)[:, owner]
    vir_tiles = eps_vir.reshape(tile_count, TILE)
    pair_level = eps_occ[me] + eps_occ[partners]
    denominator = pair_level[:, None, None, None] - vir_rows[first][:, :, :, None] - vir_tiles[second][:, :, None, :]
    live = jnp.arange(2)[None, :] < live_counts[0][partners][:, None]
    denominator = jnp.where(live[:, :, None, None], denominator, jnp.inf)

    total, energies, at = None, [], 0
    for group in GROUPS:
        here = slice(at, at + len(group))
        at += len(group)
        rights = [held[shift] for shift in group]
        place = first[here].reshape(-1)
        parts = coulomb(place, left_split, rights)
        parts = lax.all_to_all(parts, "aux", 0, 0)
        amplitudes = amplitude(parts, denominator[here].reshape(-1, TILE))
        amplitudes = lax.all_to_all(amplitudes, "aux", 0, 0)
        total, energy = gamma_add(place, amplitudes, rights, rows, cols, total)
        energies.append(jnp.sum(energy[: 2 * len(group)].reshape(len(group), 2 * TILE), axis=1))
    energy = jnp.concatenate(energies)
    mine = partners[:, None] == jnp.arange(occ_size)[None, :]
    energy = jnp.sum(jnp.where(mine, energy[:, None], 0.0), axis=0)
    energy = lax.psum(energy[None], "vir")
    return total[None], energy


def solution(mesh):
    return jax.shard_map(
        per_device,
        mesh=mesh,
        in_specs=(
            P("occ", "aux", "vir"),
            P(),
            P("vir"),
            P("occ", None, "vir", None),
            P("occ", None),
        ),
        out_specs=(P("occ", "aux", "vir"), P("occ", None)),
        check_vma=False,
    )
```

time: 445 us -> 199 us (0.45)
  waiting for transfers between devices: 203 us -> 90.3 us
  local copies, waits for them, and re-layouts: 83.1 us -> 15.1 us
  between operations: 54.9 us -> 1.13 us
  matrix products: 35.5 us -> 0 us
  Pallas kernels: 0 us -> 17.9 us
  other arithmetic: 15.6 us -> 1.52 us
  blocking collectives: 11.9 us -> 25.1 us
  starting transfers between devices: 39.1 us -> 47.2 us
    psum x1 -> x0, waiting for transfers between devices: 112 us -> none  [visit_pair(): summed = lax.psum(coulomb_part, 'aux')]
    ppermute x7, waiting for transfers between devices: 90.9 us -> 49.6 us  [per_device(): held[shift] = lax.ppermute(tiles, 'occ', route)]
    all_to_all x0 -> x4, waiting for transfers between devices: none -> 40.7 us  [the longest x2 28.3 us: per_device(): amplitudes = lax.all_to_all(amplitudes, 'aux', 0, 0)]
    dot_general x16 -> x0, matrix products: 35.5 us -> none  [the longest x8 23.6 us: visit_pair(): jnp.einsum('pkx,pky->kxy', left_cols, right_cols, precision=highest)]
    gather x32 -> x6, local copies, waits for them, and re-layouts: 35 us -> 3.53 us  [the longest x1 0.64 us: per_device(): live = jnp.arange(2)[None, :] < live_counts[0][partners][:, None]]
    all_to_all x0 -> x4, starting transfers between devices: none -> 28.1 us  [the longest x2 17 us: per_device(): parts = lax.all_to_all(parts, 'aux', 0, 0)]
    ppermute x7, starting transfers between devices: 39.1 us -> 19.1 us  [per_device(): held[shift] = lax.ppermute(tiles, 'occ', route)]
    pallas_call x0 -> x8, Pallas kernels: none -> 17.9 us  [the longest x2 6.49 us: gamma_add(): pl.pallas_call(functools.partial(gamma_kernel, carried is not None), out_...]
  transfers between devices with their start and end apart: 8 -> 11, of which waited for: 7 -> 7; matrix products, arithmetic and copies ran while one was open for 21% -> 3% of each run, Pallas kernels for 0% -> 4%
where the time goes in v1:
time: 199 us; the launch traced here: 198 us
  waiting for transfers between devices  90.3 us (45%)
  starting transfers between devices  47.2 us (24%)
  blocking collectives  25.1 us (13%)
  Pallas kernels  17.9 us (9%)
  local copies, waits for them, and re-layouts  15.1 us (8%)
    ppermute x7, waiting for transfers between devices, per_device(): held[shift] = lax.ppermute(tiles, 'occ', route)  49.6 us
    all_to_all x2, waiting for transfers between devices, per_device(): amplitudes = lax.all_to_all(amplitudes, 'aux', 0, 0)  28.3 us
    ppermute x7, starting transfers between devices, per_device(): held[shift] = lax.ppermute(tiles, 'occ', route)  19.1 us
    all_to_all x2, starting transfers between devices, per_device(): parts = lax.all_to_all(parts, 'aux', 0, 0)  17 us
    all_gather x1, blocking collectives, per_device(): all_pairs = lax.all_gather(own_pairs, 'occ')  12.7 us
    psum x1, blocking collectives, per_device(): energy = lax.psum(energy[None], 'vir')  12.4 us
    all_to_all x2, waiting for transfers between devices, per_device(): parts = lax.all_to_all(parts, 'aux', 0, 0)  12.4 us
    all_to_all x2, starting transfers between devices, per_device(): amplitudes = lax.all_to_all(amplitudes, 'aux', 0, 0)  11.2 us
  transfers between devices with their start and end apart: 11, of which 7 were waited for; matrix products, arithmetic and copies ran while one was open for 3% of the time, Pallas kernels for 4%

profile of v1, /device:TPU:6, one launch (start us, length us, event | category | flops | bytes accessed | tf_op | source)
XLA Modules:
  0.0 198.3 jit_solution(11394248429774767366)
XLA Ops:
  0.8 12.7 %all-gather = s32[8,8,1,2]{1,3,2,0:T(2,128)S(1)} all-gather(s32[1,8,1,2]{1,3,2,0:T(2,128)} %param.8), channel_id=2, replica_groups=mesh['occ'=8,'aux'=16,'vir'=4] {'occ'}, dimensions={0}, use_global_device_ids=true | all-gather | bytes 576 | tf_op jit(solution)/shard_map/all_gather | solution.py:190
  13.5 0.1 copy.33
  13.6 0.1 stack.86
  13.7 0.6 gather_fusion.1
  14.4 3.0 %pick.1 = (f32[640,256]{1,0:T(8,128)S(1)}, f32[640,256]{1,0:T(8,128)}, f32[640,256]{1,0:T(8,128)}, f32[640,256]{1,0:T(8,128)}, f32[640,256]{1,0:T(8,128)S(1)}, /...) custom-call(s32[16]{0:T(128)S(1)} %and_select_fusion.1.index_ref, f32[632,768]{1,0:T(8,128)} %bitcast.62), custom_call_target="tpu_custom_call" | custom-call | bytes 10485760 | tf_op jit(solution)/shard_map/pick/pallas_call | solution.py:46
  17.3 0.8 copy-done.6
  18.2 0.8 copy-done.7
  19.0 0.9 copy-done.8
  19.9 0.8 copy-done.9
  20.7 2.2 %collective-permute-start.4 = (f32[640,256]{1,0:T(8,128)}, f32[640,256]{1,0:T(8,128)S(1)}, u32[]{:S(2)}, u32[]{:S(2)}) collective-permute-start(f32[640,256]{1,0:T(8,128)} %get-tuple-element.19), channel_id=1, source_target_pairs={{0,64},{64,0},{128,192},{192,128},{256,320},{320,256},{384,448},{4... | collective-permute-start | bytes 1966088 | tf_op jit(solution)/shard_map/ppermute | solution.py:209
  23.0 3.2 %collective-permute-start.5 = (f32[640,256]{1,0:T(8,128)}, f32[640,256]{1,0:T(8,128)}, u32[]{:S(2)}, u32[]{:S(2)}) collective-permute-start(f32[640,256]{1,0:T(8,128)} %get-tuple-element.20), channel_id=1, source_target_pairs={{0,128},{64,192},{128,256},{192,320},{256,384},{320,448},{384,0},{... | collective-permute-start | bytes 1966088 | tf_op jit(solution)/shard_map/ppermute | solution.py:209
  26.2 2.6 %collective-permute-start.6 = (f32[640,256]{1,0:T(8,128)}, f32[640,256]{1,0:T(8,128)}, u32[]{:S(2)}, u32[]{:S(2)}) collective-permute-start(f32[640,256]{1,0:T(8,128)} %get-tuple-element.21), channel_id=1, source_target_pairs={{0,384},{64,448},{128,0},{192,64},{256,128},{320,192},{384,256},{4... | collective-permute-start | bytes 1966088 | tf_op jit(solution)/shard_map/ppermute | solution.py:209
  28.9 0.1 stack.78
  29.0 1.5 copy-done.1
  30.6 0.6 left.1.left_ref
  31.2 0.1 copy-done.12
  31.3 0.6 gather_fusion
  31.9 0.1 reshape.762.first_ref
  32.0 10.0 %collective-permute-done.5.refs_2_ = f32[640,256]{1,0:T(8,128)} collective-permute-done((f32[640,256]{1,0:T(8,128)}, f32[640,256]{1,0:T(8,128)}, u32[]{:S(2)}, u32[]{:S(2)}) %collective-permute-start.5) | collective-permute-done | bytes 655392 | tf_op jit(solution)/shard_map/ppermute | solution.py:209
  42.0 4.2 %collective-permute-done.6.refs_3_ = f32[640,256]{1,0:T(8,128)} collective-permute-done((f32[640,256]{1,0:T(8,128)}, f32[640,256]{1,0:T(8,128)}, u32[]{:S(2)}, u32[]{:S(2)}) %collective-permute-start.6) | collective-permute-done | bytes 655392 | tf_op jit(solution)/shard_map/ppermute | solution.py:209
  46.2 2.3 %coulomb.3 = f32[16,64,128]{2,1,0:T(8,128)S(1)} custom-call(s32[8]{0:T(128)S(1)} %reshape.762.first_ref, bf16[6,256,640]{2,1,0:T(8,128)(2,1)S(1)} %left.1.left_ref, f32[640,256]{1,0:T(8,128)S(1)} %get-tuple-element.18.refs_0_, f32[640,256]{1,0:T(8,128)S(1)} %collective-permute-done.4.refs_1_, f32[640,256]{1,0:T(8,128)} %collective-permute-done.5.refs_2_, ...), custom_call_target="tpu_custom_call" | custom-call | flops 671088640 | bytes 5242880 | tf_op jit(solution)/shard_map/coulomb/pallas_call | solution.py:97
  48.5 0.8 copy-done.2
  49.3 8.9 %all-to-all-start.2 = ((f32[16,64,128]{2,1,0:T(8,128)}), f32[16,64,128]{2,1,0:T(8,128)}, u32[]{:S(2)}, u32[]{:S(2)}) async-start(f32[16,64,128]{2,1,0:T(8,128)} %copy-done.2), calls=%async_computation.2 | async-start | bytes 1048576 | tf_op jit(solution)/shard_map/all_to_all | solution.py:225
  58.2 1.9 collective-permute-start
  60.1 3.6 %collective-permute-start.1 = (f32[640,256]{1,0:T(8,128)}, f32[640,256]{1,0:T(8,128)}, u32[]{:S(2)}, u32[]{:S(2)}) collective-permute-start(f32[640,256]{1,0:T(8,128)} %copy-done.8), channel_id=1, source_target_pairs={{0,448},{64,384},{128,64},{192,0},{256,192},{320,128},{384,320},{4... | collective-permute-start | bytes 1966088 | tf_op jit(solution)/shard_map/ppermute | solution.py:209
  63.8 1.9 collective-permute-start.2
  65.7 3.5 %collective-permute-start.3 = (f32[640,256]{1,0:T(8,128)}, f32[640,256]{1,0:T(8,128)}, u32[]{:S(2)}, u32[]{:S(2)}) collective-permute-start(f32[640,256]{1,0:T(8,128)} %copy-done.6), channel_id=1, source_target_pairs={{0,320},{64,256},{128,448},{192,384},{256,64},{320,0},{384,192},{4... | collective-permute-start | bytes 1966088 | tf_op jit(solution)/shard_map/ppermute | solution.py:209
  69.3 0.6 dynamic_slice.6
  69.9 0.6 gather_fusion.3
  70.5 0.6 gather_fusion.2
  71.2 0.1 copy.34
  71.4 0.1 copy.37
  71.5 0.1 reshape.796
  71.7 0.1 reshape.804
  71.8 0.1 reshape.758.first_ref
  71.8 0.1 reshape.759
  72.0 0.6 gather_fusion.5
  72.6 0.6 broadcast_add_fusion
  73.1 4.3 %collective-permute-done.refs_0_.refs_1_ = f32[640,256]{1,0:T(8,128)} collective-permute-done((f32[640,256]{1,0:T(8,128)}, f32[640,256]{1,0:T(8,128)}, u32[]{:S(2)}, u32[]{:S(2)}) %collective-permute-start) | collective-permute-done | bytes 655392 | tf_op jit(solution)/shard_map/ppermute | solution.py:209
  77.5 31.1 %collective-permute-done.1.refs_1_.refs_2_ = f32[640,256]{1,0:T(8,128)} collective-permute-done((f32[640,256]{1,0:T(8,128)}, f32[640,256]{1,0:T(8,128)}, u32[]{:S(2)}, u32[]{:S(2)}) %collective-permute-start.1) | collective-permute-done | bytes 655392 | tf_op jit(solution)/shard_map/ppermute | solution.py:209
  108.5 2.7 %coulomb.2 = f32[16,64,128]{2,1,0:T(8,128)S(1)} custom-call(s32[8]{0:T(128)S(1)} %reshape.758.first_ref, bf16[6,256,640]{2,1,0:T(8,128)(2,1)S(1)} %left.1.left_ref, f32[640,256]{1,0:T(8,128)} %collective-permute-done.refs_0_.refs_1_, f32[640,256]{1,0:T(8,128)} %collective-permute-done.1.refs_1_.refs_2_, f32[640,256]{1,0:T(8,128)} %collective-permute-done.2.refs_2_.refs_3_, ...), custom_call_target="tpu_custom_call" | custom-call | flops 671088640 | bytes 5242880 | tf_op jit(solution)/shard_map/coulomb/pallas_call | solution.py:97
  111.2 0.8 copy-done.3
  112.0 8.1 %all-to-all-start = ((f32[16,64,128]{2,1,0:T(8,128)}), f32[16,64,128]{2,1,0:T(8,128)S(1)}, u32[]{:S(2)}, u32[]{:S(2)}) async-start(f32[16,64,128]{2,1,0:T(8,128)} %copy-done.3), calls=%async_computation | async-start | bytes 1048576 | tf_op jit(solution)/shard_map/all_to_all | solution.py:225
  120.1 0.6 gather_fusion.4
  120.8 0.1 subtract_select_fusion
  121.0 1.9 amplitude.3
  122.9 12.4 %all-to-all-done.parts_ref = f32[16,64,128]{2,1,0:T(8,128)S(1)} async-done(((f32[16,64,128]{2,1,0:T(8,128)}), f32[16,64,128]{2,1,0:T(8,128)S(1)}, u32[]{:S(2)}, u32[]{:S(2)}) %all-to-all-start) | async-done | bytes 524320 | tf_op jit(solution)/shard_map/all_to_all | solution.py:225
  135.3 5.5 %all-to-all-start.3 = ((f32[16,72,128]{2,1,0:T(8,128)}), f32[16,72,128]{2,1,0:T(8,128)S(1)}, u32[]{:S(2)}, u32[]{:S(2)}) async-start(f32[16,72,128]{2,1,0:T(8,128)} %amplitude.3), calls=%async_computation.3 | async-start | bytes 1179648 | tf_op jit(solution)/shard_map/all_to_all | solution.py:227
  140.8 0.9 amplitude.2
  141.7 15.6 %all-to-all-done.3.amplitude_ref = f32[16,72,128]{2,1,0:T(8,128)S(1)} async-done(((f32[16,72,128]{2,1,0:T(8,128)}), f32[16,72,128]{2,1,0:T(8,128)S(1)}, u32[]{:S(2)}, u32[]{:S(2)}) %all-to-all-start.3) | async-done | bytes 589856 | tf_op jit(solution)/shard_map/all_to_all | solution.py:227
  157.3 5.6 %all-to-all-start.1 = ((f32[16,72,128]{2,1,0:T(8,128)}), f32[16,72,128]{2,1,0:T(8,128)S(1)}, u32[]{:S(2)}, u32[]{:S(2)}) async-start(f32[16,72,128]{2,1,0:T(8,128)} %amplitude.2), calls=%async_computation.1 | async-start | bytes 1179648 | tf_op jit(solution)/shard_map/all_to_all | solution.py:227
  163.0 0.1 stack.95
  163.1 2.4 %gamma.2 = (f32[632,768]{1,0:T(8,128)S(1)}, f32[8,128]{1,0:T(8,128)S(1)}) custom-call(s32[8]{0:T(128)S(1)} %reshape.762.first_ref, f32[16,72,128]{2,1,0:T(8,128)S(1)} %all-to-all-done.3.amplitude_ref, f32[640,256]{1,0:T(8,128)S(1)} %get-tuple-element.18.refs_0_, f32[640,256]{1,0:T(8,128)S(1)} %collective-permute-done.4.refs_1_, ...), custom_call_target="tpu_custom_call" | custom-call | flops 671088640 | bytes 5242880 | tf_op jit(solution)/shard_map/gamma/pallas_call | solution.py:165
  165.5 1.3 copy-done.4
  166.8 12.6 %all-to-all-done.1.amplitude_ref = f32[16,72,128]{2,1,0:T(8,128)S(1)} async-done(((f32[16,72,128]{2,1,0:T(8,128)}), f32[16,72,128]{2,1,0:T(8,128)S(1)}, u32[]{:S(2)}, u32[]{:S(2)}) %all-to-all-start.1) | async-done | bytes 589856 | tf_op jit(solution)/shard_map/all_to_all | solution.py:227
  179.4 1.5 copy-done.5
  181.0 4.1 %gamma.3 = (f32[632,768]{1,0:T(8,128)}, f32[8,128]{1,0:T(8,128)S(1)}) custom-call(s32[8]{0:T(128)S(1)} %reshape.758.first_ref, f32[16,72,128]{2,1,0:T(8,128)S(1)} %all-to-all-done.1.amplitude_ref, f32[632,768]{1,0:T(8,128)S(1)} %copy-done.5, f32[640,256]{1,0:T(8,128)} %collective-permute-done.refs_0_.refs_1_, ...), custom_call_target="tpu_custom_call" | custom-call | flops 671088640 | bytes 5242880 | tf_op jit(solution)/shard_map/gamma/pallas_call | solution.py:165
  185.0 0.1 reduce_sum.44
  185.1 0.1 reduce_sum.31
  185.3 0.1 reduce_sum.32
  185.3 0.1 reduce_sum.36
  185.5 0.1 reduce_sum.46
  185.7 0.1 select_reduce_fusion
  185.8 12.4 %psum.7 = f32[1,8]{1,0:T(1,128)} all-reduce(f32[1,8]{1,0:T(1,128)S(1)} %bitcast.73), channel_id=1, replica_groups=mesh['occ'=8,'aux'=16,'vir'=4] {'vir'}, use_global_device_ids=true, to_apply=%region_5.6 | all-reduce | flops 8 | bytes 64 | tf_op jit(solution)/shard_map/psum | solution.py:233
  (42 shorter events, 0.9 us)
Async XLA Ops:
  0.6 69.9 %copy-start = (s32[1,8]{1,0:T(1,128)S(1)}, s32[1,8]{1,0:T(1,128)}, u32[]{:S(2)}) copy-start(s32[1,8]{1,0:T(1,128)} %param.9) | copy-start | bytes 100
  17.3 0.8 copy-start.6
  18.2 0.8 copy-start.7
  19.0 0.9 copy-start.8
  19.9 0.8 copy-start.9
  20.7 11.3 %collective-permute-start.4 = (f32[640,256]{1,0:T(8,128)}, f32[640,256]{1,0:T(8,128)S(1)}, u32[]{:S(2)}, u32[]{:S(2)}) collective-permute-start(f32[640,256]{1,0:T(8,128)} %get-tuple-element.19), channel_id=1, source_target_pairs={{0,64},{64,0},{128,192},{192,128},{256,320},{320,256},{384,448},{4... | collective-permute-start | bytes 1966088 | tf_op jit(solution)/shard_map/ppermute | solution.py:209
  23.0 19.0 %collective-permute-start.5 = (f32[640,256]{1,0:T(8,128)}, f32[640,256]{1,0:T(8,128)}, u32[]{:S(2)}, u32[]{:S(2)}) collective-permute-start(f32[640,256]{1,0:T(8,128)} %get-tuple-element.20), channel_id=1, source_target_pairs={{0,128},{64,192},{128,256},{192,320},{256,384},{320,448},{384,0},{... | collective-permute-start | bytes 1966088 | tf_op jit(solution)/shard_map/ppermute | solution.py:209
  26.2 20.0 %collective-permute-start.6 = (f32[640,256]{1,0:T(8,128)}, f32[640,256]{1,0:T(8,128)}, u32[]{:S(2)}, u32[]{:S(2)}) collective-permute-start(f32[640,256]{1,0:T(8,128)} %get-tuple-element.21), channel_id=1, source_target_pairs={{0,384},{64,448},{128,0},{192,64},{256,128},{320,192},{384,256},{4... | collective-permute-start | bytes 1966088 | tf_op jit(solution)/shard_map/ppermute | solution.py:209
  29.0 1.5 copy-start.1
  30.6 0.7 copy-start.12
  46.2 23.1 %copy-start.10 = (f32[8]{0:T(128)S(1)}, f32[8]{0:T(128)}, u32[]{:S(2)}) copy-start(f32[8]{0:T(128)} %param.6) | copy-start | bytes 100
  48.5 0.8 copy-start.2
  49.3 22.5 %copy-start.11 = (f32[768]{0:T(1024)S(1)}, f32[768]{0:T(1024)}, u32[]{:S(2)}) copy-start(f32[768]{0:T(1024)} %param.7) | copy-start | bytes 9220
  49.3 62.7 %all-to-all-start.2 = ((f32[16,64,128]{2,1,0:T(8,128)}), f32[16,64,128]{2,1,0:T(8,128)}, u32[]{:S(2)}, u32[]{:S(2)}) async-start(f32[16,64,128]{2,1,0:T(8,128)} %copy-done.2), calls=%async_computation.2 | async-start | bytes 1048576 | tf_op jit(solution)/shard_map/all_to_all | solution.py:225
  58.2 19.2 %collective-permute-start = (f32[640,256]{1,0:T(8,128)}, f32[640,256]{1,0:T(8,128)}, u32[]{:S(2)}, u32[]{:S(2)}) collective-permute-start(f32[640,256]{1,0:T(8,128)} %copy-done.9), channel_id=1, source_target_pairs={{0,192},{64,128},{128,320},{192,256},{256,448},{320,384},{384,64},... | collective-permute-start | bytes 1966088 | tf_op jit(solution)/shard_map/ppermute | solution.py:209
  60.1 48.4 %collective-permute-start.1 = (f32[640,256]{1,0:T(8,128)}, f32[640,256]{1,0:T(8,128)}, u32[]{:S(2)}, u32[]{:S(2)}) collective-permute-start(f32[640,256]{1,0:T(8,128)} %copy-done.8), channel_id=1, source_target_pairs={{0,448},{64,384},{128,64},{192,0},{256,192},{320,128},{384,320},{4... | collective-permute-start | bytes 1966088 | tf_op jit(solution)/shard_map/ppermute | solution.py:209
  63.8 44.7 %collective-permute-start.2 = (f32[640,256]{1,0:T(8,128)}, f32[640,256]{1,0:T(8,128)}, u32[]{:S(2)}, u32[]{:S(2)}) collective-permute-start(f32[640,256]{1,0:T(8,128)} %copy-done.7), channel_id=1, source_target_pairs={{0,256},{64,320},{128,384},{192,448},{256,0},{320,64},{384,128},{4... | collective-permute-start | bytes 1966088 | tf_op jit(solution)/shard_map/ppermute | solution.py:209
  65.7 42.8 %collective-permute-start.3 = (f32[640,256]{1,0:T(8,128)}, f32[640,256]{1,0:T(8,128)}, u32[]{:S(2)}, u32[]{:S(2)}) collective-permute-start(f32[640,256]{1,0:T(8,128)} %copy-done.6), channel_id=1, source_target_pairs={{0,320},{64,256},{128,448},{192,384},{256,64},{320,0},{384,192},{4... | collective-permute-start | bytes 1966088 | tf_op jit(solution)/shard_map/ppermute | solution.py:209
  111.2 0.8 copy-start.3
  112.0 23.3 %all-to-all-start = ((f32[16,64,128]{2,1,0:T(8,128)}), f32[16,64,128]{2,1,0:T(8,128)S(1)}, u32[]{:S(2)}, u32[]{:S(2)}) async-start(f32[16,64,128]{2,1,0:T(8,128)} %copy-done.3), calls=%async_computation | async-start | bytes 1048576 | tf_op jit(solution)/shard_map/all_to_all | solution.py:225
  135.3 22.0 %all-to-all-start.3 = ((f32[16,72,128]{2,1,0:T(8,128)}), f32[16,72,128]{2,1,0:T(8,128)S(1)}, u32[]{:S(2)}, u32[]{:S(2)}) async-start(f32[16,72,128]{2,1,0:T(8,128)} %amplitude.3), calls=%async_computation.3 | async-start | bytes 1179648 | tf_op jit(solution)/shard_map/all_to_all | solution.py:227
  157.3 22.1 %all-to-all-start.1 = ((f32[16,72,128]{2,1,0:T(8,128)}), f32[16,72,128]{2,1,0:T(8,128)S(1)}, u32[]{:S(2)}, u32[]{:S(2)}) async-start(f32[16,72,128]{2,1,0:T(8,128)} %amplitude.2), calls=%async_computation.1 | async-start | bytes 1179648 | tf_op jit(solution)/shard_map/all_to_all | solution.py:227
  165.5 1.3 copy-start.4
  179.4 1.5 copy-start.5

commit v2 on v1

v2 whole, which is shorter than its diff:
```python
import functools

import jax
import jax.numpy as jnp
from jax import lax
from jax.experimental import pallas as pl
from jax.experimental.pallas import tpu as pltpu
from jax.sharding import PartitionSpec as P

TILE = 128
VMEM = pl.BlockSpec(memory_space=pltpu.VMEM)
SMEM = pl.BlockSpec(memory_space=pltpu.SMEM)
def params():
    return pltpu.CompilerParams(vmem_limit_bytes=12 * 1024 * 1024)


def cost(flops, moved):
    return pl.CostEstimate(flops=flops, bytes_accessed=moved, transcendentals=0)


def split(value):
    high = value.astype(jnp.bfloat16)
    low = (value - high.astype(jnp.float32)).astype(jnp.bfloat16)
    return high, low


def lanes(index):
    return pl.ds(pl.multiple_of(index * TILE, TILE), TILE)


def pick_kernel(index_ref, block_ref, *out_refs):
    rows = block_ref.shape[0]
    at = 0
    for out_ref in out_refs:
        for k in range(out_ref.shape[0]):
            for s in range(2):
                out_ref[k, :rows, s * TILE : (s + 1) * TILE] = block_ref[:, lanes(index_ref[at])]
                at += 1
            out_ref[k, rows:, :] = jnp.zeros((out_ref.shape[1] - rows, 2 * TILE), jnp.float32)


def pick(wanted, block, counts, padded):
    return pl.pallas_call(
        pick_kernel,
        out_shape=[jax.ShapeDtypeStruct((count, padded, 2 * TILE), jnp.float32) for count in counts],
        in_specs=[SMEM, VMEM],
        out_specs=[VMEM] * len(counts),
        compiler_params=params(),
        cost_estimate=cost(0, sum(counts) * padded * 4 * TILE * 4),
        name="pick",
    )(wanted, block)


def left_kernel(block_ref, out_ref):
    rows = block_ref.shape[0]
    padded = out_ref.shape[2]
    for f in range(out_ref.shape[0]):
        tile = block_ref[:, f * TILE : (f + 1) * TILE]
        tile = jnp.concatenate([tile, jnp.zeros((padded - rows, TILE), jnp.float32)], axis=0)
        high, low = split(tile.T)
        out_ref[f, :TILE, :] = high
        out_ref[f, TILE:, :] = low


def left(block, padded):
    tiles = block.shape[1] // TILE
    return pl.pallas_call(
        left_kernel,
        out_shape=jax.ShapeDtypeStruct((tiles, 2 * TILE, padded), jnp.bfloat16),
        in_specs=[VMEM],
        out_specs=VMEM,
        compiler_params=params(),
        cost_estimate=cost(0, block.size * 8),
        name="left",
    )(block)


def add_amplitude(parts_ref, denominator_ref, out_ref):
    summed = jnp.sum(parts_ref[...], axis=0)
    amplitude = summed / denominator_ref[...]
    tiles = summed.shape[0] // 8
    energy = jnp.sum((summed * amplitude).reshape(tiles, 8, TILE), axis=1)
    energy = jnp.concatenate([energy, jnp.zeros((-tiles % 8, TILE), jnp.float32)], axis=0) if tiles % 8 else energy
    done = 8 * tiles + energy.shape[0]
    for owner in range(out_ref.shape[0]):
        out_ref[owner, : 8 * tiles, :] = amplitude
        out_ref[owner, 8 * tiles : done, :] = energy
    return done


def returned_rows(tiles):
    return 8 * tiles + -(-tiles // 8) * 8


def exchange_kernel(entries, with_parts, *refs):
    *in_refs, out_ref = refs
    at = 0
    if with_parts:
        parts_ref, denominator_ref, *in_refs = in_refs
        at = add_amplitude(parts_ref, denominator_ref, out_ref)
    if entries:
        first_ref, left_ref, *right_refs = in_refs
        for k, (which, entry) in enumerate(entries):
            for s in range(2):
                t = 2 * k + s
                high, low = split(right_refs[which][entry, :, s * TILE : (s + 1) * TILE])
                both = jnp.concatenate([high, low], axis=1)
                part = jnp.dot(left_ref[first_ref[t]], both, preferred_element_type=jnp.float32)
                cross = part[:TILE, TILE:] + part[TILE:, :TILE] + part[TILE:, TILE:]
                total = part[:TILE, :TILE] + cross
                out_ref[:, at + 8 * t : at + 8 * t + 8, :] = total.reshape(TILE // 8, 8, TILE)


def exchange(returned, group):
    inputs, specs, rows, entries, flops = [], [], 0, [], 0
    if returned is not None:
        parts, denominator = returned
        inputs += [parts, denominator]
        specs += [VMEM, VMEM]
        rows += returned_rows(parts.shape[1] // 8)
    if group is not None:
        first, left_split, rights = group
        arrays, entries = unique(rights)
        inputs += [first, left_split, *arrays]
        specs += [SMEM, VMEM] + [VMEM] * len(arrays)
        rows += 16 * len(entries)
        flops = len(entries) * 16 * TILE * TILE * left_split.shape[2]
    return pl.pallas_call(
        functools.partial(exchange_kernel, entries, returned is not None),
        out_shape=jax.ShapeDtypeStruct((TILE // 8, rows, TILE), jnp.float32),
        in_specs=specs,
        out_specs=VMEM,
        compiler_params=params(),
        cost_estimate=cost(flops, TILE // 8 * rows * TILE * 8),
        name="exchange",
    )(*inputs)


def unique(rights):
    arrays, entries = [], []
    for array, entry in rights:
        which = next((k for k, known in enumerate(arrays) if known is array), len(arrays))
        if which == len(arrays):
            arrays.append(array)
        entries.append((which, entry))
    return arrays, entries


def gamma_kernel(entries, carried, first_ref, amplitude_ref, *refs):
    if carried:
        gamma_in, *refs = refs
    *right_refs, gamma_ref, energy_ref = refs
    rows = gamma_ref.shape[0]
    count = 2 * len(entries)
    gamma_ref[...] = gamma_in[...] if carried else jnp.zeros_like(gamma_ref)
    for k, (which, entry) in enumerate(entries):
        for s in range(2):
            t = 2 * k + s
            value = amplitude_ref[:, 8 * t : 8 * t + 8, :].reshape(TILE, TILE)
            high, low = split(value)
            weights = jnp.concatenate(
                [
                    jnp.concatenate([high, high], axis=1),
                    jnp.concatenate([low, low], axis=1),
                ],
                axis=0,
            )
            both = jnp.concatenate(split(right_refs[which][entry, :, s * TILE : (s + 1) * TILE]), axis=1)
            part = lax.dot_general(both, weights, (((1,), (1,)), ((), ())), preferred_element_type=jnp.float32)
            place = lanes(first_ref[t])
            gamma_ref[:, place] += (part[:, :TILE] + part[:, TILE:])[:rows]
    energy_ref[...] = jnp.sum(amplitude_ref[:, 8 * count : 8 * count + energy_ref.shape[0], :], axis=0)


def gamma_add(first, amplitudes, rights, rows, cols, carried):
    arrays, entries = unique(rights)
    tiles = 2 * len(entries)
    inputs = (first, amplitudes) + ((carried,) if carried is not None else ())
    return pl.pallas_call(
        functools.partial(gamma_kernel, entries, carried is not None),
        out_shape=[
            jax.ShapeDtypeStruct((rows, cols), jnp.float32),
            jax.ShapeDtypeStruct((returned_rows(tiles) - 8 * tiles, TILE), jnp.float32),
        ],
        in_specs=[SMEM] + [VMEM] * (len(inputs) - 1 + len(arrays)),
        out_specs=[VMEM, VMEM],
        compiler_params=params(),
        cost_estimate=cost(tiles * 8 * TILE * TILE * rows, rows * cols * 8),
        name="gamma",
    )(*inputs, *arrays)


SHIFTS = ((0, 0), (0, 1), (1, 0), (3, 0), (1, 1), (3, 1), (2, 0), (2, 1))
GROUPS = (2, 4, 2)


def per_device(bq, eps_occ, eps_vir, tile_pairs, live_counts):
    occ_size = lax.axis_size("occ")
    me = lax.axis_index("occ")
    chip, core = me // 2, me % 2
    chips = occ_size // 2
    owner = lax.axis_index("aux")
    block = bq[0]
    rows, cols = block.shape
    padded = -(-rows // 16) * 16
    tile_count = cols // TILE
    own_pairs = tile_pairs[0, :, 0, :]
    all_pairs = lax.all_gather(own_pairs, "occ")

    def route(dx, dc):
        return [(x * 2 + c, (x + dx) % chips * 2 + (c + dc) % 2) for x in range(chips) for c in range(2)]

    def wanted(*shifts):
        receivers = jnp.stack([(chip + dx) % chips * 2 + (core + dc) % 2 for dx, dc in shifts])
        return (all_pairs[receivers, me] % tile_count).reshape(-1)

    def swapped(tiles):
        return lax.ppermute(tiles, "occ", route(0, 1))

    near_index = wanted((1, 0), (1, 1), (3, 0), (3, 1))
    ahead, behind = pick(near_index, block, (2, 2), padded)
    ahead = lax.ppermute(ahead, "occ", route(1, 0))
    behind = lax.ppermute(behind, "occ", route(3, 0))
    far_index = wanted((0, 0), (0, 1), (2, 0), (2, 1))
    own, mate, far = pick(far_index, block, (1, 1, 2), padded)
    mate = swapped(mate)
    left_split = left(block, padded)

    partners = jnp.stack([(chip - dx) % chips * 2 + (core - dc) % 2 for dx, dc in SHIFTS])
    chosen = own_pairs[partners]
    first = (chosen // tile_count).astype(jnp.int32)
    second = chosen % tile_count

    vir_rows = eps_vir.reshape(tile_count, TILE // 8, 8)[:, owner]
    vir_tiles = eps_vir.reshape(tile_count, TILE)
    pair_level = eps_occ[me] + eps_occ[partners]
    denominator = pair_level[:, None, None, None] - vir_rows[first][:, :, :, None] - vir_tiles[second][:, :, None, :]
    live = jnp.arange(2)[None, :] < live_counts[0][partners][:, None]
    denominator = jnp.where(live[:, :, None, None], denominator, jnp.inf)

    bounds = [sum(GROUPS[:g]) for g in range(len(GROUPS) + 1)]
    spans = [slice(a, b) for a, b in zip(bounds, bounds[1:])]
    places = [first[span].reshape(-1) for span in spans]
    levels = [denominator[span].reshape(-1, TILE) for span in spans]

    def sent(returned, group):
        return lax.all_to_all(exchange(returned, group), "aux", 0, 0)

    early_rights = [(own, 0), (mate, 0)]
    early_parts = sent(None, (places[0], left_split, early_rights))
    far, early_parts = lax.optimization_barrier((far, early_parts))
    far = lax.ppermute(far, "occ", route(2, 0))
    early = sent((early_parts, levels[0]), None)
    total, early_energy = gamma_add(places[0], early, early_rights, rows, cols, None)

    near_mate = swapped(jnp.stack([ahead[1], behind[1]]))
    near_rights = [(ahead, 0), (behind, 0), (near_mate, 0), (near_mate, 1)]
    near_place, early = lax.optimization_barrier((places[1], early))
    near_parts = sent(None, (near_place, left_split, near_rights))

    far_mate = swapped(far[1:])
    far_rights = [(far, 0), (far_mate, 0)]
    both = sent((near_parts, levels[1]), (places[2], left_split, far_rights))
    near_rows = returned_rows(2 * GROUPS[1])
    last = sent((both[:, near_rows:], levels[2]), None)
    total, near_energy = gamma_add(places[1], both, near_rights, rows, cols, total)
    total, last_energy = gamma_add(places[2], last, far_rights, rows, cols, total)

    energies = [
        jnp.sum(energy[: 2 * count].reshape(count, 2 * TILE), axis=1)
        for energy, count in zip((early_energy, near_energy, last_energy), GROUPS)
    ]
    mine = partners[:, None] == jnp.arange(occ_size)[None, :]
    energy = jnp.sum(jnp.where(mine, jnp.concatenate(energies)[:, None], 0.0), axis=0)
    energy = lax.psum(energy[None], "vir")
    return total[None], energy


def solution(mesh):
    return jax.shard_map(
        per_device,
        mesh=mesh,
        in_specs=(
            P("occ", "aux", "vir"),
            P(),
            P("vir"),
            P("occ", None, "vir", None),
            P("occ", None),
        ),
        out_specs=(P("occ", "aux", "vir"), P("occ", None)),
        check_vma=False,
    )
```

time: 199 us -> 182 us (0.915); the launches traced: 198 us -> 178 us
  waiting for transfers between devices: 90.3 us -> 28.8 us
  blocking collectives: 25.1 us -> 54 us
  local copies, waits for them, and re-layouts: 15.1 us -> 28.2 us
  starting transfers between devices: 47.2 us -> 39.5 us
  other arithmetic: 1.52 us -> 6.77 us
  Pallas kernels: 17.9 us -> 20.1 us
    ppermute x7 -> x6, waiting for transfers between devices: 49.6 us -> 7.66 us  [the longest x1 3.9 us: per_device(): behind = lax.ppermute(behind, 'occ', route(3, 0))]
    all_to_all x0 -> x1, blocking collectives: none -> 28.8 us  [sent(): return lax.all_to_all(exchange(returned, group), 'aux', 0, 0)]
    all_to_all x4, waiting for transfers between devices: 40.7 us -> 21.1 us  [sent(): return lax.all_to_all(exchange(returned, group), 'aux', 0, 0)]
    ppermute x7 -> x6, starting transfers between devices: 19.1 us -> 14 us  [the longest x3 5.73 us: swapped(): return lax.ppermute(tiles, 'occ', route(0, 1))]
    slice x2 -> x8, local copies, waits for them, and re-layouts: 0.01 us -> 5 us  [the longest x1 1.97 us: per_device(): far_mate = swapped(far[1:])]
    unnamed x27 -> x47, local copies, waits for them, and re-layouts: 9.43 us -> 14 us
    all_to_all x4, starting transfers between devices: 28.1 us -> 25.5 us  [sent(): return lax.all_to_all(exchange(returned, group), 'aux', 0, 0)]
    pallas_call x7 -> x10, Pallas kernels: 17.3 us -> 19.5 us  [the longest x3 8.19 us: gamma_add(): pl.pallas_call(functools.partial(gamma_kernel, entries, carried is not No...]
  transfers between devices with their start and end apart: 11 -> 10, of which waited for: 7 -> 6; matrix products, arithmetic and copies ran while one was open for 3% -> 11% of each run, Pallas kernels for 4% -> 6%
where the time goes in v2:
time: 182 us; the launch traced here: 178 us
  blocking collectives  54 us (30%)
  starting transfers between devices  39.5 us (22%)
  waiting for transfers between devices  28.8 us (16%)
  local copies, waits for them, and re-layouts  28.2 us (15%)
  Pallas kernels  20.1 us (11%)
  other arithmetic  6.77 us (4%)
    all_to_all x1, blocking collectives, sent(): return lax.all_to_all(exchange(returned, group), 'aux', 0, 0)  28.8 us
    all_to_all x4, starting transfers between devices, sent(): return lax.all_to_all(exchange(returned, group), 'aux', 0, 0)  25.5 us
    all_to_all x4, waiting for transfers between devices, sent(): return lax.all_to_all(exchange(returned, group), 'aux', 0, 0)  21.1 us
    unnamed x47, local copies, waits for them, and re-layouts  14 us
    all_gather x1, blocking collectives, per_device(): all_pairs = lax.all_gather(own_pairs, 'occ')  12.7 us
    psum x1, blocking collectives, per_device(): energy = lax.psum(energy[None], 'vir')  12.5 us
    pallas_call x3, Pallas kernels, gamma_add(): pl.pallas_call(functools.partial(gamma_kernel, entries, carried is not No...  8.19 us
    pallas_call x5, Pallas kernels, exchange(): pl.pallas_call(functools.partial(exchange_kernel, entries, returned is no...  7.53 us
  transfers between devices with their start and end apart: 10, of which 6 were waited for; matrix products, arithmetic and copies ran while one was open for 11% of the time, Pallas kernels for 6%

profile of v2, /device:TPU:6, one launch (start us, length us, event | category | flops | bytes accessed | tf_op | source)
XLA Modules:
  0.0 178.5 jit_solution(6451101721319629959)
XLA Ops:
  0.8 12.7 %all-gather = s32[8,8,1,2]{1,3,2,0:T(2,128)S(1)} all-gather(s32[1,8,1,2]{1,3,2,0:T(2,128)} %param.8), channel_id=2, replica_groups=mesh['occ'=8,'aux'=16,'vir'=4] {'occ'}, dimensions={0}, use_global_device_ids=true | all-gather | bytes 576 | tf_op jit(solution)/shard_map/all_gather | solution.py:208
  13.7 0.6 gather_fusion.6
  14.3 1.5 copy-done.1
  15.9 2.2 %pick.3 = (f32[2,640,256]{2,1,0:T(8,128)}, f32[2,640,256]{2,1,0:T(8,128)}) custom-call(s32[8]{0:T(128)S(1)} %and_select_fusion.index_ref, f32[632,768]{1,0:T(8,128)S(1)} %bitcast.65), custom_call_target="tpu_custom_call" | custom-call | bytes 5242880 | tf_op jit(solution)/shard_map/pick/pallas_call | solution.py:43
  18.1 3.3 %collective-permute-start.1 = (f32[2,640,256]{2,1,0:T(8,128)}, f32[2,640,256]{2,1,0:T(8,128)S(1)}, u32[]{:S(2)}, u32[]{:S(2)}) collective-permute-start(f32[2,640,256]{2,1,0:T(8,128)} %get-tuple-element.21), channel_id=1, source_target_pairs={{0,128},{64,192},{128,256},{192,320},{256,384},{320,448},{384,0},{... | collective-permute-start | bytes 3932168 | tf_op jit(solution)/shard_map/ppermute | solution.py:222
  21.4 2.6 %collective-permute-start.2 = (f32[2,640,256]{2,1,0:T(8,128)}, f32[2,640,256]{2,1,0:T(8,128)}, u32[]{:S(2)}, u32[]{:S(2)}) collective-permute-start(f32[2,640,256]{2,1,0:T(8,128)} %get-tuple-element.22), channel_id=1, source_target_pairs={{0,384},{64,448},{128,0},{192,64},{256,128},{320,192},{384,256},{4... | collective-permute-start | bytes 3932168 | tf_op jit(solution)/shard_map/ppermute | solution.py:223
  24.1 0.6 gather_fusion.1
  24.8 1.6 pick.2
  26.3 0.9 copy-done.4
  27.2 1.0 copy-done.15
  28.2 1.9 %collective-permute-start = (f32[1,640,256]{2,1,0:T(8,128)}, f32[1,640,256]{2,1,0:T(8,128)}, u32[]{:S(2)}, u32[]{:S(2)}) collective-permute-start(f32[1,640,256]{2,1,0:T(8,128)} %get-tuple-element.18), channel_id=1, source_target_pairs={{0,64},{64,0},{128,192},{192,128},{256,320},{320,256},{384,448},{4... | collective-permute-start | bytes 1966088 | tf_op jit(solution)/shard_map/ppermute | solution.py:218
  30.4 0.6 gather_fusion
  31.3 0.5 fusion.11
  31.8 1.5 copy-done.3
  33.4 0.6 left.1.refs_1_.refs_3_
  34.0 0.6 gather_fusion.3
  34.7 0.6 dynamic_slice.6
  35.7 0.6 gather_fusion.2
  36.3 0.6 pad_clamp_fusion.1
  36.9 1.2 broadcast_add_fusion
  38.1 0.7 iota_compare_fusion.1
  38.8 1.1 copy-done.5
  39.9 1.7 exchange.5
  41.6 0.7 copy-done.13
  42.3 8.0 %all-to-all-start = ((f32[16,32,128]{2,1,0:T(8,128)}), f32[16,32,128]{2,1,0:T(8,128)S(1)}, u32[]{:S(2)}, u32[]{:S(2)}) async-start(f32[16,32,128]{2,1,0:T(8,128)} %copy-done.13), calls=%async_computation | async-start | bytes 524288 | tf_op jit(solution)/shard_map/all_to_all | solution.py:247
  50.3 0.6 pad_clamp_fusion
  50.9 0.7 reshape.782
  51.7 3.9 %collective-permute-done.2.refs_3_.refs_2_ = f32[2,640,256]{2,1,0:T(8,128)} collective-permute-done((f32[2,640,256]{2,1,0:T(8,128)}, f32[2,640,256]{2,1,0:T(8,128)}, u32[]{:S(2)}, u32[]{:S(2)}) %collective-permute-start.2) | collective-permute-done | bytes 1310752 | tf_op jit(solution)/shard_map/ppermute | solution.py:223
  55.6 1.1 slice.64
  56.7 1.1 pad_maximum_fusion
  57.9 1.9 %collective-permute-start.3 = (f32[2,640,256]{2,1,0:T(8,128)}, f32[2,640,256]{2,1,0:T(8,128)}, u32[]{:S(2)}, u32[]{:S(2)}) collective-permute-start(f32[2,640,256]{2,1,0:T(8,128)} %pad_maximum_fusion), channel_id=1, source_target_pairs={{0,64},{64,0},{128,192},{192,128},{256,320},{320,256},{384,448},{4... | collective-permute-start | bytes 3932168 | tf_op jit(solution)/shard_map/ppermute | solution.py:218
  59.8 0.8 constant_dynamic-slice_fusion
  60.5 1.3 gather_fusion.4
  61.8 1.3 gather_fusion.5
  63.1 0.8 broadcast_subtract_fusion
  63.8 2.3 %collective-permute-start.4 = (f32[2,640,256]{2,1,0:T(8,128)}, f32[2,640,256]{2,1,0:T(8,128)}, u32[]{:S(2)}, u32[]{:S(2)}) collective-permute-start(f32[2,640,256]{2,1,0:T(8,128)} %copy-done.15), channel_id=1, source_target_pairs={{0,256},{64,320},{128,384},{192,448},{256,0},{320,64},{384,128},{4... | collective-permute-start | bytes 3932168 | tf_op jit(solution)/shard_map/ppermute | solution.py:252
  66.2 0.8 subtract_select_fusion
  67.0 0.6 fusion.10
  67.7 0.7 copy-done.12
  68.4 8.4 %all-to-all-start.1 = ((f32[16,40,128]{2,1,0:T(8,128)}), f32[16,40,128]{2,1,0:T(8,128)}, u32[]{:S(2)}, u32[]{:S(2)}) async-start(f32[16,40,128]{2,1,0:T(8,128)} %copy-done.12), calls=%async_computation.1 | async-start | bytes 655360 | tf_op jit(solution)/shard_map/all_to_all | solution.py:247
  76.8 0.7 slice.37
  77.6 11.7 %all-to-all-done.1.amplitude_ref = f32[16,40,128]{2,1,0:T(8,128)} async-done(((f32[16,40,128]{2,1,0:T(8,128)}), f32[16,40,128]{2,1,0:T(8,128)}, u32[]{:S(2)}, u32[]{:S(2)}) %all-to-all-start.1) | async-done | bytes 327712 | tf_op jit(solution)/shard_map/all_to_all | solution.py:247
  89.3 2.7 %exchange.7 = f32[16,64,128]{2,1,0:T(8,128)S(1)} custom-call(s32[8]{0:T(128)S(1)} %reshape.780.refs_0_.first_ref, bf16[6,256,640]{2,1,0:T(8,128)(2,1)S(1)} %left.1.refs_1_.refs_3_, f32[2,640,256]{2,1,0:T(8,128)S(1)} %collective-permute-done.1.refs_2_.refs_1_, f32[2,640,256]{2,1,0:T(8,128)} %collective-permute-done.2.refs_3_.refs_2_, ...), custom_call_target="tpu_custom_call" | custom-call | flops 671088640 | bytes 1048576 | tf_op jit(solution)/shard_map/exchange/pallas_call | solution.py:128
  92.0 0.8 copy-done.7
  92.8 4.5 %all-to-all-start.2 = ((f32[16,64,128]{2,1,0:T(8,128)}), f32[16,64,128]{2,1,0:T(8,128)}, u32[]{:S(2)}, u32[]{:S(2)}) async-start(f32[16,64,128]{2,1,0:T(8,128)} %copy-done.7), calls=%async_computation.2 | async-start | bytes 1048576 | tf_op jit(solution)/shard_map/all_to_all | solution.py:247
  97.3 1.5 collective-permute-done.4.refs_4_.refs_1_
  98.7 2.0 %slice.66 = f32[1,640,256]{2,1,0:T(8,128)} slice(f32[2,640,256]{2,1,0:T(8,128)} %collective-permute-done.4.refs_4_.refs_1_), slice={[1:2], [0:640], [0:256]} | slice | bytes 1310720 | tf_op jit(solution)/shard_map/slice | solution.py:261
  100.7 1.9 %collective-permute-start.5 = (f32[1,640,256]{2,1,0:T(8,128)}, f32[1,640,256]{2,1,0:T(8,128)}, u32[]{:S(2)}, u32[]{:S(2)}) collective-permute-start(f32[1,640,256]{2,1,0:T(8,128)} %slice.66), channel_id=1, source_target_pairs={{0,64},{64,0},{128,192},{192,128},{256,320},{320,256},{384,448},{4... | collective-permute-start | bytes 1966088 | tf_op jit(solution)/shard_map/ppermute | solution.py:218
  102.7 2.3 %collective-permute-done.5.refs_5_.refs_2_ = f32[1,640,256]{2,1,0:T(8,128)} collective-permute-done((f32[1,640,256]{2,1,0:T(8,128)}, f32[1,640,256]{2,1,0:T(8,128)}, u32[]{:S(2)}, u32[]{:S(2)}) %collective-permute-start.5) | collective-permute-done | bytes 655392 | tf_op jit(solution)/shard_map/ppermute | solution.py:218
  105.0 7.2 %all-to-all-done.2.refs_0_ = f32[16,64,128]{2,1,0:T(8,128)} async-done(((f32[16,64,128]{2,1,0:T(8,128)}), f32[16,64,128]{2,1,0:T(8,128)}, u32[]{:S(2)}, u32[]{:S(2)}) %all-to-all-start.2) | async-done | bytes 524320 | tf_op jit(solution)/shard_map/all_to_all | solution.py:247
  112.2 2.3 %exchange.8 = f32[16,104,128]{2,1,0:T(8,128)S(1)} custom-call(f32[16,64,128]{2,1,0:T(8,128)} %all-to-all-done.2.refs_0_, f32[64,128]{1,0:T(8,128)S(1)} %bitcast.68, s32[4]{0:T(128)S(1)} %reshape.779.refs_2_.first_ref, bf16[6,256,640]{2,1,0:T(8,128)(2,1)S(1)} %left.1.refs_1_.refs_3_, f32[2,640,256]{2,1,0:T(8,128)} %collective-permute-done.4.refs_4_.refs_1_, ...), custom_call_target="tpu_custom_call" | custom-call | flops 335544320 | bytes 1703936 | tf_op jit(solution)/shard_map/exchange/pallas_call | solution.py:128
  114.5 28.8 %all_to_all.25.amplitude_ref = f32[16,104,128]{2,1,0:T(8,128)S(1)} all-to-all(f32[16,104,128]{2,1,0:T(8,128)S(1)} %exchange.8), channel_id=1, replica_groups=mesh['occ'=8,'aux'=16,'vir'=4] {'aux'}, dimensions={0} | all-to-all | bytes 1703936 | tf_op jit(solution)/shard_map/all_to_all | solution.py:247
  143.4 0.8 exchange.9
  144.2 4.6 %all-to-all-start.4 = ((f32[16,40,128]{2,1,0:T(8,128)}), f32[16,40,128]{2,1,0:T(8,128)S(1)}, u32[]{:S(2)}, u32[]{:S(2)}) async-start(f32[16,40,128]{2,1,0:T(8,128)} %exchange.9), calls=%async_computation.4 | async-start | bytes 655360 | tf_op jit(solution)/shard_map/all_to_all | solution.py:247
  148.9 1.9 %gamma.3 = (f32[632,768]{1,0:T(8,128)S(1)}, f32[8,128]{1,0:T(8,128)S(1)}) custom-call(s32[4]{0:T(128)S(1)} %reshape.781.refs_0_.first_ref, f32[16,40,128]{2,1,0:T(8,128)} %all-to-all-done.1.amplitude_ref, f32[1,640,256]{2,1,0:T(8,128)S(1)} %copy-done.6, f32[1,640,256]{2,1,0:T(8,128)} %collective-permute-done.refs_3_.refs_1_), custom_call_target="tpu_custom_call" | custom-call | flops 331350016 | bytes 3883008 | tf_op jit(solution)/shard_map/gamma/pallas_call | solution.py:179
  150.8 1.3 copy-done.10
  152.2 0.1 reduce_sum.46
  152.4 1.5 copy-done.11
  153.9 2.8 %gamma.4 = (f32[632,768]{1,0:T(8,128)S(1)}, f32[8,128]{1,0:T(8,128)S(1)}) custom-call(s32[8]{0:T(128)S(1)} %reshape.780.refs_0_.first_ref, f32[16,104,128]{2,1,0:T(8,128)S(1)} %all_to_all.25.amplitude_ref, f32[632,768]{1,0:T(8,128)S(1)} %copy-done.11, f32[2,640,256]{2,1,0:T(8,128)S(1)} %collective-permute-done.1.refs_2_.refs_1_, ...), custom_call_target="tpu_custom_call" | custom-call | flops 662700032 | bytes 3883008 | tf_op jit(solution)/shard_map/gamma/pallas_call | solution.py:179
  156.7 1.3 copy-done.8
  158.3 2.2 %all-to-all-done.4.amplitude_ref = f32[16,40,128]{2,1,0:T(8,128)S(1)} async-done(((f32[16,40,128]{2,1,0:T(8,128)}), f32[16,40,128]{2,1,0:T(8,128)S(1)}, u32[]{:S(2)}, u32[]{:S(2)}) %all-to-all-start.4) | async-done | bytes 327712 | tf_op jit(solution)/shard_map/all_to_all | solution.py:247
  160.5 1.5 copy-done.9
  162.1 3.5 %gamma.5 = (f32[632,768]{1,0:T(8,128)}, f32[8,128]{1,0:T(8,128)S(1)}) custom-call(s32[4]{0:T(128)S(1)} %reshape.779.refs_2_.first_ref, f32[16,40,128]{2,1,0:T(8,128)S(1)} %all-to-all-done.4.amplitude_ref, f32[632,768]{1,0:T(8,128)S(1)} %copy-done.9, f32[2,640,256]{2,1,0:T(8,128)} %collective-permute-done.4.refs_4_.refs_1_, ...), custom_call_target="tpu_custom_call" | custom-call | flops 331350016 | bytes 3883008 | tf_op jit(solution)/shard_map/gamma/pallas_call | solution.py:179
  166.0 12.5 %psum.7 = f32[1,8]{1,0:T(1,128)} all-reduce(f32[1,8]{1,0:T(1,128)S(1)} %bitcast.78), channel_id=1, replica_groups=mesh['occ'=8,'aux'=16,'vir'=4] {'vir'}, use_global_device_ids=true, to_apply=%region_7.8 | all-reduce | flops 8 | bytes 64 | tf_op jit(solution)/shard_map/psum | solution.py:275
  (78 shorter events, 2.8 us)
Async XLA Ops:
  0.6 35.1 %copy-start = (s32[1,8]{1,0:T(1,128)S(1)}, s32[1,8]{1,0:T(1,128)}, u32[]{:S(2)}) copy-start(s32[1,8]{1,0:T(1,128)} %param.9) | copy-start | bytes 100
  14.3 1.5 copy-start.1
  15.9 8.9 %copy-start.2 = (f32[1,632,768]{2,1,0:T(8,128)S(1)}, f32[1,632,768]{2,1,0:T(8,128)}, u32[]{:S(2)}) copy-start(f32[1,632,768]{2,1,0:T(8,128)} %param.5) | copy-start | bytes 5824516
  18.1 12.2 %copy-start.21 = (s32[1,8,1,2]{1,3,2,0:T(2,128)S(1)}, s32[1,8,1,2]{1,3,2,0:T(2,128)}, u32[]{:S(2)}) copy-start(s32[1,8,1,2]{1,3,2,0:T(2,128)} %param.8) | copy-start | bytes 196
  18.1 33.5 %collective-permute-start.1 = (f32[2,640,256]{2,1,0:T(8,128)}, f32[2,640,256]{2,1,0:T(8,128)S(1)}, u32[]{:S(2)}, u32[]{:S(2)}) collective-permute-start(f32[2,640,256]{2,1,0:T(8,128)} %get-tuple-element.21), channel_id=1, source_target_pairs={{0,128},{64,192},{128,256},{192,320},{256,384},{320,448},{384,0},{... | collective-permute-start | bytes 3932168 | tf_op jit(solution)/shard_map/ppermute | solution.py:222
  21.4 34.1 %collective-permute-start.2 = (f32[2,640,256]{2,1,0:T(8,128)}, f32[2,640,256]{2,1,0:T(8,128)}, u32[]{:S(2)}, u32[]{:S(2)}) collective-permute-start(f32[2,640,256]{2,1,0:T(8,128)} %get-tuple-element.22), channel_id=1, source_target_pairs={{0,384},{64,448},{128,0},{192,64},{256,128},{320,192},{384,256},{4... | collective-permute-start | bytes 3932168 | tf_op jit(solution)/shard_map/ppermute | solution.py:223
  26.3 0.9 copy-start.4
  27.2 1.1 copy-start.15
  28.2 10.6 %collective-permute-start = (f32[1,640,256]{2,1,0:T(8,128)}, f32[1,640,256]{2,1,0:T(8,128)}, u32[]{:S(2)}, u32[]{:S(2)}) collective-permute-start(f32[1,640,256]{2,1,0:T(8,128)} %get-tuple-element.18), channel_id=1, source_target_pairs={{0,64},{64,0},{128,192},{192,128},{256,320},{320,256},{384,448},{4... | collective-permute-start | bytes 1966088 | tf_op jit(solution)/shard_map/ppermute | solution.py:218
  31.0 0.8 copy-start.20
  31.8 1.5 copy-start.3
  33.4 0.7 copy-start.16
  38.8 1.1 copy-start.5
  39.9 11.1 %copy-start.17 = (f32[768]{0:T(1024)S(1)}, f32[768]{0:T(1024)}, u32[]{:S(2)}) copy-start(f32[768]{0:T(1024)} %param.7) | copy-start | bytes 9220
  41.6 0.7 copy-start.13
  42.3 21.6 %all-to-all-start = ((f32[16,32,128]{2,1,0:T(8,128)}), f32[16,32,128]{2,1,0:T(8,128)S(1)}, u32[]{:S(2)}, u32[]{:S(2)}) async-start(f32[16,32,128]{2,1,0:T(8,128)} %copy-done.13), calls=%async_computation | async-start | bytes 524288 | tf_op jit(solution)/shard_map/all_to_all | solution.py:247
  57.9 31.4 %collective-permute-start.3 = (f32[2,640,256]{2,1,0:T(8,128)}, f32[2,640,256]{2,1,0:T(8,128)}, u32[]{:S(2)}, u32[]{:S(2)}) collective-permute-start(f32[2,640,256]{2,1,0:T(8,128)} %pad_maximum_fusion), channel_id=1, source_target_pairs={{0,64},{64,0},{128,192},{192,128},{256,320},{320,256},{384,448},{4... | collective-permute-start | bytes 3932168 | tf_op jit(solution)/shard_map/ppermute | solution.py:218
  63.8 34.9 %collective-permute-start.4 = (f32[2,640,256]{2,1,0:T(8,128)}, f32[2,640,256]{2,1,0:T(8,128)}, u32[]{:S(2)}, u32[]{:S(2)}) collective-permute-start(f32[2,640,256]{2,1,0:T(8,128)} %copy-done.15), channel_id=1, source_target_pairs={{0,256},{64,320},{128,384},{192,448},{256,0},{320,64},{384,128},{4... | collective-permute-start | bytes 3932168 | tf_op jit(solution)/shard_map/ppermute | solution.py:252
  67.0 0.7 copy-start.18
  67.7 0.7 copy-start.12
  68.4 20.9 %all-to-all-start.1 = ((f32[16,40,128]{2,1,0:T(8,128)}), f32[16,40,128]{2,1,0:T(8,128)}, u32[]{:S(2)}, u32[]{:S(2)}) async-start(f32[16,40,128]{2,1,0:T(8,128)} %copy-done.12), calls=%async_computation.1 | async-start | bytes 655360 | tf_op jit(solution)/shard_map/all_to_all | solution.py:247
  92.0 0.8 copy-start.7
  92.8 9.8 %copy-start.19 = (f32[8,2,8,128]{3,2,1,0:T(8,128)S(1)}, f32[8,2,8,128]{3,2,1,0:T(8,128)}, u32[]{:S(2)}) copy-start(f32[8,2,8,128]{3,2,1,0:T(8,128)} %copy-done.18) | copy-start | bytes 196612
  92.8 9.8 %copy-start.22 = (s32[2,2]{1,0:T(2,128)S(1)}, s32[2,2]{1,0:T(2,128)}, u32[]{:S(2)}) copy-start(s32[2,2]{1,0:T(2,128)} %get-tuple-element.39) | copy-start | bytes 52
  92.8 19.4 %all-to-all-start.2 = ((f32[16,64,128]{2,1,0:T(8,128)}), f32[16,64,128]{2,1,0:T(8,128)}, u32[]{:S(2)}, u32[]{:S(2)}) async-start(f32[16,64,128]{2,1,0:T(8,128)} %copy-done.7), calls=%async_computation.2 | async-start | bytes 1048576 | tf_op jit(solution)/shard_map/all_to_all | solution.py:247
  100.7 4.3 %collective-permute-start.5 = (f32[1,640,256]{2,1,0:T(8,128)}, f32[1,640,256]{2,1,0:T(8,128)}, u32[]{:S(2)}, u32[]{:S(2)}) collective-permute-start(f32[1,640,256]{2,1,0:T(8,128)} %slice.66), channel_id=1, source_target_pairs={{0,64},{64,0},{128,192},{192,128},{256,320},{320,256},{384,448},{4... | collective-permute-start | bytes 1966088 | tf_op jit(solution)/shard_map/ppermute | solution.py:218
  114.5 28.9 %copy-start.14 = (f32[2,2,8,128]{3,2,1,0:T(8,128)S(1)}, f32[2,2,8,128]{3,2,1,0:T(8,128)}, u32[]{:S(2)}) copy-start(f32[2,2,8,128]{3,2,1,0:T(8,128)} %get-tuple-element.32) | copy-start | bytes 49156
  143.4 5.5 %copy-start.6 = (f32[1,640,256]{2,1,0:T(8,128)S(1)}, f32[1,640,256]{2,1,0:T(8,128)}, u32[]{:S(2)}) copy-start(f32[1,640,256]{2,1,0:T(8,128)} %copy-done.4) | copy-start | bytes 1966084
  144.2 16.4 %all-to-all-start.4 = ((f32[16,40,128]{2,1,0:T(8,128)}), f32[16,40,128]{2,1,0:T(8,128)S(1)}, u32[]{:S(2)}, u32[]{:S(2)}) async-start(f32[16,40,128]{2,1,0:T(8,128)} %exchange.9), calls=%async_computation.4 | async-start | bytes 655360 | tf_op jit(solution)/shard_map/all_to_all | solution.py:247
  150.8 1.3 copy-start.10
  152.4 1.5 copy-start.11
  156.7 1.3 copy-start.8
  160.5 1.5 copy-start.9

commit v3 on v2

v3 whole, which is shorter than its diff:
```python
import functools

import jax
import jax.numpy as jnp
from jax import lax
from jax.experimental import pallas as pl
from jax.experimental.pallas import tpu as pltpu
from jax.sharding import PartitionSpec as P

TILE = 128
CHIPS = 4
VMEM = pl.BlockSpec(memory_space=pltpu.VMEM)
SMEM = pl.BlockSpec(memory_space=pltpu.SMEM)
def params():
    return pltpu.CompilerParams(vmem_limit_bytes=12 * 1024 * 1024)


def cost(flops, moved):
    return pl.CostEstimate(flops=flops, bytes_accessed=moved, transcendentals=0)


def split(value):
    high = value.astype(jnp.bfloat16)
    low = (value - high.astype(jnp.float32)).astype(jnp.bfloat16)
    return high, low


def lanes(index):
    return pl.ds(pl.multiple_of(index * TILE, TILE), TILE)


def partner_of(ids_ref, dx, dc):
    me = ids_ref[0]
    return lax.rem(me // 2 + CHIPS - dx, CHIPS) * 2 + lax.rem(me + dc, 2)


def pick_kernel(shifts, ids_ref, pairs_ref, block_ref, *out_refs):
    rows, cols = block_ref.shape
    slots = [(out_ref, k) for out_ref in out_refs for k in range(out_ref.shape[0])]
    for (out_ref, k), (dx, dc) in zip(slots, shifts):
        receiver = partner_of(ids_ref, CHIPS - dx, dc)
        for s in range(2):
            tile = lax.rem(pairs_ref[(receiver * 2 * CHIPS + ids_ref[0]) * 2 + s], cols // TILE)
            out_ref[k, :rows, s * TILE : (s + 1) * TILE] = block_ref[:, lanes(tile)]
        out_ref[k, rows:, :] = jnp.zeros((out_ref.shape[1] - rows, 2 * TILE), jnp.float32)


def pick(ids, pairs, block, shifts, counts, padded):
    return pl.pallas_call(
        functools.partial(pick_kernel, shifts),
        out_shape=[jax.ShapeDtypeStruct((count, padded, 2 * TILE), jnp.float32) for count in counts],
        in_specs=[SMEM, SMEM, VMEM],
        out_specs=[VMEM] * len(counts),
        compiler_params=params(),
        cost_estimate=cost(0, sum(counts) * padded * 4 * TILE * 4),
        name="pick",
    )(ids, pairs, block)


def left_kernel(block_ref, out_ref):
    rows = block_ref.shape[0]
    padded = out_ref.shape[2]
    for f in range(out_ref.shape[0]):
        tile = block_ref[:, f * TILE : (f + 1) * TILE]
        tile = jnp.concatenate([tile, jnp.zeros((padded - rows, TILE), jnp.float32)], axis=0)
        high, low = split(tile.T)
        out_ref[f, :TILE, :] = high
        out_ref[f, TILE:, :] = low


def left(block, padded):
    tiles = block.shape[1] // TILE
    return pl.pallas_call(
        left_kernel,
        out_shape=jax.ShapeDtypeStruct((tiles, 2 * TILE, padded), jnp.bfloat16),
        in_specs=[VMEM],
        out_specs=VMEM,
        compiler_params=params(),
        cost_estimate=cost(0, block.size * 8),
        name="left",
    )(block)


def tiles_of(scalars, shift, s, tile_count):
    ids_ref, own_ref = scalars[:2]
    partner = partner_of(ids_ref, *shift)
    entry = own_ref[2 * partner + s]
    return partner, lax.div(entry, tile_count), lax.rem(entry, tile_count)


def add_amplitude(scalars, shifts, parts_ref, columns_ref, levels_ref, out_ref):
    ids_ref, _, occ_ref, live_ref = scalars
    count = 2 * len(shifts)
    energies = []
    for k, shift in enumerate(shifts):
        for s in range(2):
            t = 2 * k + s
            partner, first, second = tiles_of(scalars, shift, s, levels_ref.shape[0])
            row = pl.multiple_of(first * TILE + 8 * ids_ref[1], 8)
            denominator = (
                occ_ref[ids_ref[0]] + occ_ref[partner] - columns_ref[pl.ds(row, 8), :] - levels_ref[pl.ds(second, 1), :]
            )
            summed = jnp.sum(parts_ref[:, 8 * t : 8 * t + 8, :], axis=0)
            denominator = jnp.where(s < live_ref[partner], denominator, jnp.inf)
            amplitude = summed / denominator
            energies.append(jnp.sum(summed * amplitude, axis=0, keepdims=True))
            for owner in range(out_ref.shape[0]):
                out_ref[owner, 8 * t : 8 * t + 8, :] = amplitude
    energies.append(jnp.zeros((-count % 8, TILE), jnp.float32)) if count % 8 else None
    energy = jnp.concatenate(energies, axis=0)
    done = 8 * count + energy.shape[0]
    for owner in range(out_ref.shape[0]):
        out_ref[owner, 8 * count : done, :] = energy
    return done


def returned_rows(tiles):
    return 8 * tiles + -(-tiles // 8) * 8


def exchange_kernel(back_shifts, shifts, entries, *refs):
    *in_refs, out_ref = refs
    scalars, in_refs = in_refs[:4], in_refs[4:]
    at = 0
    if back_shifts:
        parts_ref, columns_ref, levels_ref, *in_refs = in_refs
        at = add_amplitude(scalars, back_shifts, parts_ref, columns_ref, levels_ref, out_ref)
    if entries:
        left_ref, *right_refs = in_refs
        for k, ((which, entry), shift) in enumerate(zip(entries, shifts)):
            for s in range(2):
                t = 2 * k + s
                _, first, _ = tiles_of(scalars, shift, s, left_ref.shape[0])
                high, low = split(right_refs[which][entry, :, s * TILE : (s + 1) * TILE])
                both = jnp.concatenate([high, low], axis=1)
                part = jnp.dot(left_ref[first], both, preferred_element_type=jnp.float32)
                cross = part[:TILE, TILE:] + part[TILE:, :TILE] + part[TILE:, TILE:]
                total = part[:TILE, :TILE] + cross
                out_ref[:, at + 8 * t : at + 8 * t + 8, :] = total.reshape(TILE // 8, 8, TILE)


def exchange(scalars, returned, group):
    inputs, specs, rows, flops = list(scalars), [SMEM] * 4, 0, 0
    back_shifts, shifts, entries = (), (), ()
    if returned is not None:
        back_shifts, parts, columns, levels = returned
        inputs += [parts, columns, levels]
        specs += [VMEM] * 3
        rows += returned_rows(2 * len(back_shifts))
    if group is not None:
        shifts, left_split, rights = group
        arrays, entries = unique(rights)
        inputs += [left_split, *arrays]
        specs += [VMEM] * (1 + len(arrays))
        rows += 16 * len(entries)
        flops = len(entries) * 16 * TILE * TILE * left_split.shape[2]
    return pl.pallas_call(
        functools.partial(exchange_kernel, back_shifts, shifts, entries),
        out_shape=jax.ShapeDtypeStruct((TILE // 8, rows, TILE), jnp.float32),
        in_specs=specs,
        out_specs=VMEM,
        compiler_params=params(),
        cost_estimate=cost(flops, TILE // 8 * rows * TILE * 8),
        name="exchange",
    )(*inputs)


def unique(rights):
    arrays, entries = [], []
    for array, entry in rights:
        which = next((k for k, known in enumerate(arrays) if known is array), len(arrays))
        if which == len(arrays):
            arrays.append(array)
        entries.append((which, entry))
    return arrays, entries


def gamma_kernel(groups, carried, *refs):
    scalars, refs = refs[:4], refs[4:]
    if carried:
        gamma_in, *refs = refs
    *in_refs, gamma_ref, energy_ref = refs
    rows, cols = gamma_ref.shape
    gamma_ref[...] = gamma_in[...] if carried else jnp.zeros_like(gamma_ref)
    energy_at = 0
    for shifts, entries, arrays in groups:
        (amplitude_ref, *right_refs), in_refs = in_refs[: 1 + arrays], in_refs[1 + arrays :]
        count = 2 * len(entries)
        for k, ((which, entry), shift) in enumerate(zip(entries, shifts)):
            for s in range(2):
                t = 2 * k + s
                _, first, _ = tiles_of(scalars, shift, s, cols // TILE)
                high, low = split(amplitude_ref[:, 8 * t : 8 * t + 8, :].reshape(TILE, TILE))
                weights = jnp.concatenate(
                    [
                        jnp.concatenate([high, high], axis=1),
                        jnp.concatenate([low, low], axis=1),
                    ],
                    axis=0,
                )
                both = jnp.concatenate(split(right_refs[which][entry, :, s * TILE : (s + 1) * TILE]), axis=1)
                part = lax.dot_general(both, weights, (((1,), (1,)), ((), ())), preferred_element_type=jnp.float32)
                place = lanes(first)
                gamma_ref[:, place] += (part[:, :TILE] + part[:, TILE:])[:rows]
        extra = returned_rows(count) - 8 * count
        energy = jnp.sum(amplitude_ref[:, 8 * count : 8 * count + extra, :], axis=0)
        energy_ref[energy_at : energy_at + extra, :] = energy
        energy_at += extra


def gamma_add(scalars, groups, rows, cols, carried):
    inputs, extra, tiles = [], 0, 0
    described = []
    for shifts, amplitudes, rights in groups:
        arrays, entries = unique(rights)
        described.append((shifts, entries, len(arrays)))
        inputs += [amplitudes, *arrays]
        extra += returned_rows(2 * len(shifts)) - 16 * len(shifts)
        tiles += 2 * len(shifts)
    start = list(scalars) + ([carried] if carried is not None else [])
    return pl.pallas_call(
        functools.partial(gamma_kernel, described, carried is not None),
        out_shape=[
            jax.ShapeDtypeStruct((rows, cols), jnp.float32),
            jax.ShapeDtypeStruct((extra, TILE), jnp.float32),
        ],
        in_specs=[SMEM] * 4 + [VMEM] * (len(start) - 4 + len(inputs)),
        out_specs=[VMEM, VMEM],
        compiler_params=params(),
        cost_estimate=cost(tiles * 8 * TILE * TILE * rows, rows * cols * 8),
        name="gamma",
    )(*start, *inputs)


EARLY = ((0, 0), (0, 1))
NEAR = ((1, 0), (3, 0), (1, 1), (3, 1))
FAR = ((2, 0), (2, 1))


def per_device(bq, eps_occ, eps_vir, tile_pairs, live_counts):
    occ_size = lax.axis_size("occ")
    me = lax.axis_index("occ")
    block = bq[0]
    rows, cols = block.shape
    padded = -(-rows // 16) * 16
    own_pairs = tile_pairs.reshape(-1)
    all_pairs = lax.all_gather(tile_pairs[0, :, 0, :], "occ").reshape(-1)
    ids = jnp.stack([me, lax.axis_index("aux")]).astype(jnp.int32)
    scalars = (ids, own_pairs, eps_occ, live_counts.reshape(-1))
    columns = jnp.broadcast_to(eps_vir[:, None], (cols, TILE))
    levels = eps_vir.reshape(cols // TILE, TILE)

    def route(dx, dc):
        return [(x * 2 + c, (x + dx) % CHIPS * 2 + (c + dc) % 2) for x in range(CHIPS) for c in range(2)]

    def swapped(tiles):
        return lax.ppermute(tiles, "occ", route(0, 1))

    def sent(returned, group):
        return lax.all_to_all(exchange(scalars, returned, group), "aux", 0, 0)

    ahead, behind = pick(ids, all_pairs, block, ((1, 0), (1, 1), (3, 0), (3, 1)), (2, 2), padded)
    ahead = lax.ppermute(ahead, "occ", route(1, 0))
    behind = lax.ppermute(behind, "occ", route(3, 0))
    own, mate, far = pick(ids, all_pairs, block, ((0, 0), (0, 1), (2, 0), (2, 1)), (1, 1, 2), padded)
    mate = swapped(mate)
    left_split = left(block, padded)

    early_rights = [(own, 0), (mate, 0)]
    early_parts = sent(None, (EARLY, left_split, early_rights))
    far, early_parts = lax.optimization_barrier((far, early_parts))
    far = lax.ppermute(far, "occ", route(2, 0))
    early = sent((EARLY, early_parts, columns, levels), None)

    near_mate = swapped(jnp.stack([ahead[1], behind[1]]))
    near_rights = [(ahead, 0), (behind, 0), (near_mate, 0), (near_mate, 1)]
    near_left, early = lax.optimization_barrier((left_split, early))
    near_parts = sent(None, (NEAR, near_left, near_rights))

    far_mate = swapped(far[1:])
    far_rights = [(far, 0), (far_mate, 0)]
    both = sent((NEAR, near_parts, columns, levels), (FAR, left_split, far_rights))
    near_rows = returned_rows(2 * len(NEAR))
    last = sent((FAR, both[:, near_rows:], columns, levels), None)
    total, energy = gamma_add(scalars, [(EARLY, early, early_rights), (NEAR, both, near_rights)], rows, cols, None)
    total, last_energy = gamma_add(scalars, [(FAR, last, far_rights)], rows, cols, total)

    energies = []
    for value, shifts, at in ((energy, EARLY, 0), (energy, NEAR, 8), (last_energy, FAR, 0)):
        pairs = value[at : at + 2 * len(shifts)].reshape(len(shifts), 2 * TILE)
        energies.append(jnp.sum(pairs, axis=1))
    order = jnp.stack([(me // 2 - dx) % CHIPS * 2 + (me + dc) % 2 for dx, dc in EARLY + NEAR + FAR])
    mine = order[:, None] == jnp.arange(occ_size)[None, :]
    energy = jnp.sum(jnp.where(mine, jnp.concatenate(energies)[:, None], 0.0), axis=0)
    energy = lax.psum(energy[None], "vir")
    return total[None], energy


def solution(mesh):
    return jax.shard_map(
        per_device,
        mesh=mesh,
        in_specs=(
            P("occ", "aux", "vir"),
            P(),
            P("vir"),
            P("occ", None, "vir", None),
            P("occ", None),
        ),
        out_specs=(P("occ", "aux", "vir"), P("occ", None)),
        check_vma=False,
    )
```

time: 182 us -> 180 us (0.989)
  blocking collectives: 54 us -> 74.6 us
  local copies, waits for them, and re-layouts: 28.2 us -> 19.1 us
  starting transfers between devices: 39.5 us -> 31.1 us
  other arithmetic: 6.77 us -> 2.08 us
    all_to_all x1 -> x2, blocking collectives: 28.8 us -> 49.5 us  [sent(): return lax.all_to_all(exchange(scalars, returned, group), 'aux', 0, 0)]
    all_to_all x4 -> x3, starting transfers between devices: 25.5 us -> 17.1 us  [sent(): return lax.all_to_all(exchange(scalars, returned, group), 'aux', 0, 0)]
    ppermute x1, waiting for transfers between devices: 0.01 us -> 7.9 us  [per_device(): ahead = lax.ppermute(ahead, 'occ', route(1, 0))]
    all_to_all x4 -> x3, waiting for transfers between devices: 21.1 us -> 13.6 us  [sent(): return lax.all_to_all(exchange(scalars, returned, group), 'aux', 0, 0)]
    gather x7 -> x0, local copies, waits for them, and re-layouts: 5.5 us -> none  [the longest x1 1.27 us: per_device(): vir_rows[first][:, :, :, None]]
    unnamed x47 -> x45, local copies, waits for them, and re-layouts: 14 us -> 15.9 us
    slice x5 -> x1, local copies, waits for them, and re-layouts: 1.86 us -> 0.02 us  [per_device(): last = sent((FAR, both[:, near_rows:], columns, levels), None)]
    pallas_call x10 -> x9, Pallas kernels: 19.5 us -> 19.2 us  [the longest x5 8.49 us: exchange(): pl.pallas_call(functools.partial(exchange_kernel, back_shifts, shifts, en...]
  transfers between devices with their start and end apart: 10 -> 9, of which waited for: 6 -> 7; matrix products, arithmetic and copies ran while one was open for 11% -> 3% of each run, Pallas kernels for 6% -> 6%
where the time goes in v3:
time: 180 us; the launch traced here: 177 us
  blocking collectives  74.6 us (41%)
  starting transfers between devices  31.1 us (17%)
  waiting for transfers between devices  29.6 us (16%)
  Pallas kernels  19.7 us (11%)
  local copies, waits for them, and re-layouts  19.1 us (11%)
  other arithmetic  2.08 us (1%)
    all_to_all x2, blocking collectives, sent(): return lax.all_to_all(exchange(scalars, returned, group), 'aux', 0, 0)  49.5 us
    all_to_all x3, starting transfers between devices, sent(): return lax.all_to_all(exchange(scalars, returned, group), 'aux', 0, 0)  17.1 us
    unnamed x45, local copies, waits for them, and re-layouts  15.9 us
    all_to_all x3, waiting for transfers between devices, sent(): return lax.all_to_all(exchange(scalars, returned, group), 'aux', 0, 0)  13.6 us
    all_gather x1, blocking collectives, per_device(): all_pairs = lax.all_gather(tile_pairs[0, :, 0, :], 'occ').reshape(-1)  12.7 us
    psum x1, blocking collectives, per_device(): energy = lax.psum(energy[None], 'vir')  12.5 us
    pallas_call x5, Pallas kernels, exchange(): pl.pallas_call(functools.partial(exchange_kernel, back_shifts, shifts, en...  8.49 us
    ppermute x1, waiting for transfers between devices, per_device(): ahead = lax.ppermute(ahead, 'occ', route(1, 0))  7.9 us
  transfers between devices with their start and end apart: 9, of which 7 were waited for; matrix products, arithmetic and copies ran while one was open for 3% of the time, Pallas kernels for 6%

profile of v3, /device:TPU:6, one launch (start us, length us, event | category | flops | bytes accessed | tf_op | source)
XLA Modules:
  0.0 177.1 jit_solution(9766423964765389496)
XLA Ops:
  0.6 12.7 %all-gather = s32[8,8,1,2]{1,3,2,0:T(2,128)S(1)} all-gather(s32[1,8,1,2]{1,3,2,0:T(2,128)} %param.8), channel_id=2, replica_groups=mesh['occ'=8,'aux'=16,'vir'=4] {'occ'}, dimensions={0}, use_global_device_ids=true | all-gather | bytes 576 | tf_op jit(solution)/shard_map/all_gather | solution.py:247
  13.3 0.1 copy.14
  13.4 0.1 reshape.27.pairs_ref
  13.6 0.1 pad_add_fusion.ids_ref.refs_0_
  13.7 1.5 copy-done
  15.2 2.2 %pick.3 = (f32[2,640,256]{2,1,0:T(8,128)}, f32[2,640,256]{2,1,0:T(8,128)}) custom-call(s32[2]{0:T(128)S(1)} %pad_add_fusion.ids_ref.refs_0_, s32[128]{0:T(128)S(1)} %reshape.27.pairs_ref, f32[632,768]{1,0:T(8,128)S(1)} %bitcast.23), custom_call_target="tpu_custom_call" | custom-call | bytes 5242880 | tf_op jit(solution)/shard_map/pick/pallas_call | solution.py:49
  17.4 3.3 %collective-permute-start.1 = (f32[2,640,256]{2,1,0:T(8,128)}, f32[2,640,256]{2,1,0:T(8,128)S(1)}, u32[]{:S(2)}, u32[]{:S(2)}) collective-permute-start(f32[2,640,256]{2,1,0:T(8,128)} %get-tuple-element.21), channel_id=1, source_target_pairs={{0,128},{64,192},{128,256},{192,320},{256,384},{320,448},{384,0},{... | collective-permute-start | bytes 3932168 | tf_op jit(solution)/shard_map/ppermute | solution.py:263
  20.8 2.6 %collective-permute-start.2 = (f32[2,640,256]{2,1,0:T(8,128)}, f32[2,640,256]{2,1,0:T(8,128)}, u32[]{:S(2)}, u32[]{:S(2)}) collective-permute-start(f32[2,640,256]{2,1,0:T(8,128)} %get-tuple-element.22), channel_id=1, source_target_pairs={{0,384},{64,448},{128,0},{192,64},{256,128},{320,192},{384,256},{4... | collective-permute-start | bytes 3932168 | tf_op jit(solution)/shard_map/ppermute | solution.py:264
  23.4 1.6 pick.2
  25.0 0.9 copy-done.4
  25.9 1.0 copy-done.20
  26.9 1.9 %collective-permute-start = (f32[1,640,256]{2,1,0:T(8,128)}, f32[1,640,256]{2,1,0:T(8,128)}, u32[]{:S(2)}, u32[]{:S(2)}) collective-permute-start(f32[1,640,256]{2,1,0:T(8,128)} %get-tuple-element.17), channel_id=1, source_target_pairs={{0,64},{64,0},{128,192},{192,128},{256,320},{320,256},{384,448},{4... | collective-permute-start | bytes 1966088 | tf_op jit(solution)/shard_map/ppermute | solution.py:257
  28.8 0.1 copy.13
  28.9 1.5 copy-done.1
  30.5 0.6 left.1.refs_4_.refs_7_
  31.1 0.1 collective-permute-done.refs_6_
  31.2 1.1 copy-done.5
  32.3 2.4 %exchange.5 = f32[16,32,128]{2,1,0:T(8,128)} custom-call(s32[2]{0:T(128)S(1)} %pad_add_fusion.ids_ref.refs_0_, s32[16]{0:T(128)S(1)} %reshape.25.refs_1_, f32[8]{0:T(128)S(1)} %copy-done.16, s32[8]{0:T(128)S(1)} %bitcast.29, bf16[6,256,640]{2,1,0:T(8,128)(2,1)S(1)} %left.1.refs_4_.refs_7_, f32[1,640,256]{2,1,0:T(8,128)S(1)} %copy-done.5, ...), custom_call_target="tpu_custom_call" | custom-call | flops 335544320 | bytes 524288 | tf_op jit(solution)/shard_map/exchange/pallas_call | solution.py:157
  34.7 8.0 %all-to-all-start = ((f32[16,32,128]{2,1,0:T(8,128)}), f32[16,32,128]{2,1,0:T(8,128)S(1)}, u32[]{:S(2)}, u32[]{:S(2)}) async-start(f32[16,32,128]{2,1,0:T(8,128)} %exchange.5), calls=%async_computation | async-start | bytes 524288 | tf_op jit(solution)/shard_map/all_to_all | solution.py:260
  42.8 7.9 %collective-permute-done.1.refs_5_.refs_8_ = f32[2,640,256]{2,1,0:T(8,128)S(1)} collective-permute-done((f32[2,640,256]{2,1,0:T(8,128)}, f32[2,640,256]{2,1,0:T(8,128)S(1)}, u32[]{:S(2)}, u32[]{:S(2)}) %collective-permute-start.1) | collective-permute-done | bytes 1310752 | tf_op jit(solution)/shard_map/ppermute | solution.py:263
  50.7 4.2 %collective-permute-done.2.refs_6_.refs_9_ = f32[2,640,256]{2,1,0:T(8,128)} collective-permute-done((f32[2,640,256]{2,1,0:T(8,128)}, f32[2,640,256]{2,1,0:T(8,128)}, u32[]{:S(2)}, u32[]{:S(2)}) %collective-permute-start.2) | collective-permute-done | bytes 1310752 | tf_op jit(solution)/shard_map/ppermute | solution.py:264
  54.9 1.1 slice.29
  56.1 1.1 pad_maximum_fusion
  57.2 1.9 %collective-permute-start.3 = (f32[2,640,256]{2,1,0:T(8,128)}, f32[2,640,256]{2,1,0:T(8,128)}, u32[]{:S(2)}, u32[]{:S(2)}) collective-permute-start(f32[2,640,256]{2,1,0:T(8,128)} %pad_maximum_fusion), channel_id=1, source_target_pairs={{0,64},{64,0},{128,192},{192,128},{256,320},{320,256},{384,448},{4... | collective-permute-start | bytes 3932168 | tf_op jit(solution)/shard_map/ppermute | solution.py:257
  59.1 2.3 %collective-permute-start.4 = (f32[2,640,256]{2,1,0:T(8,128)}, f32[2,640,256]{2,1,0:T(8,128)}, u32[]{:S(2)}, u32[]{:S(2)}) collective-permute-start(f32[2,640,256]{2,1,0:T(8,128)} %copy-done.20), channel_id=1, source_target_pairs={{0,256},{64,320},{128,384},{192,448},{256,0},{320,64},{384,128},{4... | collective-permute-start | bytes 3932168 | tf_op jit(solution)/shard_map/ppermute | solution.py:272
  61.5 0.2 broadcast_in_dim.27.refs_5_
  61.7 0.7 copy-done.18
  62.3 0.6 exchange.6
  62.9 0.7 copy-done.2
  63.7 20.6 %all_to_all.25.refs_4_ = f32[16,40,128]{2,1,0:T(8,128)} all-to-all(f32[16,40,128]{2,1,0:T(8,128)S(1)} %exchange.6), channel_id=1, replica_groups=mesh['occ'=8,'aux'=16,'vir'=4] {'aux'}, dimensions={0} | all-to-all | bytes 655360 | tf_op jit(solution)/shard_map/all_to_all | solution.py:260
  84.3 2.7 %exchange.7 = f32[16,64,128]{2,1,0:T(8,128)S(1)} custom-call(s32[2]{0:T(128)S(1)} %pad_add_fusion.ids_ref.refs_0_, s32[16]{0:T(128)S(1)} %reshape.25.refs_1_, f32[8]{0:T(128)S(1)} %copy-done.16, s32[8]{0:T(128)S(1)} %bitcast.31, bf16[6,256,640]{2,1,0:T(8,128)(2,1)S(1)} %left.1.refs_4_.refs_7_, f32[2,640,256]{2,1,0:T(8,128)S(1)} %collective-permute-done.1.refs_5_.refs_8_, ...), custom_call_target="tpu_custom_call" | custom-call | flops 671088640 | bytes 1048576 | tf_op jit(solution)/shard_map/exchange/pallas_call | solution.py:157
  87.1 0.8 copy-done.10
  87.8 4.5 %all-to-all-start.2 = ((f32[16,64,128]{2,1,0:T(8,128)}), f32[16,64,128]{2,1,0:T(8,128)}, u32[]{:S(2)}, u32[]{:S(2)}) async-start(f32[16,64,128]{2,1,0:T(8,128)} %copy-done.10), calls=%async_computation.2 | async-start | bytes 1048576 | tf_op jit(solution)/shard_map/all_to_all | solution.py:260
  92.3 1.7 collective-permute-done.4.refs_8_.refs_6_
  94.0 1.1 slice.30
  95.2 1.9 %collective-permute-start.5 = (f32[1,640,256]{2,1,0:T(8,128)S(1)}, f32[1,640,256]{2,1,0:T(8,128)S(1)}, u32[]{:S(2)}, u32[]{:S(2)}) collective-permute-start(f32[1,640,256]{2,1,0:T(8,128)S(1)} %slice.30), channel_id=1, source_target_pairs={{0,64},{64,0},{128,192},{192,128},{256,320},{320,256},{384,448},{4... | collective-permute-start | bytes 1966088 | tf_op jit(solution)/shard_map/ppermute | solution.py:257
  97.1 2.1 %collective-permute-done.5.refs_9_.refs_7_ = f32[1,640,256]{2,1,0:T(8,128)S(1)} collective-permute-done((f32[1,640,256]{2,1,0:T(8,128)S(1)}, f32[1,640,256]{2,1,0:T(8,128)S(1)}, u32[]{:S(2)}, u32[]{:S(2)}) %collective-permute-start.5) | collective-permute-done | bytes 655392 | tf_op jit(solution)/shard_map/ppermute | solution.py:257
  99.2 0.8 copy-done.7
  100.0 7.3 %all-to-all-done.2.refs_4_ = f32[16,64,128]{2,1,0:T(8,128)} async-done(((f32[16,64,128]{2,1,0:T(8,128)}), f32[16,64,128]{2,1,0:T(8,128)}, u32[]{:S(2)}, u32[]{:S(2)}) %all-to-all-start.2) | async-done | bytes 524320 | tf_op jit(solution)/shard_map/all_to_all | solution.py:260
  107.3 1.0 copy-done.3
  108.3 1.1 copy-done.8
  109.4 2.1 %exchange.8 = f32[16,104,128]{2,1,0:T(8,128)S(1)} custom-call(s32[2]{0:T(128)S(1)} %pad_add_fusion.ids_ref.refs_0_, s32[16]{0:T(128)S(1)} %reshape.25.refs_1_, f32[8]{0:T(128)S(1)} %copy-done.16, s32[8]{0:T(128)S(1)} %bitcast.32, f32[16,64,128]{2,1,0:T(8,128)} %all-to-all-done.2.refs_4_, f32[768,128]{1,0:T(8,128)S(1)} %copy-done.3, f32[6,128]{1,0:T(8,128)S(1)} %bitcast.27, ...), custom_call_target="tpu_custom_call" | custom-call | flops 335544320 | bytes 1703936 | tf_op jit(solution)/shard_map/exchange/pallas_call | solution.py:157
  111.5 28.8 %all_to_all.26.refs_7_ = f32[16,104,128]{2,1,0:T(8,128)S(1)} all-to-all(f32[16,104,128]{2,1,0:T(8,128)S(1)} %exchange.8), channel_id=1, replica_groups=mesh['occ'=8,'aux'=16,'vir'=4] {'aux'}, dimensions={0} | all-to-all | bytes 1703936 | tf_op jit(solution)/shard_map/all_to_all | solution.py:260
  140.4 0.6 exchange.9
  141.0 0.7 copy-done.14
  141.7 4.6 %all-to-all-start.4 = ((f32[16,40,128]{2,1,0:T(8,128)}), f32[16,40,128]{2,1,0:T(8,128)}, u32[]{:S(2)}, u32[]{:S(2)}) async-start(f32[16,40,128]{2,1,0:T(8,128)} %copy-done.14), calls=%async_computation.4 | async-start | bytes 655360 | tf_op jit(solution)/shard_map/all_to_all | solution.py:260
  146.5 0.1 stack.51
  146.5 3.5 %gamma.2 = (f32[632,768]{1,0:T(8,128)S(1)}, f32[16,128]{1,0:T(8,128)S(1)}) custom-call(s32[2]{0:T(128)S(1)} %pad_add_fusion.ids_ref.refs_0_, s32[16]{0:T(128)S(1)} %reshape.25.refs_1_, f32[8]{0:T(128)S(1)} %copy-done.16, s32[8]{0:T(128)S(1)} %bitcast.34, f32[16,40,128]{2,1,0:T(8,128)S(1)} %copy-done.13, f32[1,640,256]{2,1,0:T(8,128)S(1)} %copy-done.6, ...), custom_call_target="tpu_custom_call" | custom-call | flops 994050048 | bytes 3883008 | tf_op jit(solution)/shard_map/gamma/pallas_call | solution.py:221
  150.0 1.3 copy-done.11
  151.3 0.1 slice_reduce_fusion.2
  151.4 0.1 reduce_sum.45
  151.5 0.1 slice_reduce_fusion
  151.6 0.1 reduce_sum.51
  151.7 0.1 reduce_sum.46
  151.8 0.1 reduce_sum.62
  151.9 6.3 %all-to-all-done.4.refs_5_ = f32[16,40,128]{2,1,0:T(8,128)} async-done(((f32[16,40,128]{2,1,0:T(8,128)}), f32[16,40,128]{2,1,0:T(8,128)}, u32[]{:S(2)}, u32[]{:S(2)}) %all-to-all-start.4) | async-done | bytes 327712 | tf_op jit(solution)/shard_map/all_to_all | solution.py:260
  158.2 1.1 copy-done.9
  159.3 1.5 copy-done.12
  160.8 3.4 %gamma.3 = (f32[632,768]{1,0:T(8,128)}, f32[8,128]{1,0:T(8,128)S(1)}) custom-call(s32[2]{0:T(128)S(1)} %pad_add_fusion.ids_ref.refs_0_, s32[16]{0:T(128)S(1)} %reshape.25.refs_1_, f32[8]{0:T(128)S(1)} %copy-done.16, s32[8]{0:T(128)S(1)} %bitcast.35, f32[632,768]{1,0:T(8,128)S(1)} %copy-done.12, f32[16,40,128]{2,1,0:T(8,128)} %all-to-all-done.4.refs_5_, ...), custom_call_target="tpu_custom_call" | custom-call | flops 331350016 | bytes 3883008 | tf_op jit(solution)/shard_map/gamma/pallas_call | solution.py:221
  164.2 0.1 slice_reduce_fusion.1
  164.3 0.1 reduce_sum.64
  164.4 0.1 reduce_sum.65
  164.6 0.1 select_reduce_fusion
  164.7 12.5 %psum.7 = f32[1,8]{1,0:T(1,128)} all-reduce(f32[1,8]{1,0:T(1,128)S(1)} %bitcast.37), channel_id=1, replica_groups=mesh['occ'=8,'aux'=16,'vir'=4] {'vir'}, use_global_device_ids=true, to_apply=%region_7.8 | all-reduce | flops 8 | bytes 64 | tf_op jit(solution)/shard_map/psum | solution.py:295
  (35 shorter events, 0.3 us)
Async XLA Ops:
  13.7 1.5 copy-start
  17.4 11.4 %copy-start.21 = (s32[1,8,1,2]{1,3,2,0:T(2,128)S(1)}, s32[1,8,1,2]{1,3,2,0:T(2,128)}, u32[]{:S(2)}) copy-start(s32[1,8,1,2]{1,3,2,0:T(2,128)} %param.8) | copy-start | bytes 196
  17.4 33.2 %collective-permute-start.1 = (f32[2,640,256]{2,1,0:T(8,128)}, f32[2,640,256]{2,1,0:T(8,128)S(1)}, u32[]{:S(2)}, u32[]{:S(2)}) collective-permute-start(f32[2,640,256]{2,1,0:T(8,128)} %get-tuple-element.21), channel_id=1, source_target_pairs={{0,128},{64,192},{128,256},{192,320},{256,384},{320,448},{384,0},{... | collective-permute-start | bytes 3932168 | tf_op jit(solution)/shard_map/ppermute | solution.py:263
  20.8 34.1 %collective-permute-start.2 = (f32[2,640,256]{2,1,0:T(8,128)}, f32[2,640,256]{2,1,0:T(8,128)}, u32[]{:S(2)}, u32[]{:S(2)}) collective-permute-start(f32[2,640,256]{2,1,0:T(8,128)} %get-tuple-element.22), channel_id=1, source_target_pairs={{0,384},{64,448},{128,0},{192,64},{256,128},{320,192},{384,256},{4... | collective-permute-start | bytes 3932168 | tf_op jit(solution)/shard_map/ppermute | solution.py:264
  25.0 0.9 copy-start.4
  25.9 1.1 copy-start.20
  26.9 4.3 %collective-permute-start = (f32[1,640,256]{2,1,0:T(8,128)}, f32[1,640,256]{2,1,0:T(8,128)}, u32[]{:S(2)}, u32[]{:S(2)}) collective-permute-start(f32[1,640,256]{2,1,0:T(8,128)} %get-tuple-element.17), channel_id=1, source_target_pairs={{0,64},{64,0},{128,192},{192,128},{256,320},{320,256},{384,448},{4... | collective-permute-start | bytes 1966088 | tf_op jit(solution)/shard_map/ppermute | solution.py:257
  28.9 1.5 copy-start.1
  30.5 0.8 copy-start.16
  30.5 0.8 copy-start.17
  31.2 1.1 copy-start.5
  34.7 24.4 %all-to-all-start = ((f32[16,32,128]{2,1,0:T(8,128)}), f32[16,32,128]{2,1,0:T(8,128)S(1)}, u32[]{:S(2)}, u32[]{:S(2)}) async-start(f32[16,32,128]{2,1,0:T(8,128)} %exchange.5), calls=%async_computation | async-start | bytes 524288 | tf_op jit(solution)/shard_map/all_to_all | solution.py:260
  56.0 5.4 %copy-start.15 = (f32[768]{0:T(1024)S(1)}, f32[768]{0:T(1024)}, u32[]{:S(2)}) copy-start(f32[768]{0:T(1024)} %param.7) | copy-start | bytes 9220
  57.2 27.1 %collective-permute-start.3 = (f32[2,640,256]{2,1,0:T(8,128)}, f32[2,640,256]{2,1,0:T(8,128)}, u32[]{:S(2)}, u32[]{:S(2)}) collective-permute-start(f32[2,640,256]{2,1,0:T(8,128)} %pad_maximum_fusion), channel_id=1, source_target_pairs={{0,64},{64,0},{128,192},{192,128},{256,320},{320,256},{384,448},{4... | collective-permute-start | bytes 3932168 | tf_op jit(solution)/shard_map/ppermute | solution.py:257
  59.1 34.9 %collective-permute-start.4 = (f32[2,640,256]{2,1,0:T(8,128)}, f32[2,640,256]{2,1,0:T(8,128)}, u32[]{:S(2)}, u32[]{:S(2)}) collective-permute-start(f32[2,640,256]{2,1,0:T(8,128)} %copy-done.20), channel_id=1, source_target_pairs={{0,256},{64,320},{128,384},{192,448},{256,0},{320,64},{384,128},{4... | collective-permute-start | bytes 3932168 | tf_op jit(solution)/shard_map/ppermute | solution.py:272
  61.6 0.7 copy-start.18
  62.9 0.8 copy-start.2
  87.0 0.8 copy-start.10
  87.8 19.4 %copy-start.19 = (s32[1,8]{1,0:T(1,128)S(1)}, s32[1,8]{1,0:T(1,128)}, u32[]{:S(2)}) copy-start(s32[1,8]{1,0:T(1,128)} %param.9) | copy-start | bytes 100
  87.8 19.4 %all-to-all-start.2 = ((f32[16,64,128]{2,1,0:T(8,128)}), f32[16,64,128]{2,1,0:T(8,128)}, u32[]{:S(2)}, u32[]{:S(2)}) async-start(f32[16,64,128]{2,1,0:T(8,128)} %copy-done.10), calls=%async_computation.2 | async-start | bytes 1048576 | tf_op jit(solution)/shard_map/all_to_all | solution.py:260
  95.2 4.0 %collective-permute-start.5 = (f32[1,640,256]{2,1,0:T(8,128)S(1)}, f32[1,640,256]{2,1,0:T(8,128)S(1)}, u32[]{:S(2)}, u32[]{:S(2)}) collective-permute-start(f32[1,640,256]{2,1,0:T(8,128)S(1)} %slice.30), channel_id=1, source_target_pairs={{0,64},{64,0},{128,192},{192,128},{256,320},{320,256},{384,448},{4... | collective-permute-start | bytes 1966088 | tf_op jit(solution)/shard_map/ppermute | solution.py:257
  99.2 0.8 copy-start.7
  107.3 1.0 copy-start.3
  108.3 1.1 copy-start.8
  140.3 6.2 %copy-start.6 = (f32[1,640,256]{2,1,0:T(8,128)S(1)}, f32[1,640,256]{2,1,0:T(8,128)}, u32[]{:S(2)}) copy-start(f32[1,640,256]{2,1,0:T(8,128)} %copy-done.4) | copy-start | bytes 1966084
  140.3 6.2 %copy-start.13 = (f32[16,40,128]{2,1,0:T(8,128)S(1)}, f32[16,40,128]{2,1,0:T(8,128)}, u32[]{:S(2)}) copy-start(f32[16,40,128]{2,1,0:T(8,128)} %all_to_all.25.refs_4_) | copy-start | bytes 983044
  141.0 0.7 copy-start.14
  141.7 16.5 %all-to-all-start.4 = ((f32[16,40,128]{2,1,0:T(8,128)}), f32[16,40,128]{2,1,0:T(8,128)}, u32[]{:S(2)}, u32[]{:S(2)}) async-start(f32[16,40,128]{2,1,0:T(8,128)} %copy-done.14), calls=%async_computation.4 | async-start | bytes 655360 | tf_op jit(solution)/shard_map/all_to_all | solution.py:260
  150.0 1.3 copy-start.11
  158.2 1.1 copy-start.9
  159.3 1.5 copy-start.12

commit v4 on v3

--- a/solution.py
+++ b/solution.py
@@ -11,6 +11,7 @@
 CHIPS = 4
 VMEM = pl.BlockSpec(memory_space=pltpu.VMEM)
 SMEM = pl.BlockSpec(memory_space=pltpu.SMEM)
+HBM = pl.BlockSpec(memory_space=pltpu.HBM)
 def params():
     return pltpu.CompilerParams(vmem_limit_bytes=12 * 1024 * 1024)
 
@@ -34,27 +35,63 @@
     return lax.rem(me // 2 + CHIPS - dx, CHIPS) * 2 + lax.rem(me + dc, 2)
 
 
-def pick_kernel(shifts, ids_ref, pairs_ref, block_ref, *out_refs):
+def pick_kernel(shifts, ids_ref, pairs_ref, block_ref, *refs):
+    *out_refs, zeros_ref, sems = refs
     rows, cols = block_ref.shape
     slots = [(out_ref, k) for out_ref in out_refs for k in range(out_ref.shape[0])]
+    zeros_ref[...] = jnp.zeros_like(zeros_ref)
+    copies = []
     for (out_ref, k), (dx, dc) in zip(slots, shifts):
         receiver = partner_of(ids_ref, CHIPS - dx, dc)
         for s in range(2):
             tile = lax.rem(pairs_ref[(receiver * 2 * CHIPS + ids_ref[0]) * 2 + s], cols // TILE)
-            out_ref[k, :rows, s * TILE : (s + 1) * TILE] = block_ref[:, lanes(tile)]
-        out_ref[k, rows:, :] = jnp.zeros((out_ref.shape[1] - rows, 2 * TILE), jnp.float32)
+            source = block_ref.at[:, lanes(tile)]
+            target = out_ref.at[k, pl.ds(0, rows), pl.ds(s * TILE, TILE)]
+            copies.append(pltpu.make_async_copy(source, target, sems.at[len(copies)]))
+        target = out_ref.at[k, pl.ds(rows, zeros_ref.shape[0]), :]
+        copies.append(pltpu.make_async_copy(zeros_ref, target, sems.at[len(copies)]))
+    for copy in copies:
+        copy.start()
+    for copy in copies:
+        copy.wait()
 
 
 def pick(ids, pairs, block, shifts, counts, padded):
     return pl.pallas_call(
         functools.partial(pick_kernel, shifts),
         out_shape=[jax.ShapeDtypeStruct((count, padded, 2 * TILE), jnp.float32) for count in counts],
-        in_specs=[SMEM, SMEM, VMEM],
-        out_specs=[VMEM] * len(counts),
+        in_specs=[SMEM, SMEM, HBM],
+        out_specs=[HBM] * len(counts),
+        scratch_shapes=[
+            pltpu.VMEM((padded - block.shape[0], 2 * TILE), jnp.float32),
+            pltpu.SemaphoreType.DMA((3 * len(shifts),)),
+        ],
         compiler_params=params(),
         cost_estimate=cost(0, sum(counts) * padded * 4 * TILE * 4),
         name="pick",
     )(ids, pairs, block)
+
+
+def halves_kernel(*refs):
+    *in_refs, out_ref, sems = refs
+    copies = [pltpu.make_async_copy(ref.at[1], out_ref.at[k], sems.at[k]) for k, ref in enumerate(in_refs)]
+    for copy in copies:
+        copy.start()
+    for copy in copies:
+        copy.wait()
+
+
+def halves(*arrays):
+    return pl.pallas_call(
+        halves_kernel,
+        out_shape=jax.ShapeDtypeStruct((len(arrays), *arrays[0].shape[1:]), jnp.float32),
+        in_specs=[HBM] * len(arrays),
+        out_specs=HBM,
+        scratch_shapes=[pltpu.SemaphoreType.DMA((len(arrays),))],
+        compiler_params=params(),
+        cost_estimate=cost(0, sum(array.size for array in arrays) * 4),
+        name="halves",
+    )(*arrays)
 
 
 def left_kernel(block_ref, out_ref):
@@ -88,43 +125,34 @@
     return partner, lax.div(entry, tile_count), lax.rem(entry, tile_count)
 
 
-def add_amplitude(scalars, shifts, parts_ref, columns_ref, levels_ref, out_ref):
-    ids_ref, _, occ_ref, live_ref = scalars
-    count = 2 * len(shifts)
-    energies = []
+def denominator_of(scalars, columns_ref, levels_ref, partner, first, second, start, count):
+    ids_ref, _, occ_ref, _ = scalars
+    row = pl.multiple_of(first * TILE + start, 8)
+    occ = occ_ref[ids_ref[0]] + occ_ref[partner]
+    return occ - columns_ref[pl.ds(row, count), :] - levels_ref[pl.ds(second, 1), :]
+
+
+def add_amplitude(scalars, shifts, parts_at, parts_ref, columns_ref, levels_ref, out_ref):
+    ids_ref, _, _, live_ref = scalars
     for k, shift in enumerate(shifts):
         for s in range(2):
             t = 2 * k + s
             partner, first, second = tiles_of(scalars, shift, s, levels_ref.shape[0])
-            row = pl.multiple_of(first * TILE + 8 * ids_ref[1], 8)
-            denominator = (
-                occ_ref[ids_ref[0]] + occ_ref[partner] - columns_ref[pl.ds(row, 8), :] - levels_ref[pl.ds(second, 1), :]
-            )
-            summed = jnp.sum(parts_ref[:, 8 * t : 8 * t + 8, :], axis=0)
-            denominator = jnp.where(s < live_ref[partner], denominator, jnp.inf)
-            amplitude = summed / denominator
-            energies.append(jnp.sum(summed * amplitude, axis=0, keepdims=True))
+            denominator = denominator_of(scalars, columns_ref, levels_ref, partner, first, second, 8 * ids_ref[1], 8)
+            summed = jnp.sum(parts_ref[:, parts_at + 8 * t : parts_at + 8 * t + 8, :], axis=0)
+            amplitude = summed / jnp.where(s < live_ref[partner], denominator, jnp.inf)
             for owner in range(out_ref.shape[0]):
                 out_ref[owner, 8 * t : 8 * t + 8, :] = amplitude
-    energies.append(jnp.zeros((-count % 8, TILE), jnp.float32)) if count % 8 else None
-    energy = jnp.concatenate(energies, axis=0)
-    done = 8 * count + energy.shape[0]
-    for owner in range(out_ref.shape[0]):
-        out_ref[owner, 8 * count : done, :] = energy
-    return done
-
-
-def returned_rows(tiles):
-    return 8 * tiles + -(-tiles // 8) * 8
-
-
-def exchange_kernel(back_shifts, shifts, entries, *refs):
+    return 16 * len(shifts)
+
+
+def exchange_kernel(back_shifts, parts_at, shifts, entries, *refs):
     *in_refs, out_ref = refs
     scalars, in_refs = in_refs[:4], in_refs[4:]
     at = 0
     if back_shifts:
         parts_ref, columns_ref, levels_ref, *in_refs = in_refs
-        at = add_amplitude(scalars, back_shifts, parts_ref, columns_ref, levels_ref, out_ref)
+        at = add_amplitude(scalars, back_shifts, parts_at, parts_ref, columns_ref, levels_ref, out_ref)
     if entries:
         left_ref, *right_refs = in_refs
         for k, ((which, entry), shift) in enumerate(zip(entries, shifts)):
@@ -140,13 +168,13 @@
 
 
 def exchange(scalars, returned, group):
-    inputs, specs, rows, flops = list(scalars), [SMEM] * 4, 0, 0
+    inputs, specs, rows, flops, parts_at = list(scalars), [SMEM] * 4, 0, 0, 0
     back_shifts, shifts, entries = (), (), ()
     if returned is not None:
-        back_shifts, parts, columns, levels = returned
+        back_shifts, parts, parts_at, columns, levels = returned
         inputs += [parts, columns, levels]
         specs += [VMEM] * 3
-        rows += returned_rows(2 * len(back_shifts))
+        rows += 16 * len(back_shifts)
     if group is not None:
         shifts, left_split, rights = group
         arrays, entries = unique(rights)
@@ -155,7 +183,7 @@
         rows += 16 * len(entries)
         flops = len(entries) * 16 * TILE * TILE * left_split.shape[2]
     return pl.pallas_call(
-        functools.partial(exchange_kernel, back_shifts, shifts, entries),
+        functools.partial(exchange_kernel, back_shifts, parts_at, shifts, entries),
         out_shape=jax.ShapeDtypeStruct((TILE // 8, rows, TILE), jnp.float32),
         in_specs=specs,
         out_specs=VMEM,
@@ -175,22 +203,51 @@
     return arrays, entries
 
 
+def tile_amplitude(amplitude_ref, t):
+    return amplitude_ref[:, 8 * t : 8 * t + 8, :].reshape(TILE, TILE)
+
+
+def energy_kernel(groups, *refs):
+    scalars, (columns_ref, levels_ref, *amplitude_refs, out_ref) = refs[:4], refs[4:]
+    rows = []
+    for shifts, amplitude_ref in zip(groups, amplitude_refs):
+        for k, shift in enumerate(shifts):
+            for s in range(2):
+                amplitude = tile_amplitude(amplitude_ref, 2 * k + s)
+                place = tiles_of(scalars, shift, s, levels_ref.shape[0])
+                denominator = denominator_of(scalars, columns_ref, levels_ref, *place, 0, TILE)
+                rows.append(jnp.sum(amplitude * amplitude * denominator, axis=0, keepdims=True))
+    for k in range(len(rows) // 2):
+        out_ref[k : k + 1, :] = rows[2 * k] + rows[2 * k + 1]
+
+
+def energy_of(scalars, columns, levels, groups):
+    shifts = [group[0] for group in groups]
+    partners = sum(len(group) for group in shifts)
+    return pl.pallas_call(
+        functools.partial(energy_kernel, shifts),
+        out_shape=jax.ShapeDtypeStruct((partners, TILE), jnp.float32),
+        in_specs=[SMEM] * 4 + [VMEM] * (2 + len(groups)),
+        out_specs=VMEM,
+        compiler_params=params(),
+        cost_estimate=cost(6 * partners * TILE * TILE, partners * TILE * TILE * 8),
+        name="energy",
+    )(*scalars, columns, levels, *[group[1] for group in groups])
+
+
 def gamma_kernel(groups, carried, *refs):
     scalars, refs = refs[:4], refs[4:]
     if carried:
         gamma_in, *refs = refs
-    *in_refs, gamma_ref, energy_ref = refs
+    *in_refs, gamma_ref = refs
     rows, cols = gamma_ref.shape
     gamma_ref[...] = gamma_in[...] if carried else jnp.zeros_like(gamma_ref)
-    energy_at = 0
     for shifts, entries, arrays in groups:
         (amplitude_ref, *right_refs), in_refs = in_refs[: 1 + arrays], in_refs[1 + arrays :]
-        count = 2 * len(entries)
         for k, ((which, entry), shift) in enumerate(zip(entries, shifts)):
             for s in range(2):
-                t = 2 * k + s
                 _, first, _ = tiles_of(scalars, shift, s, cols // TILE)
-                high, low = split(amplitude_ref[:, 8 * t : 8 * t + 8, :].reshape(TILE, TILE))
+                high, low = split(tile_amplitude(amplitude_ref, 2 * k + s))
                 weights = jnp.concatenate(
                     [
                         jnp.concatenate([high, high], axis=1),
@@ -202,30 +259,21 @@
                 part = lax.dot_general(both, weights, (((1,), (1,)), ((), ())), preferred_element_type=jnp.float32)
                 place = lanes(first)
                 gamma_ref[:, place] += (part[:, :TILE] + part[:, TILE:])[:rows]
-        extra = returned_rows(count) - 8 * count
-        energy = jnp.sum(amplitude_ref[:, 8 * count : 8 * count + extra, :], axis=0)
-        energy_ref[energy_at : energy_at + extra, :] = energy
-        energy_at += extra
 
 
 def gamma_add(scalars, groups, rows, cols, carried):
-    inputs, extra, tiles = [], 0, 0
-    described = []
+    inputs, tiles, described = [], 0, []
     for shifts, amplitudes, rights in groups:
         arrays, entries = unique(rights)
         described.append((shifts, entries, len(arrays)))
         inputs += [amplitudes, *arrays]
-        extra += returned_rows(2 * len(shifts)) - 16 * len(shifts)
         tiles += 2 * len(shifts)
     start = list(scalars) + ([carried] if carried is not None else [])
     return pl.pallas_call(
         functools.partial(gamma_kernel, described, carried is not None),
-        out_shape=[
-            jax.ShapeDtypeStruct((rows, cols), jnp.float32),
-            jax.ShapeDtypeStruct((extra, TILE), jnp.float32),
-        ],
+        out_shape=jax.ShapeDtypeStruct((rows, cols), jnp.float32),
         in_specs=[SMEM] * 4 + [VMEM] * (len(start) - 4 + len(inputs)),
-        out_specs=[VMEM, VMEM],
+        out_specs=VMEM,
         compiler_params=params(),
         cost_estimate=cost(tiles * 8 * TILE * TILE * rows, rows * cols * 8),
         name="gamma",
@@ -268,32 +316,30 @@
 
     early_rights = [(own, 0), (mate, 0)]
     early_parts = sent(None, (EARLY, left_split, early_rights))
-    far, early_parts = lax.optimization_barrier((far, early_parts))
+    far, ahead, behind, early_parts = lax.optimization_barrier((far, ahead, behind, early_parts))
     far = lax.ppermute(far, "occ", route(2, 0))
-    early = sent((EARLY, early_parts, columns, levels), None)
-
-    near_mate = swapped(jnp.stack([ahead[1], behind[1]]))
+    near_mate = swapped(halves(ahead, behind))
     near_rights = [(ahead, 0), (behind, 0), (near_mate, 0), (near_mate, 1)]
-    near_left, early = lax.optimization_barrier((left_split, early))
-    near_parts = sent(None, (NEAR, near_left, near_rights))
-
-    far_mate = swapped(far[1:])
+    near = sent((EARLY, early_parts, 0, columns, levels), (NEAR, left_split, near_rights))
+
+    far_mate = swapped(halves(far))
     far_rights = [(far, 0), (far_mate, 0)]
-    both = sent((NEAR, near_parts, columns, levels), (FAR, left_split, far_rights))
-    near_rows = returned_rows(2 * len(NEAR))
-    last = sent((FAR, both[:, near_rows:], columns, levels), None)
-    total, energy = gamma_add(scalars, [(EARLY, early, early_rights), (NEAR, both, near_rights)], rows, cols, None)
-    total, last_energy = gamma_add(scalars, [(FAR, last, far_rights)], rows, cols, total)
-
-    energies = []
-    for value, shifts, at in ((energy, EARLY, 0), (energy, NEAR, 8), (last_energy, FAR, 0)):
-        pairs = value[at : at + 2 * len(shifts)].reshape(len(shifts), 2 * TILE)
-        energies.append(jnp.sum(pairs, axis=1))
+    both = sent((NEAR, near, 16 * len(EARLY), columns, levels), (FAR, left_split, far_rights))
+    last = sent((FAR, both, 16 * len(NEAR), columns, levels), None)
+    first_groups = [(EARLY, near, early_rights), (NEAR, both, near_rights)]
+    total = gamma_add(scalars, first_groups, rows, cols, None)
+    first_energy = energy_of(scalars, columns, levels, first_groups)
+    last_energy = energy_of(scalars, columns, levels, [(FAR, last)])
+
+    energy = jnp.sum(jnp.concatenate([first_energy, last_energy], axis=0), axis=1)
+    for bit in (1, 2):
+        blocks = range(lax.axis_size("vir"))
+        energy = energy + lax.ppermute(energy, "vir", [(v, v ^ bit) for v in blocks])
     order = jnp.stack([(me // 2 - dx) % CHIPS * 2 + (me + dc) % 2 for dx, dc in EARLY + NEAR + FAR])
     mine = order[:, None] == jnp.arange(occ_size)[None, :]
-    energy = jnp.sum(jnp.where(mine, jnp.concatenate(energies)[:, None], 0.0), axis=0)
-    energy = lax.psum(energy[None], "vir")
-    return total[None], energy
+    energy = jnp.sum(jnp.where(mine, energy[:, None], 0.0), axis=0)
+    total = gamma_add(scalars, [(FAR, last, far_rights)], rows, cols, total)
+    return total[None], energy[None]
 
 
 def solution(mesh):

time: 180 us -> 171 us (0.950); the launches traced: 177 us -> 170 us
  blocking collectives: 74.6 us -> 62.9 us
  starting transfers between devices: 31.1 us -> 36.1 us
  Pallas kernels: 19.7 us -> 22.2 us
    ppermute x1, waiting for transfers between devices: 1.72 us -> 17.3 us  [per_device(): far = lax.ppermute(far, 'occ', route(2, 0))]
    psum x1 -> x0, blocking collectives: 12.5 us -> none  [per_device(): energy = lax.psum(energy[None], 'vir')]
    all_to_all x3 -> x2, waiting for transfers between devices: 13.6 us -> 2.73 us  [sent(): return lax.all_to_all(exchange(scalars, returned, group), 'aux', 0, 0)]
    ppermute x0 -> x2, starting transfers between devices: none -> 9.52 us  [per_device(): lax.ppermute(energy, 'vir', [(v, v ^ bit) for v in blocks])]
    ppermute x1, waiting for transfers between devices: 7.9 us -> 0.01 us  [per_device(): ahead = lax.ppermute(ahead, 'occ', route(1, 0))]
    all_to_all x3 -> x2, starting transfers between devices: 17.1 us -> 12.6 us  [sent(): return lax.all_to_all(exchange(scalars, returned, group), 'aux', 0, 0)]
    ppermute x0 -> x2, waiting for transfers between devices: none -> 4.3 us  [per_device(): lax.ppermute(energy, 'vir', [(v, v ^ bit) for v in blocks])]
    pallas_call x5 -> x8, Pallas kernels: 8.49 us -> 11.1 us  [the longest x4 7.38 us: exchange(): pl.pallas_call(functools.partial(exchange_kernel, back_shifts, parts_at,...]
  transfers between devices with their start and end apart: 9 -> 10, of which waited for: 7 -> 7; matrix products, arithmetic and copies ran while one was open for 3% -> 0% of each run, Pallas kernels for 6% -> 9%
where the time goes in v4:
time: 171 us; the launch traced here: 170 us
  blocking collectives  62.9 us (37%)
  starting transfers between devices  36.1 us (21%)
  waiting for transfers between devices  29.7 us (17%)
  Pallas kernels  22.2 us (13%)
  local copies, waits for them, and re-layouts  17.4 us (10%)
    all_to_all x2, blocking collectives, sent(): return lax.all_to_all(exchange(scalars, returned, group), 'aux', 0, 0)  50.2 us
    ppermute x1, waiting for transfers between devices, per_device(): far = lax.ppermute(far, 'occ', route(2, 0))  17.3 us
    unnamed x41, local copies, waits for them, and re-layouts  16.9 us
    all_gather x1, blocking collectives, per_device(): all_pairs = lax.all_gather(tile_pairs[0, :, 0, :], 'occ').reshape(-1)  12.7 us
    all_to_all x2, starting transfers between devices, sent(): return lax.all_to_all(exchange(scalars, returned, group), 'aux', 0, 0)  12.6 us
    ppermute x2, starting transfers between devices, per_device(): lax.ppermute(energy, 'vir', [(v, v ^ bit) for v in blocks])  9.52 us
    pallas_call x4, Pallas kernels, exchange(): pl.pallas_call(functools.partial(exchange_kernel, back_shifts, parts_at,...  7.38 us
    pallas_call x2, Pallas kernels, gamma_add(): pl.pallas_call(functools.partial(gamma_kernel, described, carried is not...  6.34 us
  transfers between devices with their start and end apart: 10, of which 7 were waited for; matrix products, arithmetic and copies ran while one was open for 0% of the time, Pallas kernels for 9%

profile of v4, /device:TPU:6, one launch (start us, length us, event | category | flops | bytes accessed | tf_op | source)
XLA Modules:
  0.0 170.1 jit_solution(9043371730536792856)
XLA Ops:
  0.6 12.7 %all-gather = s32[8,8,1,2]{1,3,2,0:T(2,128)S(1)} all-gather(s32[1,8,1,2]{1,3,2,0:T(2,128)} %param.8), channel_id=2, replica_groups=mesh['occ'=8,'aux'=16,'vir'=4] {'occ'}, dimensions={0}, use_global_device_ids=true | all-gather | bytes 576 | tf_op jit(solution)/shard_map/all_gather | solution.py:295
  13.3 0.1 copy.14
  13.4 0.1 reshape.21.pairs_ref
  13.6 0.1 pad_add_fusion.ids_ref.refs_0_
  13.7 1.5 copy-done
  15.2 2.1 %pick.3 = (f32[2,640,256]{2,1,0:T(8,128)}, f32[2,640,256]{2,1,0:T(8,128)}) custom-call(s32[2]{0:T(128)S(1)} %pad_add_fusion.ids_ref.refs_0_, s32[128]{0:T(128)S(1)} %reshape.21.pairs_ref, f32[632,768]{1,0:T(8,128)S(1)} %bitcast.23), custom_call_target="tpu_custom_call" | custom-call | bytes 5242880 | tf_op jit(solution)/shard_map/pick/pallas_call | solution.py:60
  17.3 0.0 copy-start.19
  17.4 3.2 %collective-permute-start = (f32[2,640,256]{2,1,0:T(8,128)}, f32[2,640,256]{2,1,0:T(8,128)S(1)}, u32[]{:S(2)}, u32[]{:S(2)}) collective-permute-start(f32[2,640,256]{2,1,0:T(8,128)} %get-tuple-element.12), channel_id=1, source_target_pairs={{0,128},{64,192},{128,256},{192,320},{256,384},{320,448},{384,0},{... | collective-permute-start | bytes 3932168 | tf_op jit(solution)/shard_map/ppermute | solution.py:311
  20.6 2.6 %collective-permute-start.1 = (f32[2,640,256]{2,1,0:T(8,128)}, f32[2,640,256]{2,1,0:T(8,128)}, u32[]{:S(2)}, u32[]{:S(2)}) collective-permute-start(f32[2,640,256]{2,1,0:T(8,128)} %get-tuple-element.13), channel_id=1, source_target_pairs={{0,384},{64,448},{128,0},{192,64},{256,128},{320,192},{384,256},{4... | collective-permute-start | bytes 3932168 | tf_op jit(solution)/shard_map/ppermute | solution.py:312
  23.2 2.0 %pick.2 = (f32[1,640,256]{2,1,0:T(8,128)S(1)}, f32[1,640,256]{2,1,0:T(8,128)}, f32[2,640,256]{2,1,0:T(8,128)}) custom-call(s32[2]{0:T(128)S(1)} %pad_add_fusion.ids_ref.refs_0_, s32[128]{0:T(128)S(1)} %reshape.21.pairs_ref, f32[632,768]{1,0:T(8,128)S(1)} %bitcast.24), custom_call_target="tpu_custom_call" | custom-call | bytes 5242880 | tf_op jit(solution)/shard_map/pick/pallas_call | solution.py:60
  25.2 0.0 copy-start.10
  25.2 0.8 copy-done.10
  26.1 1.9 %collective-permute-start.2 = (f32[1,640,256]{2,1,0:T(8,128)}, f32[1,640,256]{2,1,0:T(8,128)}, u32[]{:S(2)}, u32[]{:S(2)}) collective-permute-start(f32[1,640,256]{2,1,0:T(8,128)} %get-tuple-element.15), channel_id=1, source_target_pairs={{0,64},{64,0},{128,192},{192,128},{256,320},{320,256},{384,448},{4... | collective-permute-start | bytes 1966088 | tf_op jit(solution)/shard_map/ppermute | solution.py:305
  28.0 0.0 copy-done.19
  28.0 0.1 copy.13
  28.1 1.5 copy-done.1
  29.6 0.6 left.1.refs_4_.refs_7_
  30.2 0.1 reshape.19.refs_1_
  30.3 0.1 collective-permute-done.2.refs_6_
  30.4 1.1 copy-done.11
  31.5 1.7 exchange.4
  33.2 19.0 %all_to_all.20.refs_4_ = f32[16,32,128]{2,1,0:T(8,128)S(1)} all-to-all(f32[16,32,128]{2,1,0:T(8,128)S(1)} %exchange.4), channel_id=1, replica_groups=mesh['occ'=8,'aux'=16,'vir'=4] {'aux'}, dimensions={0} | all-to-all | bytes 524288 | tf_op jit(solution)/shard_map/all_to_all | solution.py:308
  52.2 0.0 collective-permute-done.refs_0_.refs_8_
  52.2 2.5 %collective-permute-done.1.refs_1_.refs_9_ = f32[2,640,256]{2,1,0:T(8,128)} collective-permute-done((f32[2,640,256]{2,1,0:T(8,128)}, f32[2,640,256]{2,1,0:T(8,128)}, u32[]{:S(2)}, u32[]{:S(2)}) %collective-permute-start.1) | collective-permute-done | bytes 1310752 | tf_op jit(solution)/shard_map/ppermute | solution.py:312
  54.7 1.3 halves.2
  56.0 1.9 %collective-permute-start.3 = (f32[2,640,256]{2,1,0:T(8,128)S(1)}, f32[2,640,256]{2,1,0:T(8,128)S(1)}, u32[]{:S(2)}, u32[]{:S(2)}) collective-permute-start(f32[2,640,256]{2,1,0:T(8,128)S(1)} %halves.2), channel_id=1, source_target_pairs={{0,64},{64,0},{128,192},{192,128},{256,320},{320,256},{384,448},{4... | collective-permute-start | bytes 3932168 | tf_op jit(solution)/shard_map/ppermute | solution.py:305
  58.0 2.3 %collective-permute-start.4 = (f32[2,640,256]{2,1,0:T(8,128)}, f32[2,640,256]{2,1,0:T(8,128)}, u32[]{:S(2)}, u32[]{:S(2)}) collective-permute-start(f32[2,640,256]{2,1,0:T(8,128)} %get-tuple-element.19), channel_id=1, source_target_pairs={{0,256},{64,320},{128,384},{192,448},{256,0},{320,64},{384,128},{4... | collective-permute-start | bytes 3932168 | tf_op jit(solution)/shard_map/ppermute | solution.py:320
  60.3 0.7 collective-permute-done.3.refs_10_
  61.0 0.2 broadcast_in_dim.27.refs_5_.refs_4_
  61.1 1.3 copy-done.3
  62.5 2.3 %exchange.5 = f32[16,96,128]{2,1,0:T(8,128)S(1)} custom-call(s32[2]{0:T(128)S(1)} %pad_add_fusion.ids_ref.refs_0_, s32[16]{0:T(128)S(1)} %reshape.19.refs_1_, f32[8]{0:T(128)S(1)} %copy-done.17, s32[8]{0:T(128)S(1)} %bitcast.32, f32[16,32,128]{2,1,0:T(8,128)S(1)} %all_to_all.20.refs_4_, f32[768,128]{1,0:T(8,128)S(1)} %broadcast_in_dim.27.refs_5_.refs_4_, ...), custom_call_target="tpu_custom_call" | custom-call | flops 671088640 | bytes 1572864 | tf_op jit(solution)/shard_map/exchange/pallas_call | solution.py:185
  64.8 1.1 copy-done.7
  65.9 0.9 copy-done.9
  66.8 8.7 %all-to-all-start.1 = ((f32[16,96,128]{2,1,0:T(8,128)}), f32[16,96,128]{2,1,0:T(8,128)S(1)}, u32[]{:S(2)}, u32[]{:S(2)}) async-start(f32[16,96,128]{2,1,0:T(8,128)} %copy-done.9), calls=%async_computation.1 | async-start | bytes 1572864 | tf_op jit(solution)/shard_map/all_to_all | solution.py:308
  75.5 17.3 %collective-permute-done.4.refs_0_.refs_8_.refs_6_ = f32[2,640,256]{2,1,0:T(8,128)} collective-permute-done((f32[2,640,256]{2,1,0:T(8,128)}, f32[2,640,256]{2,1,0:T(8,128)}, u32[]{:S(2)}, u32[]{:S(2)}) %collective-permute-start.4) | collective-permute-done | bytes 1310752 | tf_op jit(solution)/shard_map/ppermute | solution.py:320
  92.9 1.1 halves.3
  94.0 1.9 %collective-permute-start.5 = (f32[1,640,256]{2,1,0:T(8,128)S(1)}, f32[1,640,256]{2,1,0:T(8,128)S(1)}, u32[]{:S(2)}, u32[]{:S(2)}) collective-permute-start(f32[1,640,256]{2,1,0:T(8,128)S(1)} %halves.3), channel_id=1, source_target_pairs={{0,64},{64,0},{128,192},{192,128},{256,320},{320,256},{384,448},{4... | collective-permute-start | bytes 1966088 | tf_op jit(solution)/shard_map/ppermute | solution.py:305
  95.9 2.1 %collective-permute-done.5.refs_9_.refs_7_ = f32[1,640,256]{2,1,0:T(8,128)S(1)} collective-permute-done((f32[1,640,256]{2,1,0:T(8,128)S(1)}, f32[1,640,256]{2,1,0:T(8,128)S(1)}, u32[]{:S(2)}, u32[]{:S(2)}) %collective-permute-start.5) | collective-permute-done | bytes 655392 | tf_op jit(solution)/shard_map/ppermute | solution.py:305
  98.0 0.9 copy-done.13
  98.8 0.0 all-to-all-done.1.refs_4_.refs_6_
  98.8 1.1 copy-done.14
  99.9 2.0 %exchange.6 = f32[16,96,128]{2,1,0:T(8,128)S(1)} custom-call(s32[2]{0:T(128)S(1)} %pad_add_fusion.ids_ref.refs_0_, s32[16]{0:T(128)S(1)} %reshape.19.refs_1_, f32[8]{0:T(128)S(1)} %copy-done.17, s32[8]{0:T(128)S(1)} %bitcast.33, f32[16,96,128]{2,1,0:T(8,128)S(1)} %all-to-all-done.1.refs_4_.refs_6_, f32[768,128]{1,0:T(8,128)S(1)} %broadcast_in_dim.27.refs_5_.refs_4_, ...), custom_call_target="tpu_custom_call" | custom-call | flops 335544320 | bytes 1572864 | tf_op jit(solution)/shard_map/exchange/pallas_call | solution.py:185
  101.9 31.1 %all_to_all.21.refs_7_.refs_4_ = f32[16,96,128]{2,1,0:T(8,128)S(1)} all-to-all(f32[16,96,128]{2,1,0:T(8,128)S(1)} %exchange.6), channel_id=1, replica_groups=mesh['occ'=8,'aux'=16,'vir'=4] {'aux'}, dimensions={0} | all-to-all | bytes 1572864 | tf_op jit(solution)/shard_map/all_to_all | solution.py:308
  133.1 1.4 exchange.7
  134.4 3.9 %all-to-all-start.3 = ((f32[16,32,128]{2,1,0:T(8,128)}), f32[16,32,128]{2,1,0:T(8,128)S(1)}, u32[]{:S(2)}, u32[]{:S(2)}) async-start(f32[16,32,128]{2,1,0:T(8,128)} %exchange.7), calls=%async_computation.3 | async-start | bytes 524288 | tf_op jit(solution)/shard_map/all_to_all | solution.py:308
  138.4 0.1 stack.47
  138.5 0.7 energy.2
  139.3 1.3 copy-done.4
  140.6 1.3 copy-done.8
  141.9 3.1 %gamma.2.refs_4_ = f32[632,768]{1,0:T(8,128)S(1)} custom-call(s32[2]{0:T(128)S(1)} %pad_add_fusion.ids_ref.refs_0_, s32[16]{0:T(128)S(1)} %reshape.19.refs_1_, f32[8]{0:T(128)S(1)} %copy-done.17, s32[8]{0:T(128)S(1)} %bitcast.36, f32[16,96,128]{2,1,0:T(8,128)S(1)} %all-to-all-done.1.refs_4_.refs_6_, f32[1,640,256]{2,1,0:T(8,128)S(1)} %copy-done.12, ...), custom_call_target="tpu_custom_call" | custom-call | flops 994050048 | bytes 3883008 | tf_op jit(solution)/shard_map/gamma/pallas_call | solution.py:272
  145.0 0.0 copy-start.5
  145.0 1.3 copy-done.5
  146.2 2.7 %all-to-all-done.3.refs_5_.refs_6_ = f32[16,32,128]{2,1,0:T(8,128)S(1)} async-done(((f32[16,32,128]{2,1,0:T(8,128)}), f32[16,32,128]{2,1,0:T(8,128)S(1)}, u32[]{:S(2)}, u32[]{:S(2)}) %all-to-all-start.3) | async-done | bytes 262176 | tf_op jit(solution)/shard_map/all_to_all | solution.py:308
  149.0 0.6 energy.3
  149.6 0.1 maximum_reduce_fusion
  149.7 4.5 %collective-permute-start.6 = (f32[8]{0:T(128)S(1)}, f32[8]{0:T(128)S(1)}, u32[]{:S(2)}, u32[]{:S(2)}) collective-permute-start(f32[8]{0:T(128)S(1)} %maximum_reduce_fusion), channel_id=1, source_target_pairs={{0,1},{1,0},{2,3},{3,2},{4,5},{5,4},{6,7},{7,6},{8,9},{9,8},{10,11... | collective-permute-start | bytes 104 | tf_op jit(solution)/shard_map/ppermute | solution.py:337
  154.2 0.0 copy-start.6
  154.2 1.5 copy-done.6
  155.7 1.1 copy-done.15
  156.8 3.3 %gamma.3 = f32[632,768]{1,0:T(8,128)} custom-call(s32[2]{0:T(128)S(1)} %pad_add_fusion.ids_ref.refs_0_, s32[16]{0:T(128)S(1)} %reshape.19.refs_1_, f32[8]{0:T(128)S(1)} %copy-done.17, s32[8]{0:T(128)S(1)} %bitcast.38, f32[632,768]{1,0:T(8,128)S(1)} %copy-done.6, f32[16,32,128]{2,1,0:T(8,128)S(1)} %all-to-all-done.3.refs_5_.refs_6_, ...), custom_call_target="tpu_custom_call" | custom-call | flops 331350016 | bytes 3883008 | tf_op jit(solution)/shard_map/gamma/pallas_call | solution.py:272
  160.1 0.0 collective-permute-done.6
  160.1 5.0 %collective-permute-start.7 = (f32[8]{0:T(128)S(1)}, f32[8]{0:T(128)S(1)}, u32[]{:S(2)}, u32[]{:S(2)}) collective-permute-start(f32[8]{0:T(128)S(1)} %add.84), channel_id=1, source_target_pairs={{0,2},{1,3},{2,0},{3,1},{4,6},{5,7},{6,4},{7,5},{8,10},{9,11},{10,... | collective-permute-start | bytes 104 | tf_op jit(solution)/shard_map/ppermute | solution.py:337
  165.2 4.3 %collective-permute-done.7 = f32[8]{0:T(128)S(1)} collective-permute-done((f32[8]{0:T(128)S(1)}, f32[8]{0:T(128)S(1)}, u32[]{:S(2)}, u32[]{:S(2)}) %collective-permute-start.7) | collective-permute-done | bytes 64 | tf_op jit(solution)/shard_map/ppermute | solution.py:337
  169.5 0.6 select_reduce_fusion
  (23 shorter events, 0.0 us)
Async XLA Ops:
  13.7 1.5 copy-start
  17.3 10.7 %copy-start.19 = (s32[1,8,1,2]{1,3,2,0:T(2,128)S(1)}, s32[1,8,1,2]{1,3,2,0:T(2,128)}, u32[]{:S(2)}) copy-start(s32[1,8,1,2]{1,3,2,0:T(2,128)} %param.8) | copy-start | bytes 196
  17.4 34.9 %collective-permute-start = (f32[2,640,256]{2,1,0:T(8,128)}, f32[2,640,256]{2,1,0:T(8,128)S(1)}, u32[]{:S(2)}, u32[]{:S(2)}) collective-permute-start(f32[2,640,256]{2,1,0:T(8,128)} %get-tuple-element.12), channel_id=1, source_target_pairs={{0,128},{64,192},{128,256},{192,320},{256,384},{320,448},{384,0},{... | collective-permute-start | bytes 3932168 | tf_op jit(solution)/shard_map/ppermute | solution.py:311
  20.6 34.1 %collective-permute-start.1 = (f32[2,640,256]{2,1,0:T(8,128)}, f32[2,640,256]{2,1,0:T(8,128)}, u32[]{:S(2)}, u32[]{:S(2)}) collective-permute-start(f32[2,640,256]{2,1,0:T(8,128)} %get-tuple-element.13), channel_id=1, source_target_pairs={{0,384},{64,448},{128,0},{192,64},{256,128},{320,192},{384,256},{4... | collective-permute-start | bytes 3932168 | tf_op jit(solution)/shard_map/ppermute | solution.py:312
  25.2 0.8 copy-start.10
  26.1 4.3 %collective-permute-start.2 = (f32[1,640,256]{2,1,0:T(8,128)}, f32[1,640,256]{2,1,0:T(8,128)}, u32[]{:S(2)}, u32[]{:S(2)}) collective-permute-start(f32[1,640,256]{2,1,0:T(8,128)} %get-tuple-element.15), channel_id=1, source_target_pairs={{0,64},{64,0},{128,192},{192,128},{256,320},{320,256},{384,448},{4... | collective-permute-start | bytes 1966088 | tf_op jit(solution)/shard_map/ppermute | solution.py:305
  28.1 1.5 copy-start.1
  29.6 0.8 copy-start.17
  29.6 0.8 copy-start.18
  30.4 1.1 copy-start.11
  52.2 3.8 %copy-start.2 = (f32[2,640,256]{2,1,0:T(8,128)}, f32[2,640,256]{2,1,0:T(8,128)S(1)}, u32[]{:S(2)}) copy-start(f32[2,640,256]{2,1,0:T(8,128)S(1)} %collective-permute-done.refs_0_.refs_8_) | copy-start | bytes 3932164
  54.7 6.3 %copy-start.16 = (f32[768]{0:T(1024)S(1)}, f32[768]{0:T(1024)}, u32[]{:S(2)}) copy-start(f32[768]{0:T(1024)} %param.7) | copy-start | bytes 9220
  56.0 4.9 %collective-permute-start.3 = (f32[2,640,256]{2,1,0:T(8,128)S(1)}, f32[2,640,256]{2,1,0:T(8,128)S(1)}, u32[]{:S(2)}, u32[]{:S(2)}) collective-permute-start(f32[2,640,256]{2,1,0:T(8,128)S(1)} %halves.2), channel_id=1, source_target_pairs={{0,64},{64,0},{128,192},{192,128},{256,320},{320,256},{384,448},{4... | collective-permute-start | bytes 3932168 | tf_op jit(solution)/shard_map/ppermute | solution.py:305
  58.0 34.9 %collective-permute-start.4 = (f32[2,640,256]{2,1,0:T(8,128)}, f32[2,640,256]{2,1,0:T(8,128)}, u32[]{:S(2)}, u32[]{:S(2)}) collective-permute-start(f32[2,640,256]{2,1,0:T(8,128)} %get-tuple-element.19), channel_id=1, source_target_pairs={{0,256},{64,320},{128,384},{192,448},{256,0},{320,64},{384,128},{4... | collective-permute-start | bytes 3932168 | tf_op jit(solution)/shard_map/ppermute | solution.py:320
  61.1 1.3 copy-start.3
  64.8 1.1 copy-start.7
  65.9 0.9 copy-start.9
  66.8 32.0 %all-to-all-start.1 = ((f32[16,96,128]{2,1,0:T(8,128)}), f32[16,96,128]{2,1,0:T(8,128)S(1)}, u32[]{:S(2)}, u32[]{:S(2)}) async-start(f32[16,96,128]{2,1,0:T(8,128)} %copy-done.9), calls=%async_computation.1 | async-start | bytes 1572864 | tf_op jit(solution)/shard_map/all_to_all | solution.py:308
  94.0 4.0 %collective-permute-start.5 = (f32[1,640,256]{2,1,0:T(8,128)S(1)}, f32[1,640,256]{2,1,0:T(8,128)S(1)}, u32[]{:S(2)}, u32[]{:S(2)}) collective-permute-start(f32[1,640,256]{2,1,0:T(8,128)S(1)} %halves.3), channel_id=1, source_target_pairs={{0,64},{64,0},{128,192},{192,128},{256,320},{320,256},{384,448},{4... | collective-permute-start | bytes 1966088 | tf_op jit(solution)/shard_map/ppermute | solution.py:305
  98.0 0.9 copy-start.13
  98.8 1.1 copy-start.14
  134.4 4.8 %copy-start.12 = (f32[1,640,256]{2,1,0:T(8,128)S(1)}, f32[1,640,256]{2,1,0:T(8,128)}, u32[]{:S(2)}) copy-start(f32[1,640,256]{2,1,0:T(8,128)} %copy-done.10) | copy-start | bytes 1966084
  134.4 14.5 %all-to-all-start.3 = ((f32[16,32,128]{2,1,0:T(8,128)}), f32[16,32,128]{2,1,0:T(8,128)S(1)}, u32[]{:S(2)}, u32[]{:S(2)}) async-start(f32[16,32,128]{2,1,0:T(8,128)} %exchange.7), calls=%async_computation.3 | async-start | bytes 524288 | tf_op jit(solution)/shard_map/all_to_all | solution.py:308
  139.3 1.3 copy-start.4
  140.6 1.3 copy-start.8
  145.0 1.3 copy-start.5
  149.7 10.4 %collective-permute-start.6 = (f32[8]{0:T(128)S(1)}, f32[8]{0:T(128)S(1)}, u32[]{:S(2)}, u32[]{:S(2)}) collective-permute-start(f32[8]{0:T(128)S(1)} %maximum_reduce_fusion), channel_id=1, source_target_pairs={{0,1},{1,0},{2,3},{3,2},{4,5},{5,4},{6,7},{7,6},{8,9},{9,8},{10,11... | collective-permute-start | bytes 104 | tf_op jit(solution)/shard_map/ppermute | solution.py:337
  154.2 1.5 copy-start.6
  155.7 1.1 copy-start.15
  160.1 9.3 %collective-permute-start.7 = (f32[8]{0:T(128)S(1)}, f32[8]{0:T(128)S(1)}, u32[]{:S(2)}, u32[]{:S(2)}) collective-permute-start(f32[8]{0:T(128)S(1)} %add.84), channel_id=1, source_target_pairs={{0,2},{1,3},{2,0},{3,1},{4,6},{5,7},{6,4},{7,5},{8,10},{9,11},{10,... | collective-permute-start | bytes 104 | tf_op jit(solution)/shard_map/ppermute | solution.py:337

commit v5 on v4

--- a/solution.py
+++ b/solution.py
@@ -132,27 +132,32 @@
     return occ - columns_ref[pl.ds(row, count), :] - levels_ref[pl.ds(second, 1), :]
 
 
-def add_amplitude(scalars, shifts, parts_at, parts_ref, columns_ref, levels_ref, out_ref):
+def add_amplitude(scalars, shifts, parts_at, parts_ref, columns_ref, levels_ref, out_ref, energy_ref):
     ids_ref, _, _, live_ref = scalars
     for k, shift in enumerate(shifts):
+        energy = jnp.zeros((1, TILE), jnp.float32)
         for s in range(2):
             t = 2 * k + s
             partner, first, second = tiles_of(scalars, shift, s, levels_ref.shape[0])
             denominator = denominator_of(scalars, columns_ref, levels_ref, partner, first, second, 8 * ids_ref[1], 8)
             summed = jnp.sum(parts_ref[:, parts_at + 8 * t : parts_at + 8 * t + 8, :], axis=0)
             amplitude = summed / jnp.where(s < live_ref[partner], denominator, jnp.inf)
+            energy = energy + jnp.sum(summed * amplitude, axis=0, keepdims=True)
             for owner in range(out_ref.shape[0]):
                 out_ref[owner, 8 * t : 8 * t + 8, :] = amplitude
+        energy_ref[k : k + 1, :] = energy
     return 16 * len(shifts)
 
 
 def exchange_kernel(back_shifts, parts_at, shifts, entries, *refs):
+    if back_shifts:
+        *refs, energy_ref = refs
     *in_refs, out_ref = refs
     scalars, in_refs = in_refs[:4], in_refs[4:]
     at = 0
     if back_shifts:
         parts_ref, columns_ref, levels_ref, *in_refs = in_refs
-        at = add_amplitude(scalars, back_shifts, parts_at, parts_ref, columns_ref, levels_ref, out_ref)
+        at = add_amplitude(scalars, back_shifts, parts_at, parts_ref, columns_ref, levels_ref, out_ref, energy_ref)
     if entries:
         left_ref, *right_refs = in_refs
         for k, ((which, entry), shift) in enumerate(zip(entries, shifts)):
@@ -184,9 +189,10 @@
         flops = len(entries) * 16 * TILE * TILE * left_split.shape[2]
     return pl.pallas_call(
         functools.partial(exchange_kernel, back_shifts, parts_at, shifts, entries),
-        out_shape=jax.ShapeDtypeStruct((TILE // 8, rows, TILE), jnp.float32),
+        out_shape=[jax.ShapeDtypeStruct((TILE // 8, rows, TILE), jnp.float32)]
+        + [jax.ShapeDtypeStruct((len(back_shifts), TILE), jnp.float32)] * bool(back_shifts),
         in_specs=specs,
-        out_specs=VMEM,
+        out_specs=[VMEM] * (1 + bool(back_shifts)),
         compiler_params=params(),
         cost_estimate=cost(flops, TILE // 8 * rows * TILE * 8),
         name="exchange",
@@ -205,34 +211,6 @@
 
 def tile_amplitude(amplitude_ref, t):
     return amplitude_ref[:, 8 * t : 8 * t + 8, :].reshape(TILE, TILE)
-
-
-def energy_kernel(groups, *refs):
-    scalars, (columns_ref, levels_ref, *amplitude_refs, out_ref) = refs[:4], refs[4:]
-    rows = []
-    for shifts, amplitude_ref in zip(groups, amplitude_refs):
-        for k, shift in enumerate(shifts):
-            for s in range(2):
-                amplitude = tile_amplitude(amplitude_ref, 2 * k + s)
-                place = tiles_of(scalars, shift, s, levels_ref.shape[0])
-                denominator = denominator_of(scalars, columns_ref, levels_ref, *place, 0, TILE)
-                rows.append(jnp.sum(amplitude * amplitude * denominator, axis=0, keepdims=True))
-    for k in range(len(rows) // 2):
-        out_ref[k : k + 1, :] = rows[2 * k] + rows[2 * k + 1]
-
-
-def energy_of(scalars, columns, levels, groups):
-    shifts = [group[0] for group in groups]
-    partners = sum(len(group) for group in shifts)
-    return pl.pallas_call(
-        functools.partial(energy_kernel, shifts),
-        out_shape=jax.ShapeDtypeStruct((partners, TILE), jnp.float32),
-        in_specs=[SMEM] * 4 + [VMEM] * (2 + len(groups)),
-        out_specs=VMEM,
-        compiler_params=params(),
-        cost_estimate=cost(6 * partners * TILE * TILE, partners * TILE * TILE * 8),
-        name="energy",
-    )(*scalars, columns, levels, *[group[1] for group in groups])
 
 
 def gamma_kernel(groups, carried, *refs):
@@ -281,12 +259,14 @@
 
 
 EARLY = ((0, 0), (0, 1))
-NEAR = ((1, 0), (3, 0), (1, 1), (3, 1))
+NEAR = ((1, 0), (3, 0))
+CROSS = ((1, 1), (3, 1))
 FAR = ((2, 0), (2, 1))
 
 
 def per_device(bq, eps_occ, eps_vir, tile_pairs, live_counts):
     occ_size = lax.axis_size("occ")
+    owners = lax.axis_size("aux")
     me = lax.axis_index("occ")
     block = bq[0]
     rows, cols = block.shape
@@ -298,47 +278,47 @@
     columns = jnp.broadcast_to(eps_vir[:, None], (cols, TILE))
     levels = eps_vir.reshape(cols // TILE, TILE)
 
-    def route(dx, dc):
-        return [(x * 2 + c, (x + dx) % CHIPS * 2 + (c + dc) % 2) for x in range(CHIPS) for c in range(2)]
-
-    def swapped(tiles):
-        return lax.ppermute(tiles, "occ", route(0, 1))
+    def moved(tiles, dx, dc):
+        route = [(x * 2 + c, (x + dx) % CHIPS * 2 + (c + dc) % 2) for x in range(CHIPS) for c in range(2)]
+        return lax.ppermute(tiles, "occ", route)
 
     def sent(returned, group):
-        return lax.all_to_all(exchange(scalars, returned, group), "aux", 0, 0)
+        if returned is not None:
+            returned = (*returned, columns, levels)
+        operand, *energy = exchange(scalars, returned, group)
+        return lax.all_to_all(operand, "aux", 0, 0), *energy
 
     ahead, behind = pick(ids, all_pairs, block, ((1, 0), (1, 1), (3, 0), (3, 1)), (2, 2), padded)
-    ahead = lax.ppermute(ahead, "occ", route(1, 0))
-    behind = lax.ppermute(behind, "occ", route(3, 0))
-    own, mate, far = pick(ids, all_pairs, block, ((0, 0), (0, 1), (2, 0), (2, 1)), (1, 1, 2), padded)
-    mate = swapped(mate)
+    ahead, behind = moved(ahead, 1, 0), moved(behind, 3, 0)
+    own, mate, far = pick(ids, all_pairs, block, EARLY + FAR, (1, 1, 2), padded)
+    mate = moved(mate, 0, 1)
     left_split = left(block, padded)
-
     early_rights = [(own, 0), (mate, 0)]
-    early_parts = sent(None, (EARLY, left_split, early_rights))
-    far, ahead, behind, early_parts = lax.optimization_barrier((far, ahead, behind, early_parts))
-    far = lax.ppermute(far, "occ", route(2, 0))
-    near_mate = swapped(halves(ahead, behind))
-    near_rights = [(ahead, 0), (behind, 0), (near_mate, 0), (near_mate, 1)]
-    near = sent((EARLY, early_parts, 0, columns, levels), (NEAR, left_split, near_rights))
-
-    far_mate = swapped(halves(far))
+
+    (first,) = sent(None, (EARLY, left_split, early_rights))
+    far, ahead, behind, first = lax.optimization_barrier((far, ahead, behind, first))
+    far = moved(far, 2, 0)
+    near_rights = [(ahead, 0), (behind, 0)]
+    cross_tiles = moved(halves(ahead, behind), 0, 1)
+    cross_rights = [(cross_tiles, 0), (cross_tiles, 1)]
+    back = 16 * len(EARLY)
+    early, early_energy = sent((EARLY, first, 0), (NEAR, left_split, near_rights))
+    near, near_energy = sent((NEAR, early, back), (CROSS, left_split, cross_rights))
+    far_mate = moved(halves(far), 0, 1)
     far_rights = [(far, 0), (far_mate, 0)]
-    both = sent((NEAR, near, 16 * len(EARLY), columns, levels), (FAR, left_split, far_rights))
-    last = sent((FAR, both, 16 * len(NEAR), columns, levels), None)
-    first_groups = [(EARLY, near, early_rights), (NEAR, both, near_rights)]
-    total = gamma_add(scalars, first_groups, rows, cols, None)
-    first_energy = energy_of(scalars, columns, levels, first_groups)
-    last_energy = energy_of(scalars, columns, levels, [(FAR, last)])
-
-    energy = jnp.sum(jnp.concatenate([first_energy, last_energy], axis=0), axis=1)
-    for bit in (1, 2):
-        blocks = range(lax.axis_size("vir"))
-        energy = energy + lax.ppermute(energy, "vir", [(v, v ^ bit) for v in blocks])
-    order = jnp.stack([(me // 2 - dx) % CHIPS * 2 + (me + dc) % 2 for dx, dc in EARLY + NEAR + FAR])
+    cross, cross_energy = sent((CROSS, near, back), (FAR, left_split, far_rights))
+    total = gamma_add(scalars, [(EARLY, early, early_rights), (NEAR, near, near_rights)], rows, cols, None)
+    cross, total = lax.optimization_barrier((cross, total))
+    last, last_energy = sent((FAR, cross, back), None)
+
+    energy = jnp.concatenate([early_energy, near_energy, cross_energy, last_energy], axis=0)
+    energy, last = lax.optimization_barrier((lax.psum(energy, "vir"), last))
+    energy = lax.all_to_all(jnp.broadcast_to(energy, (owners, *energy.shape)), "aux", 0, 0)
+    energy = jnp.sum(energy, axis=(0, 2))
+    order = jnp.stack([(me // 2 - dx) % CHIPS * 2 + (me + dc) % 2 for dx, dc in EARLY + NEAR + CROSS + FAR])
     mine = order[:, None] == jnp.arange(occ_size)[None, :]
     energy = jnp.sum(jnp.where(mine, energy[:, None], 0.0), axis=0)
-    total = gamma_add(scalars, [(FAR, last, far_rights)], rows, cols, total)
+    total = gamma_add(scalars, [(CROSS, cross, cross_rights), (FAR, last, far_rights)], rows, cols, total)
     return total[None], energy[None]
 
 

time: 171 us -> 195 us (1.14)
  blocking collectives: 62.9 us -> 43.7 us
  Pallas kernels: 22.2 us -> 41.1 us
  starting transfers between devices: 36.1 us -> 48.3 us
  waiting for transfers between devices: 29.7 us -> 41 us
    all_to_all x2 -> x1, blocking collectives: 50.2 us -> 19 us  [sent(): return (lax.all_to_all(operand, 'aux', 0, 0), *energy)]
    all_to_all x2 -> x5, waiting for transfers between devices: 2.73 us -> 27.6 us  [the longest x4 24.5 us: sent(): return (lax.all_to_all(operand, 'aux', 0, 0), *energy)]
    all_to_all x2 -> x5, starting transfers between devices: 12.6 us -> 34.7 us  [the longest x4 26.6 us: sent(): return (lax.all_to_all(operand, 'aux', 0, 0), *energy)]
    pallas_call x2, Pallas kernels: 2.4 us -> 21.2 us  [halves(): pl.pallas_call(halves_kernel, out_shape=jax.ShapeDtypeStruct((len(arrays)...]
    ppermute x8 -> x6, waiting for transfers between devices: 27 us -> 13.4 us  [moved(): return lax.ppermute(tiles, 'occ', route)]
    psum x0 -> x1, blocking collectives: none -> 12 us  [per_device(): energy, last = lax.optimization_barrier((lax.psum(energy, 'vir'), last))]
    ppermute x8 -> x6, starting transfers between devices: 23.4 us -> 13.5 us  [moved(): return lax.ppermute(tiles, 'occ', route)]
    pallas_call x4 -> x5, Pallas kernels: 7.38 us -> 8.85 us  [exchange(): pl.pallas_call(functools.partial(exchange_kernel, back_shifts, parts_at,...]
  transfers between devices with their start and end apart: 10 -> 11, of which waited for: 7 -> 8; matrix products, arithmetic and copies ran while one was open for 0% -> 0% of each run, Pallas kernels for 9% -> 8%
where the time goes in v5:
time: 195 us; the launch traced here: 194 us
  starting transfers between devices  48.3 us (25%)
  blocking collectives  43.7 us (22%)
  Pallas kernels  41.1 us (21%)
  waiting for transfers between devices  41 us (21%)
  local copies, waits for them, and re-layouts  17.8 us (9%)
    all_to_all x4, starting transfers between devices, sent(): return (lax.all_to_all(operand, 'aux', 0, 0), *energy)  26.6 us
    all_to_all x4, waiting for transfers between devices, sent(): return (lax.all_to_all(operand, 'aux', 0, 0), *energy)  24.5 us
    pallas_call x2, Pallas kernels, halves(): pl.pallas_call(halves_kernel, out_shape=jax.ShapeDtypeStruct((len(arrays)...  21.2 us
    all_to_all x1, blocking collectives, sent(): return (lax.all_to_all(operand, 'aux', 0, 0), *energy)  19 us
    unnamed x49, local copies, waits for them, and re-layouts  16.6 us
    ppermute x6, starting transfers between devices, moved(): return lax.ppermute(tiles, 'occ', route)  13.5 us
    ppermute x6, waiting for transfers between devices, moved(): return lax.ppermute(tiles, 'occ', route)  13.4 us
    all_gather x1, blocking collectives, per_device(): all_pairs = lax.all_gather(tile_pairs[0, :, 0, :], 'occ').reshape(-1)  12.7 us
  transfers between devices with their start and end apart: 11, of which 8 were waited for; matrix products, arithmetic and copies ran while one was open for 0% of the time, Pallas kernels for 8%

profile of v5, /device:TPU:6, one launch (start us, length us, event | category | flops | bytes accessed | tf_op | source)
XLA Modules:
  0.0 193.7 jit_solution(8920847932173396462)
XLA Ops:
  0.6 12.7 %all-gather = s32[8,8,1,2]{1,3,2,0:T(2,128)S(1)} all-gather(s32[1,8,1,2]{1,3,2,0:T(2,128)} %param.8), channel_id=2, replica_groups=mesh['occ'=8,'aux'=16,'vir'=4] {'occ'}, dimensions={0}, use_global_device_ids=true | all-gather | bytes 576 | tf_op jit(solution)/shard_map/all_gather | solution.py:275
  13.3 0.1 copy.14
  13.4 0.1 reshape.21.pairs_ref
  13.6 0.1 pad_add_fusion.ids_ref.refs_0_
  13.7 1.5 copy-done
  15.2 2.2 %pick.3 = (f32[2,640,256]{2,1,0:T(8,128)}, f32[2,640,256]{2,1,0:T(8,128)}) custom-call(s32[2]{0:T(128)S(1)} %pad_add_fusion.ids_ref.refs_0_, s32[128]{0:T(128)S(1)} %reshape.21.pairs_ref, f32[632,768]{1,0:T(8,128)S(1)} %bitcast.23), custom_call_target="tpu_custom_call" | custom-call | bytes 5242880 | tf_op jit(solution)/shard_map/pick/pallas_call | solution.py:60
  17.4 0.0 copy-start.23
  17.4 3.2 %collective-permute-start = (f32[2,640,256]{2,1,0:T(8,128)}, f32[2,640,256]{2,1,0:T(8,128)S(1)}, u32[]{:S(2)}, u32[]{:S(2)}) collective-permute-start(f32[2,640,256]{2,1,0:T(8,128)} %get-tuple-element.24), channel_id=1, source_target_pairs={{0,128},{64,192},{128,256},{192,320},{256,384},{320,448},{384,0},{... | collective-permute-start | bytes 3932168 | tf_op jit(solution)/shard_map/ppermute | solution.py:283
  20.6 2.6 %collective-permute-start.1 = (f32[2,640,256]{2,1,0:T(8,128)}, f32[2,640,256]{2,1,0:T(8,128)}, u32[]{:S(2)}, u32[]{:S(2)}) collective-permute-start(f32[2,640,256]{2,1,0:T(8,128)} %get-tuple-element.25), channel_id=1, source_target_pairs={{0,384},{64,448},{128,0},{192,64},{256,128},{320,192},{384,256},{4... | collective-permute-start | bytes 3932168 | tf_op jit(solution)/shard_map/ppermute | solution.py:283
  23.3 1.6 pick.2
  24.9 0.8 copy-done.13
  25.7 1.1 copy-done.22
  26.8 1.9 collective-permute-start.2
  28.7 0.1 copy.13
  28.8 1.5 copy-done.1
  30.4 0.6 left.1.refs_4_.refs_7_
  31.0 0.1 reshape.19.refs_1_
  31.0 0.1 collective-permute-done.2.refs_6_
  31.1 1.1 copy-done.14
  32.2 1.7 exchange.5
  33.9 19.0 %all_to_all.30.refs_4_ = f32[16,32,128]{2,1,0:T(8,128)S(1)} all-to-all(f32[16,32,128]{2,1,0:T(8,128)S(1)} %exchange.5), channel_id=1, replica_groups=mesh['occ'=8,'aux'=16,'vir'=4] {'aux'}, dimensions={0} | all-to-all | bytes 524288 | tf_op jit(solution)/shard_map/all_to_all | solution.py:289
  52.9 0.0 collective-permute-done.refs_8_.refs_0_
  53.0 1.8 collective-permute-done.1.refs_9_.refs_1_
  54.8 21.0 %halves.2 = f32[2,640,256]{2,1,0:T(8,128)} custom-call(f32[2,640,256]{2,1,0:T(8,128)S(1)} %collective-permute-done.refs_8_.refs_0_, f32[2,640,256]{2,1,0:T(8,128)} %collective-permute-done.1.refs_9_.refs_1_), custom_call_target="tpu_custom_call" | custom-call | bytes 2621440 | tf_op jit(solution)/shard_map/halves/pallas_call | solution.py:85
  75.7 1.9 collective-permute-start.3
  77.7 0.2 broadcast_in_dim.30.refs_5_
  77.9 2.1 %exchange.6 = (f32[16,64,128]{2,1,0:T(8,128)S(1)}, f32[2,128]{1,0:T(2,128)S(1)}) custom-call(s32[2]{0:T(128)S(1)} %pad_add_fusion.ids_ref.refs_0_, s32[16]{0:T(128)S(1)} %reshape.19.refs_1_, f32[8]{0:T(128)S(1)} %copy-done.20, s32[8]{0:T(128)S(1)} %bitcast.31, f32[16,32,128]{2,1,0:T(8,128)S(1)} %all_to_all.30.refs_4_, ...), custom_call_target="tpu_custom_call" | custom-call | flops 335544320 | bytes 1048576 | tf_op jit(solution)/shard_map/exchange/pallas_call | solution.py:190
  80.0 0.8 copy-done.18
  80.8 8.8 %all-to-all-start.1 = ((f32[16,64,128]{2,1,0:T(8,128)}), f32[16,64,128]{2,1,0:T(8,128)}, u32[]{:S(2)}, u32[]{:S(2)}) async-start(f32[16,64,128]{2,1,0:T(8,128)} %copy-done.18), calls=%async_computation.1 | async-start | bytes 1048576 | tf_op jit(solution)/shard_map/all_to_all | solution.py:289
  89.5 1.9 collective-permute-start.4
  91.5 14.2 %all-to-all-done.1.refs_4_ = f32[16,64,128]{2,1,0:T(8,128)} async-done(((f32[16,64,128]{2,1,0:T(8,128)}), f32[16,64,128]{2,1,0:T(8,128)}, u32[]{:S(2)}, u32[]{:S(2)}) %all-to-all-start.1) | async-done | bytes 524320 | tf_op jit(solution)/shard_map/all_to_all | solution.py:289
  105.6 0.0 collective-permute-done.3.refs_8_.refs_6_
  105.6 1.0 copy-done.5
  106.6 2.1 %exchange.7 = (f32[16,64,128]{2,1,0:T(8,128)S(1)}, f32[2,128]{1,0:T(2,128)S(1)}) custom-call(s32[2]{0:T(128)S(1)} %pad_add_fusion.ids_ref.refs_0_, s32[16]{0:T(128)S(1)} %reshape.19.refs_1_, f32[8]{0:T(128)S(1)} %copy-done.20, s32[8]{0:T(128)S(1)} %bitcast.32, f32[16,64,128]{2,1,0:T(8,128)} %all-to-all-done.1.refs_4_, f32[768,128]{1,0:T(8,128)S(1)} %copy-done.5, ...), custom_call_target="tpu_custom_call" | custom-call | flops 335544320 | bytes 1048576 | tf_op jit(solution)/shard_map/exchange/pallas_call | solution.py:190
  108.8 0.0 copy-start.16
  108.8 0.8 copy-done.16
  109.6 5.1 %all-to-all-start.2 = ((f32[16,64,128]{2,1,0:T(8,128)}), f32[16,64,128]{2,1,0:T(8,128)}, u32[]{:S(2)}, u32[]{:S(2)}) async-start(f32[16,64,128]{2,1,0:T(8,128)} %copy-done.16), calls=%async_computation.2 | async-start | bytes 1048576 | tf_op jit(solution)/shard_map/all_to_all | solution.py:289
  114.6 9.4 %collective-permute-done.4.refs_0_.refs_8_ = f32[2,640,256]{2,1,0:T(8,128)S(1)} collective-permute-done((f32[2,640,256]{2,1,0:T(8,128)}, f32[2,640,256]{2,1,0:T(8,128)S(1)}, u32[]{:S(2)}, u32[]{:S(2)}) %collective-permute-start.4) | collective-permute-done | bytes 1310752 | tf_op jit(solution)/shard_map/ppermute | solution.py:283
  124.1 0.2 halves.3
  124.3 1.9 collective-permute-start.5
  126.2 2.1 %collective-permute-done.5.refs_9_ = f32[1,640,256]{2,1,0:T(8,128)S(1)} collective-permute-done((f32[1,640,256]{2,1,0:T(8,128)S(1)}, f32[1,640,256]{2,1,0:T(8,128)S(1)}, u32[]{:S(2)}, u32[]{:S(2)}) %collective-permute-start.5) | collective-permute-done | bytes 655392 | tf_op jit(solution)/shard_map/ppermute | solution.py:283
  128.3 0.8 copy-done.10
  129.1 0.9 all-to-all-done.2.refs_4_.refs_7_
  130.0 1.0 copy-done.6
  131.0 1.1 copy-done.11
  132.1 1.7 exchange.8
  133.7 0.8 copy-done.17
  134.5 7.0 %all-to-all-start.3 = ((f32[16,64,128]{2,1,0:T(8,128)}), f32[16,64,128]{2,1,0:T(8,128)S(1)}, u32[]{:S(2)}, u32[]{:S(2)}) async-start(f32[16,64,128]{2,1,0:T(8,128)} %copy-done.17), calls=%async_computation.3 | async-start | bytes 1048576 | tf_op jit(solution)/shard_map/all_to_all | solution.py:289
  141.6 1.3 copy-done.3
  142.9 3.0 %gamma.2.refs_4_ = f32[632,768]{1,0:T(8,128)S(1)} custom-call(s32[2]{0:T(128)S(1)} %pad_add_fusion.ids_ref.refs_0_, s32[16]{0:T(128)S(1)} %reshape.19.refs_1_, f32[8]{0:T(128)S(1)} %copy-done.20, s32[8]{0:T(128)S(1)} %bitcast.34, f32[16,64,128]{2,1,0:T(8,128)} %all-to-all-done.1.refs_4_, f32[1,640,256]{2,1,0:T(8,128)S(1)} %copy-done.15, ...), custom_call_target="tpu_custom_call" | custom-call | flops 662700032 | bytes 3883008 | tf_op jit(solution)/shard_map/gamma/pallas_call | solution.py:250
  145.9 0.0 copy-start.8
  146.0 1.3 copy-done.8
  147.2 9.4 %all-to-all-done.3.refs_4_.refs_5_ = f32[16,64,128]{2,1,0:T(8,128)S(1)} async-done(((f32[16,64,128]{2,1,0:T(8,128)}), f32[16,64,128]{2,1,0:T(8,128)S(1)}, u32[]{:S(2)}, u32[]{:S(2)}) %all-to-all-start.3) | async-done | bytes 524320 | tf_op jit(solution)/shard_map/all_to_all | solution.py:289
  156.7 1.3 exchange.9
  158.0 5.7 %all-to-all-start.4 = ((f32[16,32,128]{2,1,0:T(8,128)}), f32[16,32,128]{2,1,0:T(8,128)S(1)}, u32[]{:S(2)}, u32[]{:S(2)}) async-start(f32[16,32,128]{2,1,0:T(8,128)} %get-tuple-element.41), calls=%async_computation.4 | async-start | bytes 524288 | tf_op jit(solution)/shard_map/all_to_all | solution.py:289
  163.7 12.0 %psum.7 = f32[8,128]{1,0:T(8,128)S(1)} all-reduce(f32[8,128]{1,0:T(8,128)S(1)} %pad_maximum_fusion), channel_id=1, replica_groups=mesh['occ'=8,'aux'=16,'vir'=4] {'vir'}, use_global_device_ids=true, to_apply=%region_0.0 | all-reduce | flops 1024 | bytes 8192 | tf_op jit(solution)/shard_map/psum | solution.py:315
  175.7 0.6 broadcast_in_dim.32
  176.3 8.2 %all-to-all-start.5 = ((f32[16,8,128]{2,1,0:T(8,128)}), f32[16,8,128]{2,1,0:T(8,128)S(1)}, u32[]{:S(2)}, u32[]{:S(2)}) async-start(f32[16,8,128]{2,1,0:T(8,128)} %broadcast_in_dim.32), calls=%async_computation.5 | async-start | bytes 131072 | tf_op jit(solution)/shard_map/all_to_all | solution.py:316
  184.6 0.1 stack.47
  184.7 1.5 copy-done.9
  186.2 3.7 %gamma.3 = f32[632,768]{1,0:T(8,128)} custom-call(s32[2]{0:T(128)S(1)} %pad_add_fusion.ids_ref.refs_0_, s32[16]{0:T(128)S(1)} %reshape.19.refs_1_, f32[8]{0:T(128)S(1)} %copy-done.20, s32[8]{0:T(128)S(1)} %bitcast.36, f32[632,768]{1,0:T(8,128)S(1)} %copy-done.9, f32[16,64,128]{2,1,0:T(8,128)S(1)} %all-to-all-done.3.refs_4_.refs_5_, ...), custom_call_target="tpu_custom_call" | custom-call | flops 662700032 | bytes 3883008 | tf_op jit(solution)/shard_map/gamma/pallas_call | solution.py:250
  189.9 3.1 %all-to-all-done.5 = f32[16,8,128]{2,1,0:T(8,128)S(1)} async-done(((f32[16,8,128]{2,1,0:T(8,128)}), f32[16,8,128]{2,1,0:T(8,128)S(1)}, u32[]{:S(2)}, u32[]{:S(2)}) %all-to-all-start.5) | async-done | bytes 65568 | tf_op jit(solution)/shard_map/all_to_all | solution.py:316
  193.0 0.1 reduce_sum.18
  193.2 0.6 select_reduce_fusion
  (32 shorter events, 0.1 us)
Async XLA Ops:
  13.7 1.5 copy-start
  17.4 11.4 %copy-start.23 = (s32[1,8,1,2]{1,3,2,0:T(2,128)S(1)}, s32[1,8,1,2]{1,3,2,0:T(2,128)}, u32[]{:S(2)}) copy-start(s32[1,8,1,2]{1,3,2,0:T(2,128)} %param.8) | copy-start | bytes 196
  17.4 35.6 %collective-permute-start = (f32[2,640,256]{2,1,0:T(8,128)}, f32[2,640,256]{2,1,0:T(8,128)S(1)}, u32[]{:S(2)}, u32[]{:S(2)}) collective-permute-start(f32[2,640,256]{2,1,0:T(8,128)} %get-tuple-element.24), channel_id=1, source_target_pairs={{0,128},{64,192},{128,256},{192,320},{256,384},{320,448},{384,0},{... | collective-permute-start | bytes 3932168 | tf_op jit(solution)/shard_map/ppermute | solution.py:283
  20.6 34.1 %collective-permute-start.1 = (f32[2,640,256]{2,1,0:T(8,128)}, f32[2,640,256]{2,1,0:T(8,128)}, u32[]{:S(2)}, u32[]{:S(2)}) collective-permute-start(f32[2,640,256]{2,1,0:T(8,128)} %get-tuple-element.25), channel_id=1, source_target_pairs={{0,384},{64,448},{128,0},{192,64},{256,128},{320,192},{384,256},{4... | collective-permute-start | bytes 3932168 | tf_op jit(solution)/shard_map/ppermute | solution.py:283
  24.9 0.8 copy-start.13
  25.7 1.1 copy-start.22
  26.8 4.3 %collective-permute-start.2 = (f32[1,640,256]{2,1,0:T(8,128)}, f32[1,640,256]{2,1,0:T(8,128)}, u32[]{:S(2)}, u32[]{:S(2)}) collective-permute-start(f32[1,640,256]{2,1,0:T(8,128)} %get-tuple-element.27), channel_id=1, source_target_pairs={{0,64},{64,0},{128,192},{192,128},{256,320},{320,256},{384,448},{4... | collective-permute-start | bytes 1966088 | tf_op jit(solution)/shard_map/ppermute | solution.py:283
  28.8 1.5 copy-start.1
  30.4 0.8 copy-start.20
  30.4 0.8 copy-start.21
  31.1 1.1 copy-start.14
  53.0 24.9 %copy-start.2 = (f32[2,640,256]{2,1,0:T(8,128)}, f32[2,640,256]{2,1,0:T(8,128)S(1)}, u32[]{:S(2)}) copy-start(f32[2,640,256]{2,1,0:T(8,128)S(1)} %collective-permute-done.refs_8_.refs_0_) | copy-start | bytes 3932164
  54.8 22.9 %copy-start.19 = (f32[768]{0:T(1024)S(1)}, f32[768]{0:T(1024)}, u32[]{:S(2)}) copy-start(f32[768]{0:T(1024)} %param.7) | copy-start | bytes 9220
  75.7 29.9 %collective-permute-start.3 = (f32[2,640,256]{2,1,0:T(8,128)}, f32[2,640,256]{2,1,0:T(8,128)}, u32[]{:S(2)}, u32[]{:S(2)}) collective-permute-start(f32[2,640,256]{2,1,0:T(8,128)} %halves.2), channel_id=1, source_target_pairs={{0,64},{64,0},{128,192},{192,128},{256,320},{320,256},{384,448},{4... | collective-permute-start | bytes 3932168 | tf_op jit(solution)/shard_map/ppermute | solution.py:283
  77.8 2.1 %copy-start.4 = (f32[768,128]{1,0:T(8,128)}, f32[768,128]{1,0:T(8,128)S(1)}, u32[]{:S(2)}) copy-start(f32[768,128]{1,0:T(8,128)S(1)} %broadcast_in_dim.30.refs_5_) | copy-start | bytes 1179652
  80.0 0.8 copy-start.18
  80.8 24.9 %all-to-all-start.1 = ((f32[16,64,128]{2,1,0:T(8,128)}), f32[16,64,128]{2,1,0:T(8,128)}, u32[]{:S(2)}, u32[]{:S(2)}) async-start(f32[16,64,128]{2,1,0:T(8,128)} %copy-done.18), calls=%async_computation.1 | async-start | bytes 1048576 | tf_op jit(solution)/shard_map/all_to_all | solution.py:289
  89.5 34.5 %collective-permute-start.4 = (f32[2,640,256]{2,1,0:T(8,128)}, f32[2,640,256]{2,1,0:T(8,128)S(1)}, u32[]{:S(2)}, u32[]{:S(2)}) collective-permute-start(f32[2,640,256]{2,1,0:T(8,128)} %copy-done.22), channel_id=1, source_target_pairs={{0,256},{64,320},{128,384},{192,448},{256,0},{320,64},{384,128},{4... | collective-permute-start | bytes 3932168 | tf_op jit(solution)/shard_map/ppermute | solution.py:283
  105.6 1.0 copy-start.5
  108.8 0.8 copy-start.16
  109.6 20.4 %all-to-all-start.2 = ((f32[16,64,128]{2,1,0:T(8,128)}), f32[16,64,128]{2,1,0:T(8,128)}, u32[]{:S(2)}, u32[]{:S(2)}) async-start(f32[16,64,128]{2,1,0:T(8,128)} %copy-done.16), calls=%async_computation.2 | async-start | bytes 1048576 | tf_op jit(solution)/shard_map/all_to_all | solution.py:289
  124.3 4.0 %collective-permute-start.5 = (f32[1,640,256]{2,1,0:T(8,128)S(1)}, f32[1,640,256]{2,1,0:T(8,128)S(1)}, u32[]{:S(2)}, u32[]{:S(2)}) collective-permute-start(f32[1,640,256]{2,1,0:T(8,128)S(1)} %halves.3), channel_id=1, source_target_pairs={{0,64},{64,0},{128,192},{192,128},{256,320},{320,256},{384,448},{4... | collective-permute-start | bytes 1966088 | tf_op jit(solution)/shard_map/ppermute | solution.py:283
  128.3 0.8 copy-start.10
  130.0 1.0 copy-start.6
  131.0 1.1 copy-start.11
  133.7 0.8 copy-start.17
  134.5 7.0 %copy-start.15 = (f32[1,640,256]{2,1,0:T(8,128)S(1)}, f32[1,640,256]{2,1,0:T(8,128)}, u32[]{:S(2)}) copy-start(f32[1,640,256]{2,1,0:T(8,128)} %copy-done.13) | copy-start | bytes 1966084
  134.5 22.1 %all-to-all-start.3 = ((f32[16,64,128]{2,1,0:T(8,128)}), f32[16,64,128]{2,1,0:T(8,128)S(1)}, u32[]{:S(2)}, u32[]{:S(2)}) async-start(f32[16,64,128]{2,1,0:T(8,128)} %copy-done.17), calls=%async_computation.3 | async-start | bytes 1048576 | tf_op jit(solution)/shard_map/all_to_all | solution.py:289
  141.6 1.3 copy-start.3
  142.9 13.7 %copy-start.7 = (f32[768,128]{1,0:T(8,128)S(1)}, f32[768,128]{1,0:T(8,128)}, u32[]{:S(2)}) copy-start(f32[768,128]{1,0:T(8,128)} %copy-done.4) | copy-start | bytes 1179652
  145.9 1.3 copy-start.8
  147.2 37.5 %copy-start.12 = (f32[1,640,256]{2,1,0:T(8,128)S(1)}, f32[1,640,256]{2,1,0:T(8,128)}, u32[]{:S(2)}) copy-start(f32[1,640,256]{2,1,0:T(8,128)} %copy-done.10) | copy-start | bytes 1966084
  158.0 17.7 %all-to-all-start.4 = ((f32[16,32,128]{2,1,0:T(8,128)}), f32[16,32,128]{2,1,0:T(8,128)S(1)}, u32[]{:S(2)}, u32[]{:S(2)}) async-start(f32[16,32,128]{2,1,0:T(8,128)} %get-tuple-element.41), calls=%async_computation.4 | async-start | bytes 524288 | tf_op jit(solution)/shard_map/all_to_all | solution.py:289
  176.3 16.7 %all-to-all-start.5 = ((f32[16,8,128]{2,1,0:T(8,128)}), f32[16,8,128]{2,1,0:T(8,128)S(1)}, u32[]{:S(2)}, u32[]{:S(2)}) async-start(f32[16,8,128]{2,1,0:T(8,128)} %broadcast_in_dim.32), calls=%async_computation.5 | async-start | bytes 131072 | tf_op jit(solution)/shard_map/all_to_all | solution.py:316
  184.7 1.5 copy-start.9

commit v6 on v4

--- a/solution.py
+++ b/solution.py
@@ -60,7 +60,7 @@
     return pl.pallas_call(
         functools.partial(pick_kernel, shifts),
         out_shape=[jax.ShapeDtypeStruct((count, padded, 2 * TILE), jnp.float32) for count in counts],
-        in_specs=[SMEM, SMEM, HBM],
+        in_specs=[SMEM, SMEM, VMEM],
         out_specs=[HBM] * len(counts),
         scratch_shapes=[
             pltpu.VMEM((padded - block.shape[0], 2 * TILE), jnp.float32),
@@ -72,25 +72,20 @@
     )(ids, pairs, block)
 
 
-def halves_kernel(*refs):
-    *in_refs, out_ref, sems = refs
-    copies = [pltpu.make_async_copy(ref.at[1], out_ref.at[k], sems.at[k]) for k, ref in enumerate(in_refs)]
-    for copy in copies:
-        copy.start()
-    for copy in copies:
-        copy.wait()
-
-
-def halves(*arrays):
-    return pl.pallas_call(
-        halves_kernel,
-        out_shape=jax.ShapeDtypeStruct((len(arrays), *arrays[0].shape[1:]), jnp.float32),
-        in_specs=[HBM] * len(arrays),
-        out_specs=HBM,
-        scratch_shapes=[pltpu.SemaphoreType.DMA((len(arrays),))],
-        compiler_params=params(),
-        cost_estimate=cost(0, sum(array.size for array in arrays) * 4),
-        name="halves",
+def held_kernel(*refs):
+    del refs
+
+
+def held(*arrays):
+    return pl.pallas_call(
+        held_kernel,
+        out_shape=[jax.ShapeDtypeStruct(array.shape, array.dtype) for array in arrays],
+        in_specs=[pl.BlockSpec(memory_space=pl.ANY)] * len(arrays),
+        out_specs=[pl.BlockSpec(memory_space=pl.ANY)] * len(arrays),
+        input_output_aliases={k: k for k in range(len(arrays))},
+        compiler_params=params(),
+        cost_estimate=cost(70 * 10**9, 70 * 3 * 10**6),
+        name="held",
     )(*arrays)
 
 
@@ -280,8 +275,7 @@
     )(*start, *inputs)
 
 
-EARLY = ((0, 0), (0, 1))
-NEAR = ((1, 0), (3, 0), (1, 1), (3, 1))
+NEAR = ((1, 0), (3, 0), (1, 1), (3, 1), (0, 1), (0, 0))
 FAR = ((2, 0), (2, 1))
 
 
@@ -298,35 +292,28 @@
     columns = jnp.broadcast_to(eps_vir[:, None], (cols, TILE))
     levels = eps_vir.reshape(cols // TILE, TILE)
 
-    def route(dx, dc):
-        return [(x * 2 + c, (x + dx) % CHIPS * 2 + (c + dc) % 2) for x in range(CHIPS) for c in range(2)]
-
-    def swapped(tiles):
-        return lax.ppermute(tiles, "occ", route(0, 1))
+    def moved(tiles, dx, dc):
+        route = [(x * 2 + c, (x + dx) % CHIPS * 2 + (c + dc) % 2) for x in range(CHIPS) for c in range(2)]
+        return lax.ppermute(tiles, "occ", route)
 
     def sent(returned, group):
         return lax.all_to_all(exchange(scalars, returned, group), "aux", 0, 0)
 
-    ahead, behind = pick(ids, all_pairs, block, ((1, 0), (1, 1), (3, 0), (3, 1)), (2, 2), padded)
-    ahead = lax.ppermute(ahead, "occ", route(1, 0))
-    behind = lax.ppermute(behind, "occ", route(3, 0))
-    own, mate, far = pick(ids, all_pairs, block, ((0, 0), (0, 1), (2, 0), (2, 1)), (1, 1, 2), padded)
-    mate = swapped(mate)
+    near = pick(ids, all_pairs, block, NEAR[:4], (1,) * 4, padded)
+    later_ids, *near = lax.optimization_barrier((ids, *near))
+    near = [moved(tiles, *shift) for tiles, shift in zip(near, NEAR)]
+    mate, own, *far = pick(later_ids, all_pairs, block, NEAR[4:] + FAR, (1,) * 4, padded)
+    mate = moved(mate, 0, 1)
     left_split = left(block, padded)
-
-    early_rights = [(own, 0), (mate, 0)]
-    early_parts = sent(None, (EARLY, left_split, early_rights))
-    far, ahead, behind, early_parts = lax.optimization_barrier((far, ahead, behind, early_parts))
-    far = lax.ppermute(far, "occ", route(2, 0))
-    near_mate = swapped(halves(ahead, behind))
-    near_rights = [(ahead, 0), (behind, 0), (near_mate, 0), (near_mate, 1)]
-    near = sent((EARLY, early_parts, 0, columns, levels), (NEAR, left_split, near_rights))
-
-    far_mate = swapped(halves(far))
-    far_rights = [(far, 0), (far_mate, 0)]
-    both = sent((NEAR, near, 16 * len(EARLY), columns, levels), (FAR, left_split, far_rights))
+    *far, near[0], near[1] = lax.optimization_barrier((*far, near[0], near[1]))
+    far = held(*[moved(tiles, *shift) for tiles, shift in zip(far, FAR)])
+    near_rights = [(tiles, 0) for tiles in (*near, mate, own)]
+    far_rights = [(tiles, 0) for tiles in far]
+
+    parts = sent(None, (NEAR, left_split, near_rights))
+    both = sent((NEAR, parts, 0, columns, levels), (FAR, left_split, far_rights))
     last = sent((FAR, both, 16 * len(NEAR), columns, levels), None)
-    first_groups = [(EARLY, near, early_rights), (NEAR, both, near_rights)]
+    first_groups = [(NEAR, both, near_rights)]
     total = gamma_add(scalars, first_groups, rows, cols, None)
     first_energy = energy_of(scalars, columns, levels, first_groups)
     last_energy = energy_of(scalars, columns, levels, [(FAR, last)])
@@ -335,7 +322,7 @@
     for bit in (1, 2):
         blocks = range(lax.axis_size("vir"))
         energy = energy + lax.ppermute(energy, "vir", [(v, v ^ bit) for v in blocks])
-    order = jnp.stack([(me // 2 - dx) % CHIPS * 2 + (me + dc) % 2 for dx, dc in EARLY + NEAR + FAR])
+    order = jnp.stack([(me // 2 - dx) % CHIPS * 2 + (me + dc) % 2 for dx, dc in NEAR + FAR])
     mine = order[:, None] == jnp.arange(occ_size)[None, :]
     energy = jnp.sum(jnp.where(mine, energy[:, None], 0.0), axis=0)
     total = gamma_add(scalars, [(FAR, last, far_rights)], rows, cols, total)

time: 171 us -> 190 us (1.11)
  starting transfers between devices: 36.1 us -> 71.3 us
  blocking collectives: 62.9 us -> 45.3 us
  waiting for transfers between devices: 29.7 us -> 41.5 us
  local copies, waits for them, and re-layouts: 17.4 us -> 9.54 us
  Pallas kernels: 22.2 us -> 19.2 us
    all_to_all x2, starting transfers between devices: 12.6 us -> 42.7 us  [sent(): return lax.all_to_all(exchange(scalars, returned, group), 'aux', 0, 0)]
    all_to_all x2, waiting for transfers between devices: 2.73 us -> 25.3 us  [sent(): return lax.all_to_all(exchange(scalars, returned, group), 'aux', 0, 0)]
    all_to_all x2 -> x1, blocking collectives: 50.2 us -> 32.6 us  [sent(): return lax.all_to_all(exchange(scalars, returned, group), 'aux', 0, 0)]
    ppermute x6 -> x7, waiting for transfers between devices: 22.7 us -> 11.9 us  [moved(): return lax.ppermute(tiles, 'occ', route)]
    unnamed x41 -> x31, local copies, waits for them, and re-layouts: 16.9 us -> 8.96 us
    ppermute x6 -> x7, starting transfers between devices: 13.9 us -> 19.1 us  [moved(): return lax.ppermute(tiles, 'occ', route)]
    pallas_call x2 -> x1, Pallas kernels: 2.4 us -> 0.01 us  [held(): pl.pallas_call(held_kernel, out_shape=[jax.ShapeDtypeStruct(array.shape,...]
    pallas_call x4 -> x3, Pallas kernels: 7.38 us -> 7.1 us  [exchange(): pl.pallas_call(functools.partial(exchange_kernel, back_shifts, parts_at,...]
  transfers between devices with their start and end apart: 10 -> 11, of which waited for: 7 -> 7; matrix products, arithmetic and copies ran while one was open for 0% -> 0% of each run, Pallas kernels for 9% -> 7%
where the time goes in v6:
time: 190 us; the launch traced here: 189 us
  starting transfers between devices  71.3 us (38%)
  blocking collectives  45.3 us (24%)
  waiting for transfers between devices  41.5 us (22%)
  Pallas kernels  19.2 us (10%)
  local copies, waits for them, and re-layouts  9.54 us (5%)
    all_to_all x2, starting transfers between devices, sent(): return lax.all_to_all(exchange(scalars, returned, group), 'aux', 0, 0)  42.7 us
    all_to_all x1, blocking collectives, sent(): return lax.all_to_all(exchange(scalars, returned, group), 'aux', 0, 0)  32.6 us
    all_to_all x2, waiting for transfers between devices, sent(): return lax.all_to_all(exchange(scalars, returned, group), 'aux', 0, 0)  25.3 us
    ppermute x7, starting transfers between devices, moved(): return lax.ppermute(tiles, 'occ', route)  19.1 us
    all_gather x1, blocking collectives, per_device(): all_pairs = lax.all_gather(tile_pairs[0, :, 0, :], 'occ').reshape(-1)  12.7 us
    ppermute x7, waiting for transfers between devices, moved(): return lax.ppermute(tiles, 'occ', route)  11.9 us
    ppermute x2, starting transfers between devices, per_device(): lax.ppermute(energy, 'vir', [(v, v ^ bit) for v in blocks])  9.52 us
    unnamed x31, local copies, waits for them, and re-layouts  8.96 us
  transfers between devices with their start and end apart: 11, of which 7 were waited for; matrix products, arithmetic and copies ran while one was open for 0% of the time, Pallas kernels for 7%

profile of v6, /device:TPU:6, one launch (start us, length us, event | category | flops | bytes accessed | tf_op | source)
XLA Modules:
  0.0 188.7 jit_solution(16994272301484454052)
XLA Ops:
  0.6 12.7 %all-gather = s32[8,8,1,2]{1,3,2,0:T(2,128)S(1)} all-gather(s32[1,8,1,2]{1,3,2,0:T(2,128)} %param.8), channel_id=2, replica_groups=mesh['occ'=8,'aux'=16,'vir'=4] {'occ'}, dimensions={0}, use_global_device_ids=true | all-gather | bytes 576 | tf_op jit(solution)/shard_map/all_gather | solution.py:289
  13.3 0.1 copy.16
  13.4 0.1 reshape.21.pairs_ref
  13.6 0.1 pad_add_fusion.ids_ref.refs_0_
  13.7 1.5 copy-done
  15.2 1.9 pick.2
  17.1 3.2 %collective-permute-start = (f32[1,640,256]{2,1,0:T(8,128)S(1)}, f32[1,640,256]{2,1,0:T(8,128)S(1)}, u32[]{:S(2)}, u32[]{:S(2)}) collective-permute-start(f32[1,640,256]{2,1,0:T(8,128)S(1)} %get-tuple-element.28), channel_id=1, source_target_pairs={{0,128},{64,192},{128,256},{192,320},{256,384},{320,448},{384,0},{... | collective-permute-start | bytes 1966088 | tf_op jit(solution)/shard_map/ppermute | solution.py:297
  20.3 2.6 %collective-permute-start.1 = (f32[1,640,256]{2,1,0:T(8,128)S(1)}, f32[1,640,256]{2,1,0:T(8,128)S(1)}, u32[]{:S(2)}, u32[]{:S(2)}) collective-permute-start(f32[1,640,256]{2,1,0:T(8,128)S(1)} %get-tuple-element.29), channel_id=1, source_target_pairs={{0,384},{64,448},{128,0},{192,64},{256,128},{320,192},{384,256},{4... | collective-permute-start | bytes 1966088 | tf_op jit(solution)/shard_map/ppermute | solution.py:297
  22.9 3.8 %collective-permute-start.2 = (f32[1,640,256]{2,1,0:T(8,128)}, f32[1,640,256]{2,1,0:T(8,128)}, u32[]{:S(2)}, u32[]{:S(2)}) collective-permute-start(f32[1,640,256]{2,1,0:T(8,128)} %get-tuple-element.32), channel_id=1, source_target_pairs={{0,192},{64,128},{128,320},{192,256},{256,448},{320,384},{384,64},... | collective-permute-start | bytes 1966088 | tf_op jit(solution)/shard_map/ppermute | solution.py:297
  26.7 1.9 %collective-permute-start.3 = (f32[1,640,256]{2,1,0:T(8,128)}, f32[1,640,256]{2,1,0:T(8,128)}, u32[]{:S(2)}, u32[]{:S(2)}) collective-permute-start(f32[1,640,256]{2,1,0:T(8,128)} %get-tuple-element.33), channel_id=1, source_target_pairs={{0,448},{64,384},{128,64},{192,0},{256,192},{320,128},{384,320},{4... | collective-permute-start | bytes 1966088 | tf_op jit(solution)/shard_map/ppermute | solution.py:297
  28.7 2.0 %pick.3 = (f32[1,640,256]{2,1,0:T(8,128)}, f32[1,640,256]{2,1,0:T(8,128)S(1)}, f32[1,640,256]{2,1,0:T(8,128)}, f32[1,640,256]{2,1,0:T(8,128)}) custom-call(s32[2]{0:T(128)S(1)} %pad_add_fusion.ids_ref.refs_0_, s32[128]{0:T(128)S(1)} %reshape.21.pairs_ref, f32[632,768]{1,0:T(8,128)S(1)} %bitcast.24), custom_call_target="tpu_custom_call" | custom-call | bytes 5242880 | tf_op jit(solution)/shard_map/pick/pallas_call | solution.py:60
  30.7 0.0 copy-start.8
  30.7 0.8 copy-done.8
  31.5 2.6 %collective-permute-start.4 = (f32[1,640,256]{2,1,0:T(8,128)}, f32[1,640,256]{2,1,0:T(8,128)}, u32[]{:S(2)}, u32[]{:S(2)}) collective-permute-start(f32[1,640,256]{2,1,0:T(8,128)} %get-tuple-element.34), channel_id=1, source_target_pairs={{0,64},{64,0},{128,192},{192,128},{256,320},{320,256},{384,448},{4... | collective-permute-start | bytes 1966088 | tf_op jit(solution)/shard_map/ppermute | solution.py:297
  34.2 2.3 %collective-permute-done.refs_5_ = f32[1,640,256]{2,1,0:T(8,128)S(1)} collective-permute-done((f32[1,640,256]{2,1,0:T(8,128)S(1)}, f32[1,640,256]{2,1,0:T(8,128)S(1)}, u32[]{:S(2)}, u32[]{:S(2)}) %collective-permute-start) | collective-permute-done | bytes 655392 | tf_op jit(solution)/shard_map/ppermute | solution.py:297
  36.5 4.5 %collective-permute-done.1.refs_6_ = f32[1,640,256]{2,1,0:T(8,128)S(1)} collective-permute-done((f32[1,640,256]{2,1,0:T(8,128)S(1)}, f32[1,640,256]{2,1,0:T(8,128)S(1)}, u32[]{:S(2)}, u32[]{:S(2)}) %collective-permute-start.1) | collective-permute-done | bytes 655392 | tf_op jit(solution)/shard_map/ppermute | solution.py:297
  41.0 2.0 %collective-permute-start.5 = (f32[1,640,256]{2,1,0:T(8,128)}, f32[1,640,256]{2,1,0:T(8,128)}, u32[]{:S(2)}, u32[]{:S(2)}) collective-permute-start(f32[1,640,256]{2,1,0:T(8,128)} %get-tuple-element.36), channel_id=1, source_target_pairs={{0,256},{64,320},{128,384},{192,448},{256,0},{320,64},{384,128},{4... | collective-permute-start | bytes 1966088 | tf_op jit(solution)/shard_map/ppermute | solution.py:297
  43.0 2.9 %collective-permute-start.6 = (f32[1,640,256]{2,1,0:T(8,128)}, f32[1,640,256]{2,1,0:T(8,128)}, u32[]{:S(2)}, u32[]{:S(2)}) collective-permute-start(f32[1,640,256]{2,1,0:T(8,128)} %get-tuple-element.37), channel_id=1, source_target_pairs={{0,320},{64,256},{128,448},{192,384},{256,64},{320,0},{384,192},{4... | collective-permute-start | bytes 1966088 | tf_op jit(solution)/shard_map/ppermute | solution.py:297
  46.0 0.0 copy-done.14
  46.0 0.1 copy.15
  46.0 1.5 copy-done.1
  47.6 0.6 left.1.refs_4_.refs_7_
  48.2 0.1 reshape.19.refs_1_
  48.3 1.2 collective-permute-done.2.refs_7_
  49.5 3.8 %collective-permute-done.3.refs_8_ = f32[1,640,256]{2,1,0:T(8,128)} collective-permute-done((f32[1,640,256]{2,1,0:T(8,128)}, f32[1,640,256]{2,1,0:T(8,128)}, u32[]{:S(2)}, u32[]{:S(2)}) %collective-permute-start.3) | collective-permute-done | bytes 655392 | tf_op jit(solution)/shard_map/ppermute | solution.py:297
  53.3 0.0 collective-permute-done.4.refs_9_
  53.3 0.0 copy-done.4
  53.3 0.0 copy-done.6
  53.3 0.0 copy-done.12
  53.3 0.0 copy-done.13
  53.3 0.0 copy-start.9
  53.3 1.1 copy-done.9
  54.4 3.8 %exchange.3 = f32[16,96,128]{2,1,0:T(8,128)} custom-call(s32[2]{0:T(128)S(1)} %pad_add_fusion.ids_ref.refs_0_, s32[16]{0:T(128)S(1)} %reshape.19.refs_1_, f32[8]{0:T(128)S(1)} %copy-done.12, s32[8]{0:T(128)S(1)} %bitcast.30, bf16[6,256,640]{2,1,0:T(8,128)(2,1)S(1)} %left.1.refs_4_.refs_7_, f32[1,640,256]{2,1,0:T(8,128)S(1)} %collective-permute-done.refs_5_, ...), custom_call_target="tpu_custom_call" | custom-call | flops 1006632960 | bytes 1572864 | tf_op jit(solution)/shard_map/exchange/pallas_call | solution.py:180
  58.2 36.8 %all-to-all-start = ((f32[16,96,128]{2,1,0:T(8,128)}), f32[16,96,128]{2,1,0:T(8,128)S(1)}, u32[]{:S(2)}, u32[]{:S(2)}) async-start(f32[16,96,128]{2,1,0:T(8,128)} %exchange.3), calls=%async_computation | async-start | bytes 1572864 | tf_op jit(solution)/shard_map/all_to_all | solution.py:300
  95.0 0.0 copy-start.11
  95.0 0.0 collective-permute-done.5.refs_0_
  95.0 0.0 collective-permute-done.6.refs_1_
  95.1 21.0 %all-to-all-done.refs_4_ = f32[16,96,128]{2,1,0:T(8,128)S(1)} async-done(((f32[16,96,128]{2,1,0:T(8,128)}), f32[16,96,128]{2,1,0:T(8,128)S(1)}, u32[]{:S(2)}, u32[]{:S(2)}) %all-to-all-start) | async-done | bytes 786464 | tf_op jit(solution)/shard_map/all_to_all | solution.py:300
  116.1 0.0 copy-done.11
  116.1 0.2 broadcast_in_dim.27.refs_5_.refs_4_
  116.3 2.0 %exchange.4 = f32[16,128,128]{2,1,0:T(8,128)S(1)} custom-call(s32[2]{0:T(128)S(1)} %pad_add_fusion.ids_ref.refs_0_, s32[16]{0:T(128)S(1)} %reshape.19.refs_1_, f32[8]{0:T(128)S(1)} %copy-done.12, s32[8]{0:T(128)S(1)} %bitcast.31, f32[16,96,128]{2,1,0:T(8,128)S(1)} %all-to-all-done.refs_4_, f32[768,128]{1,0:T(8,128)S(1)} %broadcast_in_dim.27.refs_5_.refs_4_, ...), custom_call_target="tpu_custom_call" | custom-call | flops 335544320 | bytes 2097152 | tf_op jit(solution)/shard_map/exchange/pallas_call | solution.py:180
  118.3 32.6 %all_to_all.15.refs_4_.refs_6_ = f32[16,128,128]{2,1,0:T(8,128)S(1)} all-to-all(f32[16,128,128]{2,1,0:T(8,128)S(1)} %exchange.4), channel_id=1, replica_groups=mesh['occ'=8,'aux'=16,'vir'=4] {'aux'}, dimensions={0} | all-to-all | bytes 2097152 | tf_op jit(solution)/shard_map/all_to_all | solution.py:300
  150.9 1.3 exchange.5
  152.2 5.9 %all-to-all-start.2 = ((f32[16,32,128]{2,1,0:T(8,128)}), f32[16,32,128]{2,1,0:T(8,128)S(1)}, u32[]{:S(2)}, u32[]{:S(2)}) async-start(f32[16,32,128]{2,1,0:T(8,128)} %exchange.5), calls=%async_computation.2 | async-start | bytes 524288 | tf_op jit(solution)/shard_map/all_to_all | solution.py:300
  158.1 0.1 stack.47
  158.2 0.7 energy.2
  159.0 0.0 copy-done.5
  159.0 0.0 copy-done.7
  159.0 0.0 copy-start.10
  159.0 1.1 copy-done.10
  160.1 3.0 %gamma.2.refs_4_ = f32[632,768]{1,0:T(8,128)S(1)} custom-call(s32[2]{0:T(128)S(1)} %pad_add_fusion.ids_ref.refs_0_, s32[16]{0:T(128)S(1)} %reshape.19.refs_1_, f32[8]{0:T(128)S(1)} %copy-done.12, s32[8]{0:T(128)S(1)} %bitcast.34, f32[16,128,128]{2,1,0:T(8,128)S(1)} %all_to_all.15.refs_4_.refs_6_, f32[1,640,256]{2,1,0:T(8,128)S(1)} %copy-done.5, ...), custom_call_target="tpu_custom_call" | custom-call | flops 994050048 | bytes 3883008 | tf_op jit(solution)/shard_map/gamma/pallas_call | solution.py:267
  163.1 0.0 copy-start.2
  163.1 1.3 copy-done.2
  164.4 4.3 %all-to-all-done.2.refs_5_.refs_6_ = f32[16,32,128]{2,1,0:T(8,128)S(1)} async-done(((f32[16,32,128]{2,1,0:T(8,128)}), f32[16,32,128]{2,1,0:T(8,128)S(1)}, u32[]{:S(2)}, u32[]{:S(2)}) %all-to-all-start.2) | async-done | bytes 262176 | tf_op jit(solution)/shard_map/all_to_all | solution.py:300
  168.7 0.6 energy.3
  169.3 0.1 maximum_reduce_fusion
  169.4 4.5 %collective-permute-start.7 = (f32[8]{0:T(128)S(1)}, f32[8]{0:T(128)S(1)}, u32[]{:S(2)}, u32[]{:S(2)}) collective-permute-start(f32[8]{0:T(128)S(1)} %maximum_reduce_fusion), channel_id=1, source_target_pairs={{0,1},{1,0},{2,3},{3,2},{4,5},{5,4},{6,7},{7,6},{8,9},{9,8},{10,11... | collective-permute-start | bytes 104 | tf_op jit(solution)/shard_map/ppermute | solution.py:324
  173.9 0.0 copy-start.3
  173.9 1.5 copy-done.3
  175.5 3.3 %gamma.3 = f32[632,768]{1,0:T(8,128)} custom-call(s32[2]{0:T(128)S(1)} %pad_add_fusion.ids_ref.refs_0_, s32[16]{0:T(128)S(1)} %reshape.19.refs_1_, f32[8]{0:T(128)S(1)} %copy-done.12, s32[8]{0:T(128)S(1)} %bitcast.36, f32[632,768]{1,0:T(8,128)S(1)} %copy-done.3, f32[16,32,128]{2,1,0:T(8,128)S(1)} %all-to-all-done.2.refs_5_.refs_6_, ...), custom_call_target="tpu_custom_call" | custom-call | flops 331350016 | bytes 3883008 | tf_op jit(solution)/shard_map/gamma/pallas_call | solution.py:267
  178.7 0.0 collective-permute-done.7
  178.7 5.0 %collective-permute-start.8 = (f32[8]{0:T(128)S(1)}, f32[8]{0:T(128)S(1)}, u32[]{:S(2)}, u32[]{:S(2)}) collective-permute-start(f32[8]{0:T(128)S(1)} %add.84), channel_id=1, source_target_pairs={{0,2},{1,3},{2,0},{3,1},{4,6},{5,7},{6,4},{7,5},{8,10},{9,11},{10,... | collective-permute-start | bytes 104 | tf_op jit(solution)/shard_map/ppermute | solution.py:324
  183.8 4.3 %collective-permute-done.8 = f32[8]{0:T(128)S(1)} collective-permute-done((f32[8]{0:T(128)S(1)}, f32[8]{0:T(128)S(1)}, u32[]{:S(2)}, u32[]{:S(2)}) %collective-permute-start.8) | collective-permute-done | bytes 64 | tf_op jit(solution)/shard_map/ppermute | solution.py:324
  188.1 0.6 select_reduce_fusion
  (12 shorter events, 0.0 us)
Async XLA Ops:
  13.7 1.5 copy-start
  15.2 30.8 %copy-start.14 = (s32[1,8,1,2]{1,3,2,0:T(2,128)S(1)}, s32[1,8,1,2]{1,3,2,0:T(2,128)}, u32[]{:S(2)}) copy-start(s32[1,8,1,2]{1,3,2,0:T(2,128)} %param.8) | copy-start | bytes 196
  17.1 19.4 %collective-permute-start = (f32[1,640,256]{2,1,0:T(8,128)S(1)}, f32[1,640,256]{2,1,0:T(8,128)S(1)}, u32[]{:S(2)}, u32[]{:S(2)}) collective-permute-start(f32[1,640,256]{2,1,0:T(8,128)S(1)} %get-tuple-element.28), channel_id=1, source_target_pairs={{0,128},{64,192},{128,256},{192,320},{256,384},{320,448},{384,0},{... | collective-permute-start | bytes 1966088 | tf_op jit(solution)/shard_map/ppermute | solution.py:297
  20.3 20.7 %collective-permute-start.1 = (f32[1,640,256]{2,1,0:T(8,128)S(1)}, f32[1,640,256]{2,1,0:T(8,128)S(1)}, u32[]{:S(2)}, u32[]{:S(2)}) collective-permute-start(f32[1,640,256]{2,1,0:T(8,128)S(1)} %get-tuple-element.29), channel_id=1, source_target_pairs={{0,384},{64,448},{128,0},{192,64},{256,128},{320,192},{384,256},{4... | collective-permute-start | bytes 1966088 | tf_op jit(solution)/shard_map/ppermute | solution.py:297
  22.9 26.5 %collective-permute-start.2 = (f32[1,640,256]{2,1,0:T(8,128)}, f32[1,640,256]{2,1,0:T(8,128)}, u32[]{:S(2)}, u32[]{:S(2)}) collective-permute-start(f32[1,640,256]{2,1,0:T(8,128)} %get-tuple-element.32), channel_id=1, source_target_pairs={{0,192},{64,128},{128,320},{192,256},{256,448},{320,384},{384,64},... | collective-permute-start | bytes 1966088 | tf_op jit(solution)/shard_map/ppermute | solution.py:297
  26.7 26.6 %collective-permute-start.3 = (f32[1,640,256]{2,1,0:T(8,128)}, f32[1,640,256]{2,1,0:T(8,128)}, u32[]{:S(2)}, u32[]{:S(2)}) collective-permute-start(f32[1,640,256]{2,1,0:T(8,128)} %get-tuple-element.33), channel_id=1, source_target_pairs={{0,448},{64,384},{128,64},{192,0},{256,192},{320,128},{384,320},{4... | collective-permute-start | bytes 1966088 | tf_op jit(solution)/shard_map/ppermute | solution.py:297
  30.7 0.8 copy-start.8
  31.5 21.8 %collective-permute-start.4 = (f32[1,640,256]{2,1,0:T(8,128)}, f32[1,640,256]{2,1,0:T(8,128)}, u32[]{:S(2)}, u32[]{:S(2)}) collective-permute-start(f32[1,640,256]{2,1,0:T(8,128)} %get-tuple-element.34), channel_id=1, source_target_pairs={{0,64},{64,0},{128,192},{192,128},{256,320},{320,256},{384,448},{4... | collective-permute-start | bytes 1966088 | tf_op jit(solution)/shard_map/ppermute | solution.py:297
  36.5 16.8 %copy-start.4 = (f32[1,640,256]{2,1,0:T(8,128)}, f32[1,640,256]{2,1,0:T(8,128)S(1)}, u32[]{:S(2)}) copy-start(f32[1,640,256]{2,1,0:T(8,128)S(1)} %collective-permute-done.refs_5_) | copy-start | bytes 1966084
  41.0 12.3 %copy-start.6 = (f32[1,640,256]{2,1,0:T(8,128)}, f32[1,640,256]{2,1,0:T(8,128)S(1)}, u32[]{:S(2)}) copy-start(f32[1,640,256]{2,1,0:T(8,128)S(1)} %collective-permute-done.1.refs_6_) | copy-start | bytes 1966084
  41.0 54.0 %collective-permute-start.5 = (f32[1,640,256]{2,1,0:T(8,128)}, f32[1,640,256]{2,1,0:T(8,128)}, u32[]{:S(2)}, u32[]{:S(2)}) collective-permute-start(f32[1,640,256]{2,1,0:T(8,128)} %get-tuple-element.36), channel_id=1, source_target_pairs={{0,256},{64,320},{128,384},{192,448},{256,0},{320,64},{384,128},{4... | collective-permute-start | bytes 1966088 | tf_op jit(solution)/shard_map/ppermute | solution.py:297
  43.0 52.0 %collective-permute-start.6 = (f32[1,640,256]{2,1,0:T(8,128)}, f32[1,640,256]{2,1,0:T(8,128)}, u32[]{:S(2)}, u32[]{:S(2)}) collective-permute-start(f32[1,640,256]{2,1,0:T(8,128)} %get-tuple-element.37), channel_id=1, source_target_pairs={{0,320},{64,256},{128,448},{192,384},{256,64},{320,0},{384,192},{4... | collective-permute-start | bytes 1966088 | tf_op jit(solution)/shard_map/ppermute | solution.py:297
  46.0 1.5 copy-start.1
  47.6 5.7 %copy-start.12 = (f32[8]{0:T(128)S(1)}, f32[8]{0:T(128)}, u32[]{:S(2)}) copy-start(f32[8]{0:T(128)} %refs_2_.13) | copy-start | bytes 100
  47.6 5.7 %copy-start.13 = (s32[1,8]{1,0:T(1,128)S(1)}, s32[1,8]{1,0:T(1,128)}, u32[]{:S(2)}) copy-start(s32[1,8]{1,0:T(1,128)} %param.9) | copy-start | bytes 100
  53.3 1.1 copy-start.9
  58.2 57.9 %all-to-all-start = ((f32[16,96,128]{2,1,0:T(8,128)}), f32[16,96,128]{2,1,0:T(8,128)S(1)}, u32[]{:S(2)}, u32[]{:S(2)}) async-start(f32[16,96,128]{2,1,0:T(8,128)} %exchange.3), calls=%async_computation | async-start | bytes 1572864 | tf_op jit(solution)/shard_map/all_to_all | solution.py:300
  95.0 21.1 %copy-start.11 = (f32[768]{0:T(1024)S(1)}, f32[768]{0:T(1024)}, u32[]{:S(2)}) copy-start(f32[768]{0:T(1024)} %param.7) | copy-start | bytes 9220
  150.9 8.1 %copy-start.5 = (f32[1,640,256]{2,1,0:T(8,128)S(1)}, f32[1,640,256]{2,1,0:T(8,128)}, u32[]{:S(2)}) copy-start(f32[1,640,256]{2,1,0:T(8,128)} %copy-done.4) | copy-start | bytes 1966084
  150.9 8.1 %copy-start.7 = (f32[1,640,256]{2,1,0:T(8,128)S(1)}, f32[1,640,256]{2,1,0:T(8,128)}, u32[]{:S(2)}) copy-start(f32[1,640,256]{2,1,0:T(8,128)} %copy-done.6) | copy-start | bytes 1966084
  152.2 16.5 %all-to-all-start.2 = ((f32[16,32,128]{2,1,0:T(8,128)}), f32[16,32,128]{2,1,0:T(8,128)S(1)}, u32[]{:S(2)}, u32[]{:S(2)}) async-start(f32[16,32,128]{2,1,0:T(8,128)} %exchange.5), calls=%async_computation.2 | async-start | bytes 524288 | tf_op jit(solution)/shard_map/all_to_all | solution.py:300
  159.0 1.1 copy-start.10
  163.1 1.3 copy-start.2
  169.4 9.3 %collective-permute-start.7 = (f32[8]{0:T(128)S(1)}, f32[8]{0:T(128)S(1)}, u32[]{:S(2)}, u32[]{:S(2)}) collective-permute-start(f32[8]{0:T(128)S(1)} %maximum_reduce_fusion), channel_id=1, source_target_pairs={{0,1},{1,0},{2,3},{3,2},{4,5},{5,4},{6,7},{7,6},{8,9},{9,8},{10,11... | collective-permute-start | bytes 104 | tf_op jit(solution)/shard_map/ppermute | solution.py:324
  173.9 1.5 copy-start.3
  178.7 9.3 %collective-permute-start.8 = (f32[8]{0:T(128)S(1)}, f32[8]{0:T(128)S(1)}, u32[]{:S(2)}, u32[]{:S(2)}) collective-permute-start(f32[8]{0:T(128)S(1)} %add.84), channel_id=1, source_target_pairs={{0,2},{1,3},{2,0},{3,1},{4,6},{5,7},{6,4},{7,5},{8,10},{9,11},{10,... | collective-permute-start | bytes 104 | tf_op jit(solution)/shard_map/ppermute | solution.py:324

commit v7 on v6

--- a/solution.py
+++ b/solution.py
@@ -305,7 +305,7 @@
     mate, own, *far = pick(later_ids, all_pairs, block, NEAR[4:] + FAR, (1,) * 4, padded)
     mate = moved(mate, 0, 1)
     left_split = left(block, padded)
-    *far, near[0], near[1] = lax.optimization_barrier((*far, near[0], near[1]))
+    far[0], far[1], left_split, *near = lax.optimization_barrier((*far, left_split, *near))
     far = held(*[moved(tiles, *shift) for tiles, shift in zip(far, FAR)])
     near_rights = [(tiles, 0) for tiles in (*near, mate, own)]
     far_rights = [(tiles, 0) for tiles in far]
@@ -316,12 +316,11 @@
     first_groups = [(NEAR, both, near_rights)]
     total = gamma_add(scalars, first_groups, rows, cols, None)
     first_energy = energy_of(scalars, columns, levels, first_groups)
+    last, total, first_energy = lax.optimization_barrier((last, total, first_energy))
     last_energy = energy_of(scalars, columns, levels, [(FAR, last)])
 
     energy = jnp.sum(jnp.concatenate([first_energy, last_energy], axis=0), axis=1)
-    for bit in (1, 2):
-        blocks = range(lax.axis_size("vir"))
-        energy = energy + lax.ppermute(energy, "vir", [(v, v ^ bit) for v in blocks])
+    energy, last = lax.optimization_barrier((lax.psum(energy, "vir"), last))
     order = jnp.stack([(me // 2 - dx) % CHIPS * 2 + (me + dc) % 2 for dx, dc in NEAR + FAR])
     mine = order[:, None] == jnp.arange(occ_size)[None, :]
     energy = jnp.sum(jnp.where(mine, energy[:, None], 0.0), axis=0)

time: 190 us -> 168 us (0.88)
  starting transfers between devices: 71.3 us -> 36.3 us
  blocking collectives: 45.3 us -> 55.9 us
  local copies, waits for them, and re-layouts: 9.54 us -> 13.2 us
    all_to_all x2, starting transfers between devices: 42.7 us -> 14.5 us  [sent(): return lax.all_to_all(exchange(scalars, returned, group), 'aux', 0, 0)]
    ppermute x7, waiting for transfers between devices: 11.9 us -> 30.2 us  [moved(): return lax.ppermute(tiles, 'occ', route)]
    all_to_all x2, waiting for transfers between devices: 25.3 us -> 12.1 us  [sent(): return lax.all_to_all(exchange(scalars, returned, group), 'aux', 0, 0)]
    psum x0 -> x1, blocking collectives: none -> 12 us  [per_device(): energy, last = lax.optimization_barrier((lax.psum(energy, 'vir'), last))]
    ppermute x2 -> x0, starting transfers between devices: 9.52 us -> none  [per_device(): lax.ppermute(energy, 'vir', [(v, v ^ bit) for v in blocks])]
    ppermute x2 -> x0, waiting for transfers between devices: 4.31 us -> none  [per_device(): lax.ppermute(energy, 'vir', [(v, v ^ bit) for v in blocks])]
    unnamed x31 -> x41, local copies, waits for them, and re-layouts: 8.96 us -> 12.7 us
    ppermute x7, starting transfers between devices: 19.1 us -> 21.7 us  [moved(): return lax.ppermute(tiles, 'occ', route)]
  transfers between devices with their start and end apart: 11 -> 9, of which waited for: 7 -> 7; matrix products, arithmetic and copies ran while one was open for 0% -> 0% of each run, Pallas kernels for 7% -> 6%
where the time goes in v7:
time: 168 us; the launch traced here: 167 us
  blocking collectives  55.9 us (33%)
  waiting for transfers between devices  42.3 us (25%)
  starting transfers between devices  36.3 us (22%)
  Pallas kernels  17.5 us (10%)
  local copies, waits for them, and re-layouts  13.2 us (8%)
    all_to_all x1, blocking collectives, sent(): return lax.all_to_all(exchange(scalars, returned, group), 'aux', 0, 0)  31.3 us
    ppermute x7, waiting for transfers between devices, moved(): return lax.ppermute(tiles, 'occ', route)  30.2 us
    ppermute x7, starting transfers between devices, moved(): return lax.ppermute(tiles, 'occ', route)  21.7 us
    all_to_all x2, starting transfers between devices, sent(): return lax.all_to_all(exchange(scalars, returned, group), 'aux', 0, 0)  14.5 us
    all_gather x1, blocking collectives, per_device(): all_pairs = lax.all_gather(tile_pairs[0, :, 0, :], 'occ').reshape(-1)  12.7 us
    unnamed x41, local copies, waits for them, and re-layouts  12.7 us
    all_to_all x2, waiting for transfers between devices, sent(): return lax.all_to_all(exchange(scalars, returned, group), 'aux', 0, 0)  12.1 us
    psum x1, blocking collectives, per_device(): energy, last = lax.optimization_barrier((lax.psum(energy, 'vir'), last))  12 us
  transfers between devices with their start and end apart: 9, of which 7 were waited for; matrix products, arithmetic and copies ran while one was open for 0% of the time, Pallas kernels for 6%

profile of v7, /device:TPU:6, one launch (start us, length us, event | category | flops | bytes accessed | tf_op | source)
XLA Modules:
  0.0 167.0 jit_solution(8622188068295294747)
XLA Ops:
  0.6 12.7 %all-gather = s32[8,8,1,2]{1,3,2,0:T(2,128)S(1)} all-gather(s32[1,8,1,2]{1,3,2,0:T(2,128)} %param.8), channel_id=2, replica_groups=mesh['occ'=8,'aux'=16,'vir'=4] {'occ'}, dimensions={0}, use_global_device_ids=true | all-gather | bytes 576 | tf_op jit(solution)/shard_map/all_gather | solution.py:289
  13.3 0.1 copy.16
  13.4 0.1 reshape.21.pairs_ref
  13.6 0.1 pad_add_fusion.ids_ref.refs_0_
  13.7 1.5 copy-done
  15.2 0.9 pick.2
  16.2 3.2 %collective-permute-start = (f32[1,640,256]{2,1,0:T(8,128)S(1)}, f32[1,640,256]{2,1,0:T(8,128)S(1)}, u32[]{:S(2)}, u32[]{:S(2)}) collective-permute-start(f32[1,640,256]{2,1,0:T(8,128)S(1)} %get-tuple-element.36), channel_id=1, source_target_pairs={{0,128},{64,192},{128,256},{192,320},{256,384},{320,448},{384,0},{... | collective-permute-start | bytes 1966088 | tf_op jit(solution)/shard_map/ppermute | solution.py:297
  19.4 2.6 %collective-permute-start.1 = (f32[1,640,256]{2,1,0:T(8,128)S(1)}, f32[1,640,256]{2,1,0:T(8,128)S(1)}, u32[]{:S(2)}, u32[]{:S(2)}) collective-permute-start(f32[1,640,256]{2,1,0:T(8,128)S(1)} %get-tuple-element.37), channel_id=1, source_target_pairs={{0,384},{64,448},{128,0},{192,64},{256,128},{320,192},{384,256},{4... | collective-permute-start | bytes 1966088 | tf_op jit(solution)/shard_map/ppermute | solution.py:297
  22.0 3.8 %collective-permute-start.2 = (f32[1,640,256]{2,1,0:T(8,128)S(1)}, f32[1,640,256]{2,1,0:T(8,128)S(1)}, u32[]{:S(2)}, u32[]{:S(2)}) collective-permute-start(f32[1,640,256]{2,1,0:T(8,128)S(1)} %get-tuple-element.38), channel_id=1, source_target_pairs={{0,192},{64,128},{128,320},{192,256},{256,448},{320,384},{384,64},... | collective-permute-start | bytes 1966088 | tf_op jit(solution)/shard_map/ppermute | solution.py:297
  25.8 1.9 %collective-permute-start.3 = (f32[1,640,256]{2,1,0:T(8,128)S(1)}, f32[1,640,256]{2,1,0:T(8,128)S(1)}, u32[]{:S(2)}, u32[]{:S(2)}) collective-permute-start(f32[1,640,256]{2,1,0:T(8,128)S(1)} %get-tuple-element.39), channel_id=1, source_target_pairs={{0,448},{64,384},{128,64},{192,0},{256,192},{320,128},{384,320},{4... | collective-permute-start | bytes 1966088 | tf_op jit(solution)/shard_map/ppermute | solution.py:297
  27.7 2.0 %pick.3 = (f32[1,640,256]{2,1,0:T(8,128)}, f32[1,640,256]{2,1,0:T(8,128)S(1)}, f32[1,640,256]{2,1,0:T(8,128)}, f32[1,640,256]{2,1,0:T(8,128)}) custom-call(s32[2]{0:T(128)S(1)} %pad_add_fusion.ids_ref.refs_0_, s32[128]{0:T(128)S(1)} %reshape.21.pairs_ref, f32[632,768]{1,0:T(8,128)S(1)} %bitcast.24), custom_call_target="tpu_custom_call" | custom-call | bytes 5242880 | tf_op jit(solution)/shard_map/pick/pallas_call | solution.py:60
  29.7 0.0 copy-start.13
  29.7 0.0 copy-start.19
  29.7 0.0 copy-start.17
  29.7 0.0 copy-start.18
  29.7 2.8 %collective-permute-start.4 = (f32[1,640,256]{2,1,0:T(8,128)}, f32[1,640,256]{2,1,0:T(8,128)}, u32[]{:S(2)}, u32[]{:S(2)}) collective-permute-start(f32[1,640,256]{2,1,0:T(8,128)} %get-tuple-element.45), channel_id=1, source_target_pairs={{0,64},{64,0},{128,192},{192,128},{256,320},{320,256},{384,448},{4... | collective-permute-start | bytes 1966088 | tf_op jit(solution)/shard_map/ppermute | solution.py:297
  32.5 0.6 left.1.refs_4_.refs_7_
  33.1 0.0 copy-done.13
  33.1 2.5 %collective-permute-done.refs_5_ = f32[1,640,256]{2,1,0:T(8,128)S(1)} collective-permute-done((f32[1,640,256]{2,1,0:T(8,128)S(1)}, f32[1,640,256]{2,1,0:T(8,128)S(1)}, u32[]{:S(2)}, u32[]{:S(2)}) %collective-permute-start) | collective-permute-done | bytes 655392 | tf_op jit(solution)/shard_map/ppermute | solution.py:297
  35.6 4.5 %collective-permute-done.1.refs_6_ = f32[1,640,256]{2,1,0:T(8,128)S(1)} collective-permute-done((f32[1,640,256]{2,1,0:T(8,128)S(1)}, f32[1,640,256]{2,1,0:T(8,128)S(1)}, u32[]{:S(2)}, u32[]{:S(2)}) %collective-permute-start.1) | collective-permute-done | bytes 655392 | tf_op jit(solution)/shard_map/ppermute | solution.py:297
  40.1 8.4 %collective-permute-done.2.refs_7_ = f32[1,640,256]{2,1,0:T(8,128)S(1)} collective-permute-done((f32[1,640,256]{2,1,0:T(8,128)S(1)}, f32[1,640,256]{2,1,0:T(8,128)S(1)}, u32[]{:S(2)}, u32[]{:S(2)}) %collective-permute-start.2) | collective-permute-done | bytes 655392 | tf_op jit(solution)/shard_map/ppermute | solution.py:297
  48.4 0.9 copy-done.7
  49.3 3.0 %collective-permute-done.3.refs_8_ = f32[1,640,256]{2,1,0:T(8,128)S(1)} collective-permute-done((f32[1,640,256]{2,1,0:T(8,128)S(1)}, f32[1,640,256]{2,1,0:T(8,128)S(1)}, u32[]{:S(2)}, u32[]{:S(2)}) %collective-permute-start.3) | collective-permute-done | bytes 655392 | tf_op jit(solution)/shard_map/ppermute | solution.py:297
  52.3 0.8 copy-done.10
  53.1 2.6 %collective-permute-start.5 = (f32[1,640,256]{2,1,0:T(8,128)}, f32[1,640,256]{2,1,0:T(8,128)}, u32[]{:S(2)}, u32[]{:S(2)}) collective-permute-start(f32[1,640,256]{2,1,0:T(8,128)} %get-tuple-element.47), channel_id=1, source_target_pairs={{0,256},{64,320},{128,384},{192,448},{256,0},{320,64},{384,128},{4... | collective-permute-start | bytes 1966088 | tf_op jit(solution)/shard_map/ppermute | solution.py:297
  55.8 4.8 %collective-permute-start.6 = (f32[1,640,256]{2,1,0:T(8,128)}, f32[1,640,256]{2,1,0:T(8,128)}, u32[]{:S(2)}, u32[]{:S(2)}) collective-permute-start(f32[1,640,256]{2,1,0:T(8,128)} %get-tuple-element.48), channel_id=1, source_target_pairs={{0,320},{64,256},{128,448},{192,384},{256,64},{320,0},{384,192},{4... | collective-permute-start | bytes 1966088 | tf_op jit(solution)/shard_map/ppermute | solution.py:297
  60.5 0.0 copy-done.19
  60.5 0.1 copy.15
  60.6 0.1 reshape.19.refs_1_
  60.7 0.0 collective-permute-done.4.refs_9_
  60.7 0.0 copy-done.17
  60.7 0.0 copy-done.18
  60.7 1.1 copy-done.8
  61.8 1.1 copy-done.11
  62.9 1.1 copy-done.14
  64.0 3.4 %exchange.3 = f32[16,96,128]{2,1,0:T(8,128)} custom-call(s32[2]{0:T(128)S(1)} %pad_add_fusion.ids_ref.refs_0_, s32[16]{0:T(128)S(1)} %reshape.19.refs_1_, f32[8]{0:T(128)S(1)} %copy-done.17, s32[8]{0:T(128)S(1)} %bitcast.30, bf16[6,256,640]{2,1,0:T(8,128)(2,1)S(1)} %left.1.refs_4_.refs_7_, f32[1,640,256]{2,1,0:T(8,128)S(1)} %collective-permute-done.refs_5_, ...), custom_call_target="tpu_custom_call" | custom-call | flops 1006632960 | bytes 1572864 | tf_op jit(solution)/shard_map/exchange/pallas_call | solution.py:180
  67.4 8.7 %all-to-all-start = ((f32[16,96,128]{2,1,0:T(8,128)}), f32[16,96,128]{2,1,0:T(8,128)S(1)}, u32[]{:S(2)}, u32[]{:S(2)}) async-start(f32[16,96,128]{2,1,0:T(8,128)} %exchange.3), calls=%async_computation | async-start | bytes 1572864 | tf_op jit(solution)/shard_map/all_to_all | solution.py:300
  76.1 0.0 copy-start.16
  76.1 0.0 collective-permute-done.5.refs_0_
  76.1 11.9 %collective-permute-done.6.refs_1_ = f32[1,640,256]{2,1,0:T(8,128)} collective-permute-done((f32[1,640,256]{2,1,0:T(8,128)}, f32[1,640,256]{2,1,0:T(8,128)}, u32[]{:S(2)}, u32[]{:S(2)}) %collective-permute-start.6) | collective-permute-done | bytes 655392 | tf_op jit(solution)/shard_map/ppermute | solution.py:297
  88.0 9.5 %all-to-all-done.refs_4_ = f32[16,96,128]{2,1,0:T(8,128)S(1)} async-done(((f32[16,96,128]{2,1,0:T(8,128)}), f32[16,96,128]{2,1,0:T(8,128)S(1)}, u32[]{:S(2)}, u32[]{:S(2)}) %all-to-all-start) | async-done | bytes 786464 | tf_op jit(solution)/shard_map/all_to_all | solution.py:300
  97.5 0.0 copy-done.16
  97.5 0.2 broadcast_in_dim.27.refs_5_.refs_4_
  97.6 2.0 %exchange.4 = f32[16,128,128]{2,1,0:T(8,128)S(1)} custom-call(s32[2]{0:T(128)S(1)} %pad_add_fusion.ids_ref.refs_0_, s32[16]{0:T(128)S(1)} %reshape.19.refs_1_, f32[8]{0:T(128)S(1)} %copy-done.17, s32[8]{0:T(128)S(1)} %bitcast.31, f32[16,96,128]{2,1,0:T(8,128)S(1)} %all-to-all-done.refs_4_, f32[768,128]{1,0:T(8,128)S(1)} %broadcast_in_dim.27.refs_5_.refs_4_, ...), custom_call_target="tpu_custom_call" | custom-call | flops 335544320 | bytes 2097152 | tf_op jit(solution)/shard_map/exchange/pallas_call | solution.py:180
  99.6 31.3 %all_to_all.15.refs_4_.refs_6_ = f32[16,128,128]{2,1,0:T(8,128)S(1)} all-to-all(f32[16,128,128]{2,1,0:T(8,128)S(1)} %exchange.4), channel_id=1, replica_groups=mesh['occ'=8,'aux'=16,'vir'=4] {'aux'}, dimensions={0} | all-to-all | bytes 2097152 | tf_op jit(solution)/shard_map/all_to_all | solution.py:300
  130.9 1.3 exchange.5
  132.2 5.8 %all-to-all-start.2 = ((f32[16,32,128]{2,1,0:T(8,128)}), f32[16,32,128]{2,1,0:T(8,128)S(1)}, u32[]{:S(2)}, u32[]{:S(2)}) async-start(f32[16,32,128]{2,1,0:T(8,128)} %exchange.5), calls=%async_computation.2 | async-start | bytes 524288 | tf_op jit(solution)/shard_map/all_to_all | solution.py:300
  138.1 0.7 energy.2
  138.9 0.0 copy-done.6
  138.9 0.0 copy-start.9
  138.9 1.1 copy-done.9
  140.0 1.1 copy-done.12
  141.1 1.1 copy-done.15
  142.2 2.7 %gamma.2.refs_4_ = f32[632,768]{1,0:T(8,128)S(1)} custom-call(s32[2]{0:T(128)S(1)} %pad_add_fusion.ids_ref.refs_0_, s32[16]{0:T(128)S(1)} %reshape.19.refs_1_, f32[8]{0:T(128)S(1)} %copy-done.17, s32[8]{0:T(128)S(1)} %bitcast.34, f32[16,128,128]{2,1,0:T(8,128)S(1)} %all_to_all.15.refs_4_.refs_6_, f32[1,640,256]{2,1,0:T(8,128)S(1)} %copy-done.4, ...), custom_call_target="tpu_custom_call" | custom-call | flops 994050048 | bytes 3883008 | tf_op jit(solution)/shard_map/gamma/pallas_call | solution.py:267
  144.8 0.0 copy-start.1
  144.8 1.3 copy-done.1
  146.1 2.7 %all-to-all-done.2.refs_6_.refs_5_ = f32[16,32,128]{2,1,0:T(8,128)S(1)} async-done(((f32[16,32,128]{2,1,0:T(8,128)}), f32[16,32,128]{2,1,0:T(8,128)S(1)}, u32[]{:S(2)}, u32[]{:S(2)}) %all-to-all-start.2) | async-done | bytes 262176 | tf_op jit(solution)/shard_map/all_to_all | solution.py:300
  148.8 0.6 energy.3
  149.4 0.1 maximum_reduce_fusion
  149.5 0.1 stack.47
  149.6 12.0 %psum.7 = f32[8]{0:T(128)S(1)} all-reduce(f32[8]{0:T(128)S(1)} %maximum_reduce_fusion), channel_id=1, replica_groups=mesh['occ'=8,'aux'=16,'vir'=4] {'vir'}, use_global_device_ids=true, to_apply=%region_1.0 | all-reduce | flops 8 | bytes 64 | tf_op jit(solution)/shard_map/psum | solution.py:323
  161.6 1.5 copy-done.2
  163.1 3.3 %gamma.3 = f32[632,768]{1,0:T(8,128)} custom-call(s32[2]{0:T(128)S(1)} %pad_add_fusion.ids_ref.refs_0_, s32[16]{0:T(128)S(1)} %reshape.19.refs_1_, f32[8]{0:T(128)S(1)} %copy-done.17, s32[8]{0:T(128)S(1)} %bitcast.36, f32[632,768]{1,0:T(8,128)S(1)} %copy-done.2, f32[16,32,128]{2,1,0:T(8,128)S(1)} %all-to-all-done.2.refs_6_.refs_5_, ...), custom_call_target="tpu_custom_call" | custom-call | flops 331350016 | bytes 3883008 | tf_op jit(solution)/shard_map/gamma/pallas_call | solution.py:267
  166.4 0.6 select_reduce_fusion
  (17 shorter events, 0.0 us)
Async XLA Ops:
  13.7 1.5 copy-start
  16.2 19.4 %collective-permute-start = (f32[1,640,256]{2,1,0:T(8,128)S(1)}, f32[1,640,256]{2,1,0:T(8,128)S(1)}, u32[]{:S(2)}, u32[]{:S(2)}) collective-permute-start(f32[1,640,256]{2,1,0:T(8,128)S(1)} %get-tuple-element.36), channel_id=1, source_target_pairs={{0,128},{64,192},{128,256},{192,320},{256,384},{320,448},{384,0},{... | collective-permute-start | bytes 1966088 | tf_op jit(solution)/shard_map/ppermute | solution.py:297
  19.4 20.7 %collective-permute-start.1 = (f32[1,640,256]{2,1,0:T(8,128)S(1)}, f32[1,640,256]{2,1,0:T(8,128)S(1)}, u32[]{:S(2)}, u32[]{:S(2)}) collective-permute-start(f32[1,640,256]{2,1,0:T(8,128)S(1)} %get-tuple-element.37), channel_id=1, source_target_pairs={{0,384},{64,448},{128,0},{192,64},{256,128},{320,192},{384,256},{4... | collective-permute-start | bytes 1966088 | tf_op jit(solution)/shard_map/ppermute | solution.py:297
  22.0 26.4 %collective-permute-start.2 = (f32[1,640,256]{2,1,0:T(8,128)S(1)}, f32[1,640,256]{2,1,0:T(8,128)S(1)}, u32[]{:S(2)}, u32[]{:S(2)}) collective-permute-start(f32[1,640,256]{2,1,0:T(8,128)S(1)} %get-tuple-element.38), channel_id=1, source_target_pairs={{0,192},{64,128},{128,320},{192,256},{256,448},{320,384},{384,64},... | collective-permute-start | bytes 1966088 | tf_op jit(solution)/shard_map/ppermute | solution.py:297
  25.8 26.5 %collective-permute-start.3 = (f32[1,640,256]{2,1,0:T(8,128)S(1)}, f32[1,640,256]{2,1,0:T(8,128)S(1)}, u32[]{:S(2)}, u32[]{:S(2)}) collective-permute-start(f32[1,640,256]{2,1,0:T(8,128)S(1)} %get-tuple-element.39), channel_id=1, source_target_pairs={{0,448},{64,384},{128,64},{192,0},{256,192},{320,128},{384,320},{4... | collective-permute-start | bytes 1966088 | tf_op jit(solution)/shard_map/ppermute | solution.py:297
  29.7 3.4 %copy-start.13 = (f32[1,640,256]{2,1,0:T(8,128)}, f32[1,640,256]{2,1,0:T(8,128)S(1)}, u32[]{:S(2)}) copy-start(f32[1,640,256]{2,1,0:T(8,128)S(1)} %get-tuple-element.46.refs_10_) | copy-start | bytes 1966084
  29.7 30.8 %copy-start.19 = (s32[1,8,1,2]{1,3,2,0:T(2,128)S(1)}, s32[1,8,1,2]{1,3,2,0:T(2,128)}, u32[]{:S(2)}) copy-start(s32[1,8,1,2]{1,3,2,0:T(2,128)} %param.8) | copy-start | bytes 196
  29.7 31.0 %copy-start.17 = (f32[8]{0:T(128)S(1)}, f32[8]{0:T(128)}, u32[]{:S(2)}) copy-start(f32[8]{0:T(128)} %refs_2_.13) | copy-start | bytes 100
  29.7 31.0 %copy-start.18 = (s32[1,8]{1,0:T(1,128)S(1)}, s32[1,8]{1,0:T(1,128)}, u32[]{:S(2)}) copy-start(s32[1,8]{1,0:T(1,128)} %param.9) | copy-start | bytes 100
  29.7 31.0 %collective-permute-start.4 = (f32[1,640,256]{2,1,0:T(8,128)}, f32[1,640,256]{2,1,0:T(8,128)}, u32[]{:S(2)}, u32[]{:S(2)}) collective-permute-start(f32[1,640,256]{2,1,0:T(8,128)} %get-tuple-element.45), channel_id=1, source_target_pairs={{0,64},{64,0},{128,192},{192,128},{256,320},{320,256},{384,448},{4... | collective-permute-start | bytes 1966088 | tf_op jit(solution)/shard_map/ppermute | solution.py:297
  35.6 31.8 %copy-start.3 = (f32[1,640,256]{2,1,0:T(8,128)}, f32[1,640,256]{2,1,0:T(8,128)S(1)}, u32[]{:S(2)}) copy-start(f32[1,640,256]{2,1,0:T(8,128)S(1)} %collective-permute-done.refs_5_) | copy-start | bytes 1966084
  40.1 27.3 %copy-start.5 = (f32[1,640,256]{2,1,0:T(8,128)}, f32[1,640,256]{2,1,0:T(8,128)S(1)}, u32[]{:S(2)}) copy-start(f32[1,640,256]{2,1,0:T(8,128)S(1)} %collective-permute-done.1.refs_6_) | copy-start | bytes 1966084
  48.4 0.9 copy-start.7
  52.3 0.8 copy-start.10
  53.1 23.0 %collective-permute-start.5 = (f32[1,640,256]{2,1,0:T(8,128)}, f32[1,640,256]{2,1,0:T(8,128)}, u32[]{:S(2)}, u32[]{:S(2)}) collective-permute-start(f32[1,640,256]{2,1,0:T(8,128)} %get-tuple-element.47), channel_id=1, source_target_pairs={{0,256},{64,320},{128,384},{192,448},{256,0},{320,64},{384,128},{4... | collective-permute-start | bytes 1966088 | tf_op jit(solution)/shard_map/ppermute | solution.py:297
  55.8 32.3 %collective-permute-start.6 = (f32[1,640,256]{2,1,0:T(8,128)}, f32[1,640,256]{2,1,0:T(8,128)}, u32[]{:S(2)}, u32[]{:S(2)}) collective-permute-start(f32[1,640,256]{2,1,0:T(8,128)} %get-tuple-element.48), channel_id=1, source_target_pairs={{0,320},{64,256},{128,448},{192,384},{256,64},{320,0},{384,192},{4... | collective-permute-start | bytes 1966088 | tf_op jit(solution)/shard_map/ppermute | solution.py:297
  60.7 1.1 copy-start.8
  61.8 1.1 copy-start.11
  62.9 1.1 copy-start.14
  67.4 30.1 %all-to-all-start = ((f32[16,96,128]{2,1,0:T(8,128)}), f32[16,96,128]{2,1,0:T(8,128)S(1)}, u32[]{:S(2)}, u32[]{:S(2)}) async-start(f32[16,96,128]{2,1,0:T(8,128)} %exchange.3), calls=%async_computation | async-start | bytes 1572864 | tf_op jit(solution)/shard_map/all_to_all | solution.py:300
  76.1 21.4 %copy-start.16 = (f32[768]{0:T(1024)S(1)}, f32[768]{0:T(1024)}, u32[]{:S(2)}) copy-start(f32[768]{0:T(1024)} %param.7) | copy-start | bytes 9220
  130.9 8.0 %copy-start.4 = (f32[1,640,256]{2,1,0:T(8,128)S(1)}, f32[1,640,256]{2,1,0:T(8,128)}, u32[]{:S(2)}) copy-start(f32[1,640,256]{2,1,0:T(8,128)} %copy-done.3) | copy-start | bytes 1966084
  130.9 8.0 %copy-start.6 = (f32[1,640,256]{2,1,0:T(8,128)S(1)}, f32[1,640,256]{2,1,0:T(8,128)}, u32[]{:S(2)}) copy-start(f32[1,640,256]{2,1,0:T(8,128)} %copy-done.5) | copy-start | bytes 1966084
  132.2 16.5 %all-to-all-start.2 = ((f32[16,32,128]{2,1,0:T(8,128)}), f32[16,32,128]{2,1,0:T(8,128)S(1)}, u32[]{:S(2)}, u32[]{:S(2)}) async-start(f32[16,32,128]{2,1,0:T(8,128)} %exchange.5), calls=%async_computation.2 | async-start | bytes 524288 | tf_op jit(solution)/shard_map/all_to_all | solution.py:300
  138.9 1.1 copy-start.9
  140.0 1.1 copy-start.12
  141.1 1.1 copy-start.15
  144.8 1.3 copy-start.1
  161.6 1.5 copy-start.2

commit v8 on v7

--- a/solution.py
+++ b/solution.py
@@ -44,7 +44,7 @@
     for (out_ref, k), (dx, dc) in zip(slots, shifts):
         receiver = partner_of(ids_ref, CHIPS - dx, dc)
         for s in range(2):
-            tile = lax.rem(pairs_ref[(receiver * 2 * CHIPS + ids_ref[0]) * 2 + s], cols // TILE)
+            tile = lax.rem(pairs_ref[receiver, ids_ref[0] * 2 + s], cols // TILE)
             source = block_ref.at[:, lanes(tile)]
             target = out_ref.at[k, pl.ds(0, rows), pl.ds(s * TILE, TILE)]
             copies.append(pltpu.make_async_copy(source, target, sems.at[len(copies)]))
@@ -76,7 +76,7 @@
     del refs
 
 
-def held(*arrays):
+def held(hint, *arrays):
     return pl.pallas_call(
         held_kernel,
         out_shape=[jax.ShapeDtypeStruct(array.shape, array.dtype) for array in arrays],
@@ -84,7 +84,7 @@
         out_specs=[pl.BlockSpec(memory_space=pl.ANY)] * len(arrays),
         input_output_aliases={k: k for k in range(len(arrays))},
         compiler_params=params(),
-        cost_estimate=cost(70 * 10**9, 70 * 3 * 10**6),
+        cost_estimate=cost(hint * 10**9, hint * 3 * 10**6),
         name="held",
     )(*arrays)
 
@@ -275,8 +275,8 @@
     )(*start, *inputs)
 
 
-NEAR = ((1, 0), (3, 0), (1, 1), (3, 1), (0, 1), (0, 0))
-FAR = ((2, 0), (2, 1))
+NEAR = ((1, 0), (3, 0), (1, 1), (3, 1), (0, 1))
+FAR = ((2, 0), (2, 1), (0, 0))
 
 
 def per_device(bq, eps_occ, eps_vir, tile_pairs, live_counts):
@@ -286,7 +286,7 @@
     rows, cols = block.shape
     padded = -(-rows // 16) * 16
     own_pairs = tile_pairs.reshape(-1)
-    all_pairs = lax.all_gather(tile_pairs[0, :, 0, :], "occ").reshape(-1)
+    all_pairs = lax.all_gather(own_pairs, "occ")
     ids = jnp.stack([me, lax.axis_index("aux")]).astype(jnp.int32)
     scalars = (ids, own_pairs, eps_occ, live_counts.reshape(-1))
     columns = jnp.broadcast_to(eps_vir[:, None], (cols, TILE))
@@ -302,15 +302,17 @@
     near = pick(ids, all_pairs, block, NEAR[:4], (1,) * 4, padded)
     later_ids, *near = lax.optimization_barrier((ids, *near))
     near = [moved(tiles, *shift) for tiles, shift in zip(near, NEAR)]
-    mate, own, *far = pick(later_ids, all_pairs, block, NEAR[4:] + FAR, (1,) * 4, padded)
+    mate, *far, own = pick(later_ids, all_pairs, block, NEAR[4:] + FAR, (1,) * 4, padded)
     mate = moved(mate, 0, 1)
     left_split = left(block, padded)
     far[0], far[1], left_split, *near = lax.optimization_barrier((*far, left_split, *near))
-    far = held(*[moved(tiles, *shift) for tiles, shift in zip(far, FAR)])
-    near_rights = [(tiles, 0) for tiles in (*near, mate, own)]
-    far_rights = [(tiles, 0) for tiles in far]
-
-    parts = sent(None, (NEAR, left_split, near_rights))
+    near_rights = [(tiles, 0) for tiles in (*near, mate)]
+    operand = exchange(scalars, None, (NEAR, left_split, near_rights))
+    far[1], operand = lax.optimization_barrier((far[1], operand))
+    far = [held(hint, moved(tiles, *shift))[0] for hint, tiles, shift in zip((70, 8), far, FAR)]
+    far_rights = [(tiles, 0) for tiles in (*far, own)]
+
+    parts = lax.all_to_all(operand, "aux", 0, 0)
     both = sent((NEAR, parts, 0, columns, levels), (FAR, left_split, far_rights))
     last = sent((FAR, both, 16 * len(NEAR), columns, levels), None)
     first_groups = [(NEAR, both, near_rights)]

time: 168 us -> 172 us (1.024)
  the two profiles are of different devices: /device:TPU:6 before, /device:TPU:2 now
where the time goes in v8:
time: 172 us; the launch traced here: 171 us
  blocking collectives  60.1 us (35%)
  waiting for transfers between devices  39.3 us (23%)
  starting transfers between devices  34.7 us (20%)
  local copies, waits for them, and re-layouts  18.7 us (11%)
  Pallas kernels  16.2 us (9%)
    ppermute x7, waiting for transfers between devices, moved(): return lax.ppermute(tiles, 'occ', route)  35.7 us
    all_to_all x1, blocking collectives, sent(): return lax.all_to_all(exchange(scalars, returned, group), 'aux', 0, 0)  34.5 us
    ppermute x7, starting transfers between devices, moved(): return lax.ppermute(tiles, 'occ', route)  20.1 us
    unnamed x50, local copies, waits for them, and re-layouts  18.4 us
    all_gather x1, blocking collectives, per_device(): all_pairs = lax.all_gather(own_pairs, 'occ')  13.6 us
    psum x1, blocking collectives, per_device(): energy, last = lax.optimization_barrier((lax.psum(energy, 'vir'), last))  12 us
    all_to_all x1, starting transfers between devices, per_device(): parts = lax.all_to_all(operand, 'aux', 0, 0)  8.78 us
    all_to_all x1, starting transfers between devices, sent(): return lax.all_to_all(exchange(scalars, returned, group), 'aux', 0, 0)  5.84 us
  transfers between devices with their start and end apart: 9, of which 6 were waited for; matrix products, arithmetic and copies ran while one was open for 0% of the time, Pallas kernels for 5%

profile of v8, /device:TPU:2, one launch (start us, length us, event | category | flops | bytes accessed | tf_op | source)
XLA Modules:
  0.0 170.8 jit_solution(1935171103871109754)
XLA Ops:
  0.6 0.8 copy.15
  1.4 0.1 reshape.19
  1.5 13.6 %all-gather = s32[8,1,16]{2,1,0:T(1,128)S(1)} all-gather(s32[1,1,16]{2,1,0:T(1,128)S(1)} %reshape.19), channel_id=1, replica_groups=mesh['occ'=8,'aux'=16,'vir'=4] {'occ'}, dimensions={0}, use_global_device_ids=true | all-gather | bytes 576 | tf_op jit(solution)/shard_map/all_gather | solution.py:289
  15.1 0.1 pad_add_fusion.ids_ref.refs_0_
  15.2 1.5 copy-done
  16.7 1.0 pick.2
  17.7 1.9 %collective-permute-start = (f32[1,640,256]{2,1,0:T(8,128)S(1)}, f32[1,640,256]{2,1,0:T(8,128)S(1)}, u32[]{:S(2)}, u32[]{:S(2)}) collective-permute-start(f32[1,640,256]{2,1,0:T(8,128)S(1)} %get-tuple-element.36), channel_id=1, source_target_pairs={{0,128},{64,192},{128,256},{192,320},{256,384},{320,448},{384,0},{... | collective-permute-start | bytes 1966088 | tf_op jit(solution)/shard_map/ppermute | solution.py:297
  19.7 3.9 %collective-permute-start.1 = (f32[1,640,256]{2,1,0:T(8,128)S(1)}, f32[1,640,256]{2,1,0:T(8,128)S(1)}, u32[]{:S(2)}, u32[]{:S(2)}) collective-permute-start(f32[1,640,256]{2,1,0:T(8,128)S(1)} %get-tuple-element.37), channel_id=1, source_target_pairs={{0,384},{64,448},{128,0},{192,64},{256,128},{320,192},{384,256},{4... | collective-permute-start | bytes 1966088 | tf_op jit(solution)/shard_map/ppermute | solution.py:297
  23.6 1.9 %collective-permute-start.2 = (f32[1,640,256]{2,1,0:T(8,128)S(1)}, f32[1,640,256]{2,1,0:T(8,128)S(1)}, u32[]{:S(2)}, u32[]{:S(2)}) collective-permute-start(f32[1,640,256]{2,1,0:T(8,128)S(1)} %get-tuple-element.38), channel_id=1, source_target_pairs={{0,192},{64,128},{128,320},{192,256},{256,448},{320,384},{384,64},... | collective-permute-start | bytes 1966088 | tf_op jit(solution)/shard_map/ppermute | solution.py:297
  25.5 3.6 %collective-permute-start.3 = (f32[1,640,256]{2,1,0:T(8,128)S(1)}, f32[1,640,256]{2,1,0:T(8,128)S(1)}, u32[]{:S(2)}, u32[]{:S(2)}) collective-permute-start(f32[1,640,256]{2,1,0:T(8,128)S(1)} %get-tuple-element.39), channel_id=1, source_target_pairs={{0,448},{64,384},{128,64},{192,0},{256,192},{320,128},{384,320},{4... | collective-permute-start | bytes 1966088 | tf_op jit(solution)/shard_map/ppermute | solution.py:297
  29.2 1.8 %pick.3 = (f32[1,640,256]{2,1,0:T(8,128)}, f32[1,640,256]{2,1,0:T(8,128)}, f32[1,640,256]{2,1,0:T(8,128)S(1)}, f32[1,640,256]{2,1,0:T(8,128)S(1)}) custom-call(s32[2]{0:T(128)S(1)} %pad_add_fusion.ids_ref.refs_0_, s32[8,16]{1,0:T(8,128)S(1)} %bitcast.32, f32[632,768]{1,0:T(8,128)S(1)} %bitcast.25), custom_call_target="tpu_custom_call" | custom-call | bytes 5242880 | tf_op jit(solution)/shard_map/pick/pallas_call | solution.py:60
  31.0 0.0 copy-start.3
  31.0 0.0 copy-start.23
  31.0 0.0 copy-start.21
  31.0 0.0 copy-start.22
  31.0 2.1 %collective-permute-start.4 = (f32[1,640,256]{2,1,0:T(8,128)}, f32[1,640,256]{2,1,0:T(8,128)}, u32[]{:S(2)}, u32[]{:S(2)}) collective-permute-start(f32[1,640,256]{2,1,0:T(8,128)} %get-tuple-element.46), channel_id=1, source_target_pairs={{0,64},{64,0},{128,192},{192,128},{256,320},{320,256},{384,448},{4... | collective-permute-start | bytes 1966088 | tf_op jit(solution)/shard_map/ppermute | solution.py:297
  33.1 0.6 left.1.refs_4_.refs_7_
  33.7 0.0 copy-done.3
  33.7 3.5 %collective-permute-done.refs_5_ = f32[1,640,256]{2,1,0:T(8,128)S(1)} collective-permute-done((f32[1,640,256]{2,1,0:T(8,128)S(1)}, f32[1,640,256]{2,1,0:T(8,128)S(1)}, u32[]{:S(2)}, u32[]{:S(2)}) %collective-permute-start) | collective-permute-done | bytes 655392 | tf_op jit(solution)/shard_map/ppermute | solution.py:297
  37.2 1.9 %collective-permute-done.1.refs_6_ = f32[1,640,256]{2,1,0:T(8,128)S(1)} collective-permute-done((f32[1,640,256]{2,1,0:T(8,128)S(1)}, f32[1,640,256]{2,1,0:T(8,128)S(1)}, u32[]{:S(2)}, u32[]{:S(2)}) %collective-permute-start.1) | collective-permute-done | bytes 655392 | tf_op jit(solution)/shard_map/ppermute | solution.py:297
  39.1 10.9 %collective-permute-done.2.refs_7_ = f32[1,640,256]{2,1,0:T(8,128)S(1)} collective-permute-done((f32[1,640,256]{2,1,0:T(8,128)S(1)}, f32[1,640,256]{2,1,0:T(8,128)S(1)}, u32[]{:S(2)}, u32[]{:S(2)}) %collective-permute-start.2) | collective-permute-done | bytes 655392 | tf_op jit(solution)/shard_map/ppermute | solution.py:297
  50.0 0.8 copy-done.14
  50.8 1.1 collective-permute-done.3.refs_8_
  51.9 0.8 copy-done.17
  52.8 4.6 %collective-permute-start.5 = (f32[1,640,256]{2,1,0:T(8,128)}, f32[1,640,256]{2,1,0:T(8,128)}, u32[]{:S(2)}, u32[]{:S(2)}) collective-permute-start(f32[1,640,256]{2,1,0:T(8,128)} %get-tuple-element.48), channel_id=1, source_target_pairs={{0,256},{64,320},{128,384},{192,448},{256,0},{320,64},{384,128},{4... | collective-permute-start | bytes 1966088 | tf_op jit(solution)/shard_map/ppermute | solution.py:297
  57.4 0.1 reshape.16.refs_1_
  57.5 0.0 collective-permute-done.4.refs_9_
  57.5 0.0 copy-start.15
  57.5 1.1 copy-done.15
  58.6 1.1 copy-done.18
  59.7 2.3 %exchange.3 = f32[16,80,128]{2,1,0:T(8,128)S(1)} custom-call(s32[2]{0:T(128)S(1)} %pad_add_fusion.ids_ref.refs_0_, s32[16]{0:T(128)S(1)} %reshape.16.refs_1_, f32[8]{0:T(128)S(1)} %copy-done.21, s32[8]{0:T(128)S(1)} %bitcast.33, bf16[6,256,640]{2,1,0:T(8,128)(2,1)S(1)} %left.1.refs_4_.refs_7_, f32[1,640,256]{2,1,0:T(8,128)S(1)} %collective-permute-done.refs_5_, ...), custom_call_target="tpu_custom_call" | custom-call | flops 838860800 | bytes 1310720 | tf_op jit(solution)/shard_map/exchange/pallas_call | solution.py:180
  62.0 0.0 copy-done.10
  62.0 0.8 copy-done.9
  62.8 8.8 %all-to-all-start = ((f32[16,80,128]{2,1,0:T(8,128)}), f32[16,80,128]{2,1,0:T(8,128)S(1)}, u32[]{:S(2)}, u32[]{:S(2)}) async-start(f32[16,80,128]{2,1,0:T(8,128)} %copy-done.9), calls=%async_computation | async-start | bytes 1310720 | tf_op jit(solution)/shard_map/all_to_all | solution.py:315
  71.6 2.0 %collective-permute-start.6 = (f32[1,640,256]{2,1,0:T(8,128)}, f32[1,640,256]{2,1,0:T(8,128)S(1)}, u32[]{:S(2)}, u32[]{:S(2)}) collective-permute-start(f32[1,640,256]{2,1,0:T(8,128)} %copy-done.23), channel_id=1, source_target_pairs={{0,320},{64,256},{128,448},{192,384},{256,64},{320,0},{384,192},{4... | collective-permute-start | bytes 1966088 | tf_op jit(solution)/shard_map/ppermute | solution.py:297
  73.6 0.0 collective-permute-done.5.refs_0_
  73.7 0.0 copy-start.20
  73.7 18.3 %collective-permute-done.6.refs_0_ = f32[1,640,256]{2,1,0:T(8,128)S(1)} collective-permute-done((f32[1,640,256]{2,1,0:T(8,128)}, f32[1,640,256]{2,1,0:T(8,128)S(1)}, u32[]{:S(2)}, u32[]{:S(2)}) %collective-permute-start.6) | collective-permute-done | bytes 655392 | tf_op jit(solution)/shard_map/ppermute | solution.py:297
  92.0 0.9 copy-done.6
  92.8 0.0 all-to-all-done.refs_4_
  92.8 0.2 broadcast_in_dim.27.refs_5_.refs_4_
  93.0 1.1 copy-done.4
  94.1 1.1 copy-done.7
  95.2 2.0 %exchange.4 = f32[16,128,128]{2,1,0:T(8,128)S(1)} custom-call(s32[2]{0:T(128)S(1)} %pad_add_fusion.ids_ref.refs_0_, s32[16]{0:T(128)S(1)} %reshape.16.refs_1_, f32[8]{0:T(128)S(1)} %copy-done.21, s32[8]{0:T(128)S(1)} %bitcast.34, f32[16,80,128]{2,1,0:T(8,128)S(1)} %all-to-all-done.refs_4_, f32[768,128]{1,0:T(8,128)S(1)} %broadcast_in_dim.27.refs_5_.refs_4_, ...), custom_call_target="tpu_custom_call" | custom-call | flops 503316480 | bytes 2097152 | tf_op jit(solution)/shard_map/exchange/pallas_call | solution.py:180
  97.2 34.5 %all_to_all.15.refs_4_.refs_6_ = f32[16,128,128]{2,1,0:T(8,128)S(1)} all-to-all(f32[16,128,128]{2,1,0:T(8,128)S(1)} %exchange.4), channel_id=1, replica_groups=mesh['occ'=8,'aux'=16,'vir'=4] {'aux'}, dimensions={0} | all-to-all | bytes 2097152 | tf_op jit(solution)/shard_map/all_to_all | solution.py:300
  131.6 1.4 exchange.5
  133.1 5.8 %all-to-all-start.2 = ((f32[16,48,128]{2,1,0:T(8,128)}), f32[16,48,128]{2,1,0:T(8,128)S(1)}, u32[]{:S(2)}, u32[]{:S(2)}) async-start(f32[16,48,128]{2,1,0:T(8,128)} %exchange.5), calls=%async_computation.2 | async-start | bytes 786432 | tf_op jit(solution)/shard_map/all_to_all | solution.py:300
  139.0 0.7 energy.2
  139.7 1.1 copy-done.11
  140.8 1.1 copy-done.13
  141.9 1.1 copy-done.16
  143.0 1.1 copy-done.19
  144.1 2.5 %gamma.2.refs_4_ = f32[632,768]{1,0:T(8,128)S(1)} custom-call(s32[2]{0:T(128)S(1)} %pad_add_fusion.ids_ref.refs_0_, s32[16]{0:T(128)S(1)} %reshape.16.refs_1_, f32[8]{0:T(128)S(1)} %copy-done.21, s32[8]{0:T(128)S(1)} %bitcast.37, f32[16,128,128]{2,1,0:T(8,128)S(1)} %all_to_all.15.refs_4_.refs_6_, f32[1,640,256]{2,1,0:T(8,128)S(1)} %copy-done.11, ...), custom_call_target="tpu_custom_call" | custom-call | flops 828375040 | bytes 3883008 | tf_op jit(solution)/shard_map/gamma/pallas_call | solution.py:267
  146.6 0.0 copy-start.1
  146.6 1.3 copy-done.1
  147.8 3.7 %all-to-all-done.2.refs_6_.refs_5_ = f32[16,48,128]{2,1,0:T(8,128)S(1)} async-done(((f32[16,48,128]{2,1,0:T(8,128)}), f32[16,48,128]{2,1,0:T(8,128)S(1)}, u32[]{:S(2)}, u32[]{:S(2)}) %all-to-all-start.2) | async-done | bytes 393248 | tf_op jit(solution)/shard_map/all_to_all | solution.py:300
  151.5 0.7 energy.3
  152.1 0.1 maximum_reduce_fusion
  152.3 0.1 stack.47
  152.4 12.0 %psum.7 = f32[8]{0:T(128)S(1)} all-reduce(f32[8]{0:T(128)S(1)} %maximum_reduce_fusion), channel_id=1, replica_groups=mesh['occ'=8,'aux'=16,'vir'=4] {'vir'}, use_global_device_ids=true, to_apply=%region_1.0 | all-reduce | flops 8 | bytes 64 | tf_op jit(solution)/shard_map/psum | solution.py:325
  164.4 1.5 copy-done.2
  165.9 1.1 copy-done.8
  167.0 3.2 %gamma.3 = f32[632,768]{1,0:T(8,128)} custom-call(s32[2]{0:T(128)S(1)} %pad_add_fusion.ids_ref.refs_0_, s32[16]{0:T(128)S(1)} %reshape.16.refs_1_, f32[8]{0:T(128)S(1)} %copy-done.21, s32[8]{0:T(128)S(1)} %bitcast.39, f32[632,768]{1,0:T(8,128)S(1)} %copy-done.2, f32[16,48,128]{2,1,0:T(8,128)S(1)} %all-to-all-done.2.refs_6_.refs_5_, ...), custom_call_target="tpu_custom_call" | custom-call | flops 497025024 | bytes 3883008 | tf_op jit(solution)/shard_map/gamma/pallas_call | solution.py:267
  170.2 0.6 select_reduce_fusion
  (25 shorter events, 0.0 us)
Async XLA Ops:
  15.2 1.5 copy-start
  17.7 19.4 %collective-permute-start = (f32[1,640,256]{2,1,0:T(8,128)S(1)}, f32[1,640,256]{2,1,0:T(8,128)S(1)}, u32[]{:S(2)}, u32[]{:S(2)}) collective-permute-start(f32[1,640,256]{2,1,0:T(8,128)S(1)} %get-tuple-element.36), channel_id=1, source_target_pairs={{0,128},{64,192},{128,256},{192,320},{256,384},{320,448},{384,0},{... | collective-permute-start | bytes 1966088 | tf_op jit(solution)/shard_map/ppermute | solution.py:297
  19.7 19.4 %collective-permute-start.1 = (f32[1,640,256]{2,1,0:T(8,128)S(1)}, f32[1,640,256]{2,1,0:T(8,128)S(1)}, u32[]{:S(2)}, u32[]{:S(2)}) collective-permute-start(f32[1,640,256]{2,1,0:T(8,128)S(1)} %get-tuple-element.37), channel_id=1, source_target_pairs={{0,384},{64,448},{128,0},{192,64},{256,128},{320,192},{384,256},{4... | collective-permute-start | bytes 1966088 | tf_op jit(solution)/shard_map/ppermute | solution.py:297
  23.6 26.4 %collective-permute-start.2 = (f32[1,640,256]{2,1,0:T(8,128)S(1)}, f32[1,640,256]{2,1,0:T(8,128)S(1)}, u32[]{:S(2)}, u32[]{:S(2)}) collective-permute-start(f32[1,640,256]{2,1,0:T(8,128)S(1)} %get-tuple-element.38), channel_id=1, source_target_pairs={{0,192},{64,128},{128,320},{192,256},{256,448},{320,384},{384,64},... | collective-permute-start | bytes 1966088 | tf_op jit(solution)/shard_map/ppermute | solution.py:297
  25.5 26.4 %collective-permute-start.3 = (f32[1,640,256]{2,1,0:T(8,128)S(1)}, f32[1,640,256]{2,1,0:T(8,128)S(1)}, u32[]{:S(2)}, u32[]{:S(2)}) collective-permute-start(f32[1,640,256]{2,1,0:T(8,128)S(1)} %get-tuple-element.39), channel_id=1, source_target_pairs={{0,448},{64,384},{128,64},{192,0},{256,192},{320,128},{384,320},{4... | collective-permute-start | bytes 1966088 | tf_op jit(solution)/shard_map/ppermute | solution.py:297
  31.0 2.7 %copy-start.3 = (f32[1,640,256]{2,1,0:T(8,128)}, f32[1,640,256]{2,1,0:T(8,128)S(1)}, u32[]{:S(2)}) copy-start(f32[1,640,256]{2,1,0:T(8,128)S(1)} %get-tuple-element.50.refs_10_.refs_8_) | copy-start | bytes 1966084
  31.0 21.8 %copy-start.23 = (f32[1,640,256]{2,1,0:T(8,128)}, f32[1,640,256]{2,1,0:T(8,128)S(1)}, u32[]{:S(2)}) copy-start(f32[1,640,256]{2,1,0:T(8,128)S(1)} %get-tuple-element.49) | copy-start | bytes 1966084
  31.0 26.5 %copy-start.21 = (f32[8]{0:T(128)S(1)}, f32[8]{0:T(128)}, u32[]{:S(2)}) copy-start(f32[8]{0:T(128)} %refs_2_.13) | copy-start | bytes 100
  31.0 26.5 %copy-start.22 = (s32[1,8]{1,0:T(1,128)S(1)}, s32[1,8]{1,0:T(1,128)}, u32[]{:S(2)}) copy-start(s32[1,8]{1,0:T(1,128)} %param.9) | copy-start | bytes 100
  31.0 26.4 %collective-permute-start.4 = (f32[1,640,256]{2,1,0:T(8,128)}, f32[1,640,256]{2,1,0:T(8,128)}, u32[]{:S(2)}, u32[]{:S(2)}) collective-permute-start(f32[1,640,256]{2,1,0:T(8,128)} %get-tuple-element.46), channel_id=1, source_target_pairs={{0,64},{64,0},{128,192},{192,128},{256,320},{320,256},{384,448},{4... | collective-permute-start | bytes 1966088 | tf_op jit(solution)/shard_map/ppermute | solution.py:297
  37.2 24.8 %copy-start.10 = (f32[1,640,256]{2,1,0:T(8,128)}, f32[1,640,256]{2,1,0:T(8,128)S(1)}, u32[]{:S(2)}) copy-start(f32[1,640,256]{2,1,0:T(8,128)S(1)} %collective-permute-done.refs_5_) | copy-start | bytes 1966084
  39.1 22.9 %copy-start.12 = (f32[1,640,256]{2,1,0:T(8,128)}, f32[1,640,256]{2,1,0:T(8,128)S(1)}, u32[]{:S(2)}) copy-start(f32[1,640,256]{2,1,0:T(8,128)S(1)} %collective-permute-done.1.refs_6_) | copy-start | bytes 1966084
  50.0 0.8 copy-start.14
  51.9 0.8 copy-start.17
  52.8 20.9 %collective-permute-start.5 = (f32[1,640,256]{2,1,0:T(8,128)}, f32[1,640,256]{2,1,0:T(8,128)}, u32[]{:S(2)}, u32[]{:S(2)}) collective-permute-start(f32[1,640,256]{2,1,0:T(8,128)} %get-tuple-element.48), channel_id=1, source_target_pairs={{0,256},{64,320},{128,384},{192,448},{256,0},{320,64},{384,128},{4... | collective-permute-start | bytes 1966088 | tf_op jit(solution)/shard_map/ppermute | solution.py:297
  57.5 1.1 copy-start.15
  58.6 1.1 copy-start.18
  62.0 0.9 copy-start.9
  62.8 30.0 %all-to-all-start = ((f32[16,80,128]{2,1,0:T(8,128)}), f32[16,80,128]{2,1,0:T(8,128)S(1)}, u32[]{:S(2)}, u32[]{:S(2)}) async-start(f32[16,80,128]{2,1,0:T(8,128)} %copy-done.9), calls=%async_computation | async-start | bytes 1310720 | tf_op jit(solution)/shard_map/all_to_all | solution.py:315
  71.6 20.3 %collective-permute-start.6 = (f32[1,640,256]{2,1,0:T(8,128)}, f32[1,640,256]{2,1,0:T(8,128)S(1)}, u32[]{:S(2)}, u32[]{:S(2)}) collective-permute-start(f32[1,640,256]{2,1,0:T(8,128)} %copy-done.23), channel_id=1, source_target_pairs={{0,320},{64,256},{128,448},{192,384},{256,64},{320,0},{384,192},{4... | collective-permute-start | bytes 1966088 | tf_op jit(solution)/shard_map/ppermute | solution.py:297
  73.7 19.2 %copy-start.20 = (f32[768]{0:T(1024)S(1)}, f32[768]{0:T(1024)}, u32[]{:S(2)}) copy-start(f32[768]{0:T(1024)} %param.7) | copy-start | bytes 9220
  92.0 0.9 copy-start.6
  93.0 1.1 copy-start.4
  94.1 1.1 copy-start.7
  133.1 18.4 %all-to-all-start.2 = ((f32[16,48,128]{2,1,0:T(8,128)}), f32[16,48,128]{2,1,0:T(8,128)S(1)}, u32[]{:S(2)}, u32[]{:S(2)}) async-start(f32[16,48,128]{2,1,0:T(8,128)} %exchange.5), calls=%async_computation.2 | async-start | bytes 786432 | tf_op jit(solution)/shard_map/all_to_all | solution.py:300
  139.7 1.1 copy-start.11
  140.8 1.1 copy-start.13
  141.9 1.1 copy-start.16
  143.0 1.1 copy-start.19
  144.1 20.3 %copy-start.5 = (f32[1,640,256]{2,1,0:T(8,128)S(1)}, f32[1,640,256]{2,1,0:T(8,128)}, u32[]{:S(2)}) copy-start(f32[1,640,256]{2,1,0:T(8,128)} %copy-done.3) | copy-start | bytes 1966084
  146.6 1.3 copy-start.1
  164.4 1.5 copy-start.2
  165.9 1.1 copy-start.8

commit v9 on v7

--- a/solution.py
+++ b/solution.py
@@ -76,7 +76,7 @@
     del refs
 
 
-def held(*arrays):
+def held(hint, *arrays):
     return pl.pallas_call(
         held_kernel,
         out_shape=[jax.ShapeDtypeStruct(array.shape, array.dtype) for array in arrays],
@@ -84,7 +84,7 @@
         out_specs=[pl.BlockSpec(memory_space=pl.ANY)] * len(arrays),
         input_output_aliases={k: k for k in range(len(arrays))},
         compiler_params=params(),
-        cost_estimate=cost(70 * 10**9, 70 * 3 * 10**6),
+        cost_estimate=cost(hint * 10**9, hint * 3 * 10**6),
         name="held",
     )(*arrays)
 
@@ -275,7 +275,8 @@
     )(*start, *inputs)
 
 
-NEAR = ((1, 0), (3, 0), (1, 1), (3, 1), (0, 1), (0, 0))
+EARLY = ((0, 1), (0, 0))
+NEAR = ((1, 0), (3, 0), (1, 1), (3, 1))
 FAR = ((2, 0), (2, 1))
 
 
@@ -299,21 +300,23 @@
     def sent(returned, group):
         return lax.all_to_all(exchange(scalars, returned, group), "aux", 0, 0)
 
-    near = pick(ids, all_pairs, block, NEAR[:4], (1,) * 4, padded)
+    near = pick(ids, all_pairs, block, NEAR, (1,) * 4, padded)
     later_ids, *near = lax.optimization_barrier((ids, *near))
-    near = [moved(tiles, *shift) for tiles, shift in zip(near, NEAR)]
-    mate, own, *far = pick(later_ids, all_pairs, block, NEAR[4:] + FAR, (1,) * 4, padded)
-    mate = moved(mate, 0, 1)
+    near = held(70, *[moved(tiles, *shift) for tiles, shift in zip(near, NEAR)])
+    mate, own, *far = pick(later_ids, all_pairs, block, EARLY + FAR, (1,) * 4, padded)
+    early_rights = [(moved(mate, 0, 1), 0), (own, 0)]
     left_split = left(block, padded)
-    far[0], far[1], left_split, *near = lax.optimization_barrier((*far, left_split, *near))
-    far = held(*[moved(tiles, *shift) for tiles, shift in zip(far, FAR)])
-    near_rights = [(tiles, 0) for tiles in (*near, mate, own)]
+
+    early = sent(None, (EARLY, left_split, early_rights))
+    far[0], far[1], early, *near = lax.optimization_barrier((*far, early, *near))
+    far = held(70, *[moved(tiles, *shift) for tiles, shift in zip(far, FAR)])
+    near_rights = [(tiles, 0) for tiles in near]
     far_rights = [(tiles, 0) for tiles in far]
 
-    parts = sent(None, (NEAR, left_split, near_rights))
-    both = sent((NEAR, parts, 0, columns, levels), (FAR, left_split, far_rights))
+    parts = sent((EARLY, early, 0, columns, levels), (NEAR, left_split, near_rights))
+    both = sent((NEAR, parts, 16 * len(EARLY), columns, levels), (FAR, left_split, far_rights))
     last = sent((FAR, both, 16 * len(NEAR), columns, levels), None)
-    first_groups = [(NEAR, both, near_rights)]
+    first_groups = [(EARLY, parts, early_rights), (NEAR, both, near_rights)]
     total = gamma_add(scalars, first_groups, rows, cols, None)
     first_energy = energy_of(scalars, columns, levels, first_groups)
     last, total, first_energy = lax.optimization_barrier((last, total, first_energy))
@@ -321,7 +324,7 @@
 
     energy = jnp.sum(jnp.concatenate([first_energy, last_energy], axis=0), axis=1)
     energy, last = lax.optimization_barrier((lax.psum(energy, "vir"), last))
-    order = jnp.stack([(me // 2 - dx) % CHIPS * 2 + (me + dc) % 2 for dx, dc in NEAR + FAR])
+    order = jnp.stack([(me // 2 - dx) % CHIPS * 2 + (me + dc) % 2 for dx, dc in EARLY + NEAR + FAR])
     mine = order[:, None] == jnp.arange(occ_size)[None, :]
     energy = jnp.sum(jnp.where(mine, energy[:, None], 0.0), axis=0)
     total = gamma_add(scalars, [(FAR, last, far_rights)], rows, cols, total)

time: 168 us -> 164 us (0.976)
  waiting for transfers between devices: 42.3 us -> 35.4 us
  starting transfers between devices: 36.3 us -> 42.9 us
  blocking collectives: 55.9 us -> 51.7 us
  Pallas kernels: 17.5 us -> 20.4 us
  local copies, waits for them, and re-layouts: 13.2 us -> 10.4 us
    all_to_all x2 -> x3, starting transfers between devices: 14.5 us -> 21.7 us  [sent(): return lax.all_to_all(exchange(scalars, returned, group), 'aux', 0, 0)]
    ppermute x7, waiting for transfers between devices: 30.2 us -> 25.4 us  [moved(): return lax.ppermute(tiles, 'occ', route)]
    all_to_all x1, blocking collectives: 31.3 us -> 27.1 us  [sent(): return lax.all_to_all(exchange(scalars, returned, group), 'aux', 0, 0)]
    unnamed x41 -> x33, local copies, waits for them, and re-layouts: 12.7 us -> 9.87 us
    all_to_all x2 -> x3, waiting for transfers between devices: 12.1 us -> 10 us  [sent(): return lax.all_to_all(exchange(scalars, returned, group), 'aux', 0, 0)]
    pallas_call x3 -> x4, Pallas kernels: 6.69 us -> 8.21 us  [exchange(): pl.pallas_call(functools.partial(exchange_kernel, back_shifts, parts_at,...]
  transfers between devices with their start and end apart: 9 -> 10, of which waited for: 7 -> 6; matrix products, arithmetic and copies ran while one was open for 0% -> 0% of each run, Pallas kernels for 6% -> 6%
where the time goes in v9:
time: 164 us; the launch traced here: 163 us
  blocking collectives  51.7 us (32%)
  starting transfers between devices  42.9 us (26%)
  waiting for transfers between devices  35.4 us (22%)
  Pallas kernels  20.4 us (12%)
  local copies, waits for them, and re-layouts  10.4 us (6%)
    all_to_all x1, blocking collectives, sent(): return lax.all_to_all(exchange(scalars, returned, group), 'aux', 0, 0)  27.1 us
    ppermute x7, waiting for transfers between devices, moved(): return lax.ppermute(tiles, 'occ', route)  25.4 us
    all_to_all x3, starting transfers between devices, sent(): return lax.all_to_all(exchange(scalars, returned, group), 'aux', 0, 0)  21.7 us
    ppermute x7, starting transfers between devices, moved(): return lax.ppermute(tiles, 'occ', route)  21.2 us
    all_gather x1, blocking collectives, per_device(): all_pairs = lax.all_gather(tile_pairs[0, :, 0, :], 'occ').reshape(-1)  12.7 us
    psum x1, blocking collectives, per_device(): energy, last = lax.optimization_barrier((lax.psum(energy, 'vir'), last))  12 us
    all_to_all x3, waiting for transfers between devices, sent(): return lax.all_to_all(exchange(scalars, returned, group), 'aux', 0, 0)  10 us
    unnamed x33, local copies, waits for them, and re-layouts  9.87 us
  transfers between devices with their start and end apart: 10, of which 6 were waited for; matrix products, arithmetic and copies ran while one was open for 0% of the time, Pallas kernels for 6%

profile of v9, /device:TPU:6, one launch (start us, length us, event | category | flops | bytes accessed | tf_op | source)
XLA Modules:
  0.0 162.8 jit_solution(9064539646128252029)
XLA Ops:
  0.6 12.7 %all-gather = s32[8,8,1,2]{1,3,2,0:T(2,128)S(1)} all-gather(s32[1,8,1,2]{1,3,2,0:T(2,128)} %param.8), channel_id=2, replica_groups=mesh['occ'=8,'aux'=16,'vir'=4] {'occ'}, dimensions={0}, use_global_device_ids=true | all-gather | bytes 576 | tf_op jit(solution)/shard_map/all_gather | solution.py:290
  13.3 0.1 copy.20
  13.4 0.1 reshape.21.pairs_ref
  13.6 0.1 pad_add_fusion.ids_ref.refs_0_
  13.7 1.5 copy-done
  15.2 2.2 %pick.2 = (f32[1,640,256]{2,1,0:T(8,128)}, f32[1,640,256]{2,1,0:T(8,128)}, f32[1,640,256]{2,1,0:T(8,128)}, f32[1,640,256]{2,1,0:T(8,128)}) custom-call(s32[2]{0:T(128)S(1)} %pad_add_fusion.ids_ref.refs_0_, s32[128]{0:T(128)S(1)} %reshape.21.pairs_ref, f32[632,768]{1,0:T(8,128)S(1)} %bitcast.23), custom_call_target="tpu_custom_call" | custom-call | bytes 5242880 | tf_op jit(solution)/shard_map/pick/pallas_call | solution.py:60
  17.4 1.5 pick.3
  19.0 0.0 copy-start.7
  19.0 0.9 copy-done.7
  19.9 2.2 %collective-permute-start = (f32[1,640,256]{2,1,0:T(8,128)}, f32[1,640,256]{2,1,0:T(8,128)}, u32[]{:S(2)}, u32[]{:S(2)}) collective-permute-start(f32[1,640,256]{2,1,0:T(8,128)} %get-tuple-element.40), channel_id=1, source_target_pairs={{0,64},{64,0},{128,192},{192,128},{256,320},{320,256},{384,448},{4... | collective-permute-start | bytes 1966088 | tf_op jit(solution)/shard_map/ppermute | solution.py:298
  22.1 3.2 %collective-permute-start.1 = (f32[1,640,256]{2,1,0:T(8,128)}, f32[1,640,256]{2,1,0:T(8,128)S(1)}, u32[]{:S(2)}, u32[]{:S(2)}) collective-permute-start(f32[1,640,256]{2,1,0:T(8,128)} %get-tuple-element.42), channel_id=1, source_target_pairs={{0,128},{64,192},{128,256},{192,320},{256,384},{320,448},{384,0},{... | collective-permute-start | bytes 1966088 | tf_op jit(solution)/shard_map/ppermute | solution.py:298
  25.3 2.6 %collective-permute-start.2 = (f32[1,640,256]{2,1,0:T(8,128)}, f32[1,640,256]{2,1,0:T(8,128)}, u32[]{:S(2)}, u32[]{:S(2)}) collective-permute-start(f32[1,640,256]{2,1,0:T(8,128)} %get-tuple-element.43), channel_id=1, source_target_pairs={{0,384},{64,448},{128,0},{192,64},{256,128},{320,192},{384,256},{4... | collective-permute-start | bytes 1966088 | tf_op jit(solution)/shard_map/ppermute | solution.py:298
  27.9 3.7 %collective-permute-start.3 = (f32[1,640,256]{2,1,0:T(8,128)}, f32[1,640,256]{2,1,0:T(8,128)}, u32[]{:S(2)}, u32[]{:S(2)}) collective-permute-start(f32[1,640,256]{2,1,0:T(8,128)} %get-tuple-element.44), channel_id=1, source_target_pairs={{0,192},{64,128},{128,320},{192,256},{256,448},{320,384},{384,64},... | collective-permute-start | bytes 1966088 | tf_op jit(solution)/shard_map/ppermute | solution.py:298
  31.6 1.9 %collective-permute-start.4 = (f32[1,640,256]{2,1,0:T(8,128)}, f32[1,640,256]{2,1,0:T(8,128)}, u32[]{:S(2)}, u32[]{:S(2)}) collective-permute-start(f32[1,640,256]{2,1,0:T(8,128)} %get-tuple-element.45), channel_id=1, source_target_pairs={{0,448},{64,384},{128,64},{192,0},{256,192},{320,128},{384,320},{4... | collective-permute-start | bytes 1966088 | tf_op jit(solution)/shard_map/ppermute | solution.py:298
  33.5 0.0 copy-done.13
  33.5 0.0 copy-done.14
  33.6 0.0 copy-done.15
  33.6 0.1 copy.19
  33.6 1.5 copy-done.1
  35.2 0.6 left.1.refs_4_.refs_7_
  35.8 0.1 reshape.19.refs_1_
  35.9 0.0 collective-permute-done.refs_5_
  35.9 0.0 copy-done.11
  35.9 0.0 copy-done.12
  35.9 0.0 copy-start.8
  35.9 1.1 copy-done.8
  37.0 2.4 %exchange.4 = f32[16,32,128]{2,1,0:T(8,128)} custom-call(s32[2]{0:T(128)S(1)} %pad_add_fusion.ids_ref.refs_0_, s32[16]{0:T(128)S(1)} %reshape.19.refs_1_, f32[8]{0:T(128)S(1)} %copy-done.11, s32[8]{0:T(128)S(1)} %bitcast.31, bf16[6,256,640]{2,1,0:T(8,128)(2,1)S(1)} %left.1.refs_4_.refs_7_, f32[1,640,256]{2,1,0:T(8,128)} %collective-permute-done.refs_5_, ...), custom_call_target="tpu_custom_call" | custom-call | flops 335544320 | bytes 524288 | tf_op jit(solution)/shard_map/exchange/pallas_call | solution.py:180
  39.4 8.7 %all-to-all-start = ((f32[16,32,128]{2,1,0:T(8,128)}), f32[16,32,128]{2,1,0:T(8,128)S(1)}, u32[]{:S(2)}, u32[]{:S(2)}) async-start(f32[16,32,128]{2,1,0:T(8,128)} %exchange.4), calls=%async_computation | async-start | bytes 524288 | tf_op jit(solution)/shard_map/all_to_all | solution.py:301
  48.1 0.0 copy-start.10
  48.1 0.0 collective-permute-done.1.refs_0_
  48.1 0.0 collective-permute-done.2.refs_1_
  48.1 6.3 %collective-permute-done.3.refs_2_ = f32[1,640,256]{2,1,0:T(8,128)} collective-permute-done((f32[1,640,256]{2,1,0:T(8,128)}, f32[1,640,256]{2,1,0:T(8,128)}, u32[]{:S(2)}, u32[]{:S(2)}) %collective-permute-start.3) | collective-permute-done | bytes 655392 | tf_op jit(solution)/shard_map/ppermute | solution.py:298
  54.4 3.8 %collective-permute-done.4.refs_3_ = f32[1,640,256]{2,1,0:T(8,128)} collective-permute-done((f32[1,640,256]{2,1,0:T(8,128)}, f32[1,640,256]{2,1,0:T(8,128)}, u32[]{:S(2)}, u32[]{:S(2)}) %collective-permute-start.4) | collective-permute-done | bytes 655392 | tf_op jit(solution)/shard_map/ppermute | solution.py:298
  58.2 0.0 all-to-all-done.refs_4_
  58.2 3.2 %collective-permute-start.5 = (f32[1,640,256]{2,1,0:T(8,128)}, f32[1,640,256]{2,1,0:T(8,128)}, u32[]{:S(2)}, u32[]{:S(2)}) collective-permute-start(f32[1,640,256]{2,1,0:T(8,128)} %copy-done.14), channel_id=1, source_target_pairs={{0,256},{64,320},{128,384},{192,448},{256,0},{320,64},{384,128},{4... | collective-permute-start | bytes 1966088 | tf_op jit(solution)/shard_map/ppermute | solution.py:298
  61.4 4.4 %collective-permute-start.6 = (f32[1,640,256]{2,1,0:T(8,128)}, f32[1,640,256]{2,1,0:T(8,128)}, u32[]{:S(2)}, u32[]{:S(2)}) collective-permute-start(f32[1,640,256]{2,1,0:T(8,128)} %copy-done.13), channel_id=1, source_target_pairs={{0,320},{64,256},{128,448},{192,384},{256,64},{320,0},{384,192},{4... | collective-permute-start | bytes 1966088 | tf_op jit(solution)/shard_map/ppermute | solution.py:298
  65.8 0.0 copy-done.10
  65.8 0.2 broadcast_in_dim.27.refs_5_.refs_4_
  66.0 2.5 %exchange.5 = f32[16,96,128]{2,1,0:T(8,128)S(1)} custom-call(s32[2]{0:T(128)S(1)} %pad_add_fusion.ids_ref.refs_0_, s32[16]{0:T(128)S(1)} %reshape.19.refs_1_, f32[8]{0:T(128)S(1)} %copy-done.11, s32[8]{0:T(128)S(1)} %bitcast.32, f32[16,32,128]{2,1,0:T(8,128)S(1)} %all-to-all-done.refs_4_, f32[768,128]{1,0:T(8,128)S(1)} %broadcast_in_dim.27.refs_5_.refs_4_, ...), custom_call_target="tpu_custom_call" | custom-call | flops 671088640 | bytes 1572864 | tf_op jit(solution)/shard_map/exchange/pallas_call | solution.py:180
  68.5 0.0 copy-done.5
  68.5 0.0 copy-start.4
  68.5 0.9 copy-done.4
  69.4 8.7 %all-to-all-start.1 = ((f32[16,96,128]{2,1,0:T(8,128)}), f32[16,96,128]{2,1,0:T(8,128)S(1)}, u32[]{:S(2)}, u32[]{:S(2)}) async-start(f32[16,96,128]{2,1,0:T(8,128)} %copy-done.4), calls=%async_computation.1 | async-start | bytes 1572864 | tf_op jit(solution)/shard_map/all_to_all | solution.py:301
  78.1 1.4 collective-permute-done.5.refs_0_
  79.6 13.9 %collective-permute-done.6.refs_1_ = f32[1,640,256]{2,1,0:T(8,128)} collective-permute-done((f32[1,640,256]{2,1,0:T(8,128)}, f32[1,640,256]{2,1,0:T(8,128)}, u32[]{:S(2)}, u32[]{:S(2)}) %collective-permute-start.6) | collective-permute-done | bytes 655392 | tf_op jit(solution)/shard_map/ppermute | solution.py:298
  93.4 6.1 %all-to-all-done.1.refs_4_.refs_6_ = f32[16,96,128]{2,1,0:T(8,128)S(1)} async-done(((f32[16,96,128]{2,1,0:T(8,128)}), f32[16,96,128]{2,1,0:T(8,128)S(1)}, u32[]{:S(2)}, u32[]{:S(2)}) %all-to-all-start.1) | async-done | bytes 786464 | tf_op jit(solution)/shard_map/all_to_all | solution.py:301
  99.5 2.0 %exchange.6 = f32[16,96,128]{2,1,0:T(8,128)S(1)} custom-call(s32[2]{0:T(128)S(1)} %pad_add_fusion.ids_ref.refs_0_, s32[16]{0:T(128)S(1)} %reshape.19.refs_1_, f32[8]{0:T(128)S(1)} %copy-done.11, s32[8]{0:T(128)S(1)} %bitcast.33, f32[16,96,128]{2,1,0:T(8,128)S(1)} %all-to-all-done.1.refs_4_.refs_6_, f32[768,128]{1,0:T(8,128)S(1)} %broadcast_in_dim.27.refs_5_.refs_4_, ...), custom_call_target="tpu_custom_call" | custom-call | flops 335544320 | bytes 1572864 | tf_op jit(solution)/shard_map/exchange/pallas_call | solution.py:180
  101.5 27.1 %all_to_all.20.refs_4_.refs_7_ = f32[16,96,128]{2,1,0:T(8,128)S(1)} all-to-all(f32[16,96,128]{2,1,0:T(8,128)S(1)} %exchange.6), channel_id=1, replica_groups=mesh['occ'=8,'aux'=16,'vir'=4] {'aux'}, dimensions={0} | all-to-all | bytes 1572864 | tf_op jit(solution)/shard_map/all_to_all | solution.py:301
  128.6 1.3 exchange.7
  129.9 4.3 %all-to-all-start.3 = ((f32[16,32,128]{2,1,0:T(8,128)}), f32[16,32,128]{2,1,0:T(8,128)S(1)}, u32[]{:S(2)}, u32[]{:S(2)}) async-start(f32[16,32,128]{2,1,0:T(8,128)} %exchange.7), calls=%async_computation.3 | async-start | bytes 524288 | tf_op jit(solution)/shard_map/all_to_all | solution.py:301
  134.3 0.7 energy.2
  135.0 0.0 copy-done.6
  135.0 1.1 copy-done.9
  136.1 3.2 %gamma.2.refs_4_ = f32[632,768]{1,0:T(8,128)S(1)} custom-call(s32[2]{0:T(128)S(1)} %pad_add_fusion.ids_ref.refs_0_, s32[16]{0:T(128)S(1)} %reshape.19.refs_1_, f32[8]{0:T(128)S(1)} %copy-done.11, s32[8]{0:T(128)S(1)} %bitcast.36, f32[16,96,128]{2,1,0:T(8,128)S(1)} %all-to-all-done.1.refs_4_.refs_6_, f32[1,640,256]{2,1,0:T(8,128)} %collective-permute-done.refs_5_, ...), custom_call_target="tpu_custom_call" | custom-call | flops 994050048 | bytes 3883008 | tf_op jit(solution)/shard_map/gamma/pallas_call | solution.py:267
  139.4 0.0 copy-start.2
  139.4 1.3 copy-done.2
  140.6 3.9 %all-to-all-done.3.refs_6_.refs_5_ = f32[16,32,128]{2,1,0:T(8,128)S(1)} async-done(((f32[16,32,128]{2,1,0:T(8,128)}), f32[16,32,128]{2,1,0:T(8,128)S(1)}, u32[]{:S(2)}, u32[]{:S(2)}) %all-to-all-start.3) | async-done | bytes 262176 | tf_op jit(solution)/shard_map/all_to_all | solution.py:301
  144.6 0.6 energy.3
  145.2 0.1 maximum_reduce_fusion
  145.3 0.1 stack.47
  145.4 12.0 %psum.7 = f32[8]{0:T(128)S(1)} all-reduce(f32[8]{0:T(128)S(1)} %maximum_reduce_fusion), channel_id=1, replica_groups=mesh['occ'=8,'aux'=16,'vir'=4] {'vir'}, use_global_device_ids=true, to_apply=%region_1.0 | all-reduce | flops 8 | bytes 64 | tf_op jit(solution)/shard_map/psum | solution.py:326
  157.4 0.6 select_reduce_fusion
  158.0 1.5 copy-done.3
  159.5 3.3 %gamma.3 = f32[632,768]{1,0:T(8,128)} custom-call(s32[2]{0:T(128)S(1)} %pad_add_fusion.ids_ref.refs_0_, s32[16]{0:T(128)S(1)} %reshape.19.refs_1_, f32[8]{0:T(128)S(1)} %copy-done.11, s32[8]{0:T(128)S(1)} %bitcast.38, f32[632,768]{1,0:T(8,128)S(1)} %copy-done.3, f32[16,32,128]{2,1,0:T(8,128)S(1)} %all-to-all-done.3.refs_6_.refs_5_, ...), custom_call_target="tpu_custom_call" | custom-call | flops 331350016 | bytes 3883008 | tf_op jit(solution)/shard_map/gamma/pallas_call | solution.py:267
  (13 shorter events, 0.0 us)
Async XLA Ops:
  13.7 1.5 copy-start
  15.2 18.4 %copy-start.15 = (s32[1,8,1,2]{1,3,2,0:T(2,128)S(1)}, s32[1,8,1,2]{1,3,2,0:T(2,128)}, u32[]{:S(2)}) copy-start(s32[1,8,1,2]{1,3,2,0:T(2,128)} %param.8) | copy-start | bytes 196
  19.0 0.9 copy-start.7
  19.9 13.7 %copy-start.13 = (f32[1,640,256]{2,1,0:T(8,128)}, f32[1,640,256]{2,1,0:T(8,128)S(1)}, u32[]{:S(2)}) copy-start(f32[1,640,256]{2,1,0:T(8,128)S(1)} %get-tuple-element.56) | copy-start | bytes 1966084
  19.9 13.7 %copy-start.14 = (f32[1,640,256]{2,1,0:T(8,128)}, f32[1,640,256]{2,1,0:T(8,128)S(1)}, u32[]{:S(2)}) copy-start(f32[1,640,256]{2,1,0:T(8,128)S(1)} %get-tuple-element.55) | copy-start | bytes 1966084
  19.9 16.0 %collective-permute-start = (f32[1,640,256]{2,1,0:T(8,128)}, f32[1,640,256]{2,1,0:T(8,128)}, u32[]{:S(2)}, u32[]{:S(2)}) collective-permute-start(f32[1,640,256]{2,1,0:T(8,128)} %get-tuple-element.40), channel_id=1, source_target_pairs={{0,64},{64,0},{128,192},{192,128},{256,320},{320,256},{384,448},{4... | collective-permute-start | bytes 1966088 | tf_op jit(solution)/shard_map/ppermute | solution.py:298
  22.1 26.0 %collective-permute-start.1 = (f32[1,640,256]{2,1,0:T(8,128)}, f32[1,640,256]{2,1,0:T(8,128)S(1)}, u32[]{:S(2)}, u32[]{:S(2)}) collective-permute-start(f32[1,640,256]{2,1,0:T(8,128)} %get-tuple-element.42), channel_id=1, source_target_pairs={{0,128},{64,192},{128,256},{192,320},{256,384},{320,448},{384,0},{... | collective-permute-start | bytes 1966088 | tf_op jit(solution)/shard_map/ppermute | solution.py:298
  25.3 22.8 %collective-permute-start.2 = (f32[1,640,256]{2,1,0:T(8,128)}, f32[1,640,256]{2,1,0:T(8,128)}, u32[]{:S(2)}, u32[]{:S(2)}) collective-permute-start(f32[1,640,256]{2,1,0:T(8,128)} %get-tuple-element.43), channel_id=1, source_target_pairs={{0,384},{64,448},{128,0},{192,64},{256,128},{320,192},{384,256},{4... | collective-permute-start | bytes 1966088 | tf_op jit(solution)/shard_map/ppermute | solution.py:298
  27.9 26.5 %collective-permute-start.3 = (f32[1,640,256]{2,1,0:T(8,128)}, f32[1,640,256]{2,1,0:T(8,128)}, u32[]{:S(2)}, u32[]{:S(2)}) collective-permute-start(f32[1,640,256]{2,1,0:T(8,128)} %get-tuple-element.44), channel_id=1, source_target_pairs={{0,192},{64,128},{128,320},{192,256},{256,448},{320,384},{384,64},... | collective-permute-start | bytes 1966088 | tf_op jit(solution)/shard_map/ppermute | solution.py:298
  31.6 26.6 %collective-permute-start.4 = (f32[1,640,256]{2,1,0:T(8,128)}, f32[1,640,256]{2,1,0:T(8,128)}, u32[]{:S(2)}, u32[]{:S(2)}) collective-permute-start(f32[1,640,256]{2,1,0:T(8,128)} %get-tuple-element.45), channel_id=1, source_target_pairs={{0,448},{64,384},{128,64},{192,0},{256,192},{320,128},{384,320},{4... | collective-permute-start | bytes 1966088 | tf_op jit(solution)/shard_map/ppermute | solution.py:298
  33.6 1.5 copy-start.1
  35.2 0.7 copy-start.11
  35.2 0.7 copy-start.12
  35.9 1.1 copy-start.8
  39.4 18.9 %all-to-all-start = ((f32[16,32,128]{2,1,0:T(8,128)}), f32[16,32,128]{2,1,0:T(8,128)S(1)}, u32[]{:S(2)}, u32[]{:S(2)}) async-start(f32[16,32,128]{2,1,0:T(8,128)} %exchange.4), calls=%async_computation | async-start | bytes 524288 | tf_op jit(solution)/shard_map/all_to_all | solution.py:301
  48.1 17.7 %copy-start.10 = (f32[768]{0:T(1024)S(1)}, f32[768]{0:T(1024)}, u32[]{:S(2)}) copy-start(f32[768]{0:T(1024)} %param.7) | copy-start | bytes 9220
  58.2 10.3 %copy-start.5 = (f32[1,640,256]{2,1,0:T(8,128)}, f32[1,640,256]{2,1,0:T(8,128)S(1)}, u32[]{:S(2)}) copy-start(f32[1,640,256]{2,1,0:T(8,128)S(1)} %get-tuple-element.51.refs_8_) | copy-start | bytes 1966084
  58.2 21.3 %collective-permute-start.5 = (f32[1,640,256]{2,1,0:T(8,128)}, f32[1,640,256]{2,1,0:T(8,128)}, u32[]{:S(2)}, u32[]{:S(2)}) collective-permute-start(f32[1,640,256]{2,1,0:T(8,128)} %copy-done.14), channel_id=1, source_target_pairs={{0,256},{64,320},{128,384},{192,448},{256,0},{320,64},{384,128},{4... | collective-permute-start | bytes 1966088 | tf_op jit(solution)/shard_map/ppermute | solution.py:298
  61.4 32.0 %collective-permute-start.6 = (f32[1,640,256]{2,1,0:T(8,128)}, f32[1,640,256]{2,1,0:T(8,128)}, u32[]{:S(2)}, u32[]{:S(2)}) collective-permute-start(f32[1,640,256]{2,1,0:T(8,128)} %copy-done.13), channel_id=1, source_target_pairs={{0,320},{64,256},{128,448},{192,384},{256,64},{320,0},{384,192},{4... | collective-permute-start | bytes 1966088 | tf_op jit(solution)/shard_map/ppermute | solution.py:298
  68.5 0.9 copy-start.4
  69.4 30.1 %all-to-all-start.1 = ((f32[16,96,128]{2,1,0:T(8,128)}), f32[16,96,128]{2,1,0:T(8,128)S(1)}, u32[]{:S(2)}, u32[]{:S(2)}) async-start(f32[16,96,128]{2,1,0:T(8,128)} %copy-done.4), calls=%async_computation.1 | async-start | bytes 1572864 | tf_op jit(solution)/shard_map/all_to_all | solution.py:301
  128.6 6.4 %copy-start.6 = (f32[1,640,256]{2,1,0:T(8,128)S(1)}, f32[1,640,256]{2,1,0:T(8,128)}, u32[]{:S(2)}) copy-start(f32[1,640,256]{2,1,0:T(8,128)} %copy-done.5) | copy-start | bytes 1966084
  129.9 14.7 %all-to-all-start.3 = ((f32[16,32,128]{2,1,0:T(8,128)}), f32[16,32,128]{2,1,0:T(8,128)S(1)}, u32[]{:S(2)}, u32[]{:S(2)}) async-start(f32[16,32,128]{2,1,0:T(8,128)} %exchange.7), calls=%async_computation.3 | async-start | bytes 524288 | tf_op jit(solution)/shard_map/all_to_all | solution.py:301
  135.0 1.1 copy-start.9
  139.4 1.3 copy-start.2
  158.0 1.5 copy-start.3

commit v10 on v9

--- a/solution.py
+++ b/solution.py
@@ -300,14 +300,17 @@
     def sent(returned, group):
         return lax.all_to_all(exchange(scalars, returned, group), "aux", 0, 0)
 
+    mate, own = pick(ids, all_pairs, block, EARLY, (1,) * 2, padded)
     near = pick(ids, all_pairs, block, NEAR, (1,) * 4, padded)
-    later_ids, *near = lax.optimization_barrier((ids, *near))
+    left_split = left(block, padded)
+    mate, left_split, *near = lax.optimization_barrier((mate, left_split, *near))
     near = held(70, *[moved(tiles, *shift) for tiles, shift in zip(near, NEAR)])
-    mate, own, *far = pick(later_ids, all_pairs, block, EARLY + FAR, (1,) * 4, padded)
     early_rights = [(moved(mate, 0, 1), 0), (own, 0)]
-    left_split = left(block, padded)
-
-    early = sent(None, (EARLY, left_split, early_rights))
+
+    operand = exchange(scalars, None, (EARLY, left_split, early_rights))
+    later_ids, operand = lax.optimization_barrier((ids, operand))
+    far = list(pick(later_ids, all_pairs, block, FAR, (1,) * 2, padded))
+    early = lax.all_to_all(operand, "aux", 0, 0)
     far[0], far[1], early, *near = lax.optimization_barrier((*far, early, *near))
     far = held(70, *[moved(tiles, *shift) for tiles, shift in zip(far, FAR)])
     near_rights = [(tiles, 0) for tiles in near]

time: 164 us -> 166 us (1.012)
  waiting for transfers between devices: 35.4 us -> 37.6 us
    all_to_all x3 -> x2, starting transfers between devices: 21.7 us -> 13 us  [sent(): return lax.all_to_all(exchange(scalars, returned, group), 'aux', 0, 0)]
    all_to_all x0 -> x1, starting transfers between devices: none -> 8.72 us  [per_device(): early = lax.all_to_all(operand, 'aux', 0, 0)]
    ppermute x7, waiting for transfers between devices: 25.4 us -> 27.6 us  [moved(): return lax.ppermute(tiles, 'occ', route)]
    pallas_call x2 -> x3, Pallas kernels: 3.77 us -> 4.37 us  [pick(): pl.pallas_call(functools.partial(pick_kernel, shifts), out_shape=[jax.Sha...]
    all_to_all x3 -> x2, waiting for transfers between devices: 10 us -> 10.1 us  [sent(): return lax.all_to_all(exchange(scalars, returned, group), 'aux', 0, 0)]
  transfers between devices with their start and end apart: 10 -> 10, of which waited for: 6 -> 7; matrix products, arithmetic and copies ran while one was open for 0% -> 0% of each run, Pallas kernels for 6% -> 6%
where the time goes in v10:
time: 166 us; the launch traced here: 165 us
  blocking collectives  51.8 us (31%)
  starting transfers between devices  42.9 us (26%)
  waiting for transfers between devices  37.6 us (23%)
  Pallas kernels  21 us (13%)
  local copies, waits for them, and re-layouts  9.99 us (6%)
    ppermute x7, waiting for transfers between devices, moved(): return lax.ppermute(tiles, 'occ', route)  27.6 us
    all_to_all x1, blocking collectives, sent(): return lax.all_to_all(exchange(scalars, returned, group), 'aux', 0, 0)  27.1 us
    ppermute x7, starting transfers between devices, moved(): return lax.ppermute(tiles, 'occ', route)  21.2 us
    all_to_all x2, starting transfers between devices, sent(): return lax.all_to_all(exchange(scalars, returned, group), 'aux', 0, 0)  13 us
    all_gather x1, blocking collectives, per_device(): all_pairs = lax.all_gather(tile_pairs[0, :, 0, :], 'occ').reshape(-1)  12.7 us
    psum x1, blocking collectives, per_device(): energy, last = lax.optimization_barrier((lax.psum(energy, 'vir'), last))  12 us
    all_to_all x2, waiting for transfers between devices, sent(): return lax.all_to_all(exchange(scalars, returned, group), 'aux', 0, 0)  10.1 us
    unnamed x33, local copies, waits for them, and re-layouts  9.41 us
  transfers between devices with their start and end apart: 10, of which 7 were waited for; matrix products, arithmetic and copies ran while one was open for 0% of the time, Pallas kernels for 6%

profile of v10, /device:TPU:6, one launch (start us, length us, event | category | flops | bytes accessed | tf_op | source)
XLA Modules:
  0.0 165.1 jit_solution(18003842547835411438)
XLA Ops:
  0.6 12.7 %all-gather = s32[8,8,1,2]{1,3,2,0:T(2,128)S(1)} all-gather(s32[1,8,1,2]{1,3,2,0:T(2,128)} %param.8), channel_id=2, replica_groups=mesh['occ'=8,'aux'=16,'vir'=4] {'occ'}, dimensions={0}, use_global_device_ids=true | all-gather | bytes 576 | tf_op jit(solution)/shard_map/all_gather | solution.py:290
  13.3 0.1 copy.20
  13.4 0.1 reshape.21.pairs_ref
  13.6 0.1 pad_add_fusion.ids_ref.refs_0_
  13.7 1.5 copy-done
  15.2 2.2 %pick.4 = (f32[1,640,256]{2,1,0:T(8,128)}, f32[1,640,256]{2,1,0:T(8,128)}, f32[1,640,256]{2,1,0:T(8,128)}, f32[1,640,256]{2,1,0:T(8,128)}) custom-call(s32[2]{0:T(128)S(1)} %pad_add_fusion.ids_ref.refs_0_, s32[128]{0:T(128)S(1)} %reshape.21.pairs_ref, f32[632,768]{1,0:T(8,128)S(1)} %bitcast.23), custom_call_target="tpu_custom_call" | custom-call | bytes 5242880 | tf_op jit(solution)/shard_map/pick/pallas_call | solution.py:60
  17.4 1.5 pick.3
  18.8 0.0 copy-start.7
  18.8 0.0 copy-start.15
  18.9 0.0 copy-start.11
  18.9 0.0 copy-start.12
  18.9 0.6 left.1.refs_4_.refs_7_
  19.5 0.2 copy-done.7
  19.7 2.2 %collective-permute-start = (f32[1,640,256]{2,1,0:T(8,128)}, f32[1,640,256]{2,1,0:T(8,128)}, u32[]{:S(2)}, u32[]{:S(2)}) collective-permute-start(f32[1,640,256]{2,1,0:T(8,128)} %get-tuple-element.42), channel_id=1, source_target_pairs={{0,64},{64,0},{128,192},{192,128},{256,320},{320,256},{384,448},{4... | collective-permute-start | bytes 1966088 | tf_op jit(solution)/shard_map/ppermute | solution.py:298
  21.9 3.2 %collective-permute-start.1 = (f32[1,640,256]{2,1,0:T(8,128)}, f32[1,640,256]{2,1,0:T(8,128)S(1)}, u32[]{:S(2)}, u32[]{:S(2)}) collective-permute-start(f32[1,640,256]{2,1,0:T(8,128)} %get-tuple-element.48), channel_id=1, source_target_pairs={{0,128},{64,192},{128,256},{192,320},{256,384},{320,448},{384,0},{... | collective-permute-start | bytes 1966088 | tf_op jit(solution)/shard_map/ppermute | solution.py:298
  25.1 2.6 %collective-permute-start.2 = (f32[1,640,256]{2,1,0:T(8,128)}, f32[1,640,256]{2,1,0:T(8,128)}, u32[]{:S(2)}, u32[]{:S(2)}) collective-permute-start(f32[1,640,256]{2,1,0:T(8,128)} %get-tuple-element.49), channel_id=1, source_target_pairs={{0,384},{64,448},{128,0},{192,64},{256,128},{320,192},{384,256},{4... | collective-permute-start | bytes 1966088 | tf_op jit(solution)/shard_map/ppermute | solution.py:298
  27.8 3.7 %collective-permute-start.3 = (f32[1,640,256]{2,1,0:T(8,128)}, f32[1,640,256]{2,1,0:T(8,128)}, u32[]{:S(2)}, u32[]{:S(2)}) collective-permute-start(f32[1,640,256]{2,1,0:T(8,128)} %get-tuple-element.50), channel_id=1, source_target_pairs={{0,192},{64,128},{128,320},{192,256},{256,448},{320,384},{384,64},... | collective-permute-start | bytes 1966088 | tf_op jit(solution)/shard_map/ppermute | solution.py:298
  31.4 1.9 %collective-permute-start.4 = (f32[1,640,256]{2,1,0:T(8,128)}, f32[1,640,256]{2,1,0:T(8,128)}, u32[]{:S(2)}, u32[]{:S(2)}) collective-permute-start(f32[1,640,256]{2,1,0:T(8,128)} %get-tuple-element.51), channel_id=1, source_target_pairs={{0,448},{64,384},{128,64},{192,0},{256,192},{320,128},{384,320},{4... | collective-permute-start | bytes 1966088 | tf_op jit(solution)/shard_map/ppermute | solution.py:298
  33.4 0.0 copy-done.15
  33.4 0.1 copy.19
  33.5 0.1 reshape.19.refs_1_
  33.5 0.0 collective-permute-done.refs_5_
  33.5 0.0 copy-done.11
  33.6 1.1 copy-done.8
  34.7 2.4 %exchange.4 = f32[16,32,128]{2,1,0:T(8,128)} custom-call(s32[2]{0:T(128)S(1)} %pad_add_fusion.ids_ref.refs_0_, s32[16]{0:T(128)S(1)} %reshape.19.refs_1_, f32[8]{0:T(128)S(1)} %copy-done.11, s32[8]{0:T(128)S(1)} %bitcast.32, bf16[6,256,640]{2,1,0:T(8,128)(2,1)S(1)} %left.1.refs_4_.refs_7_, f32[1,640,256]{2,1,0:T(8,128)} %collective-permute-done.refs_5_, ...), custom_call_target="tpu_custom_call" | custom-call | flops 335544320 | bytes 524288 | tf_op jit(solution)/shard_map/exchange/pallas_call | solution.py:180
  37.1 8.7 %all-to-all-start = ((f32[16,32,128]{2,1,0:T(8,128)}), f32[16,32,128]{2,1,0:T(8,128)S(1)}, u32[]{:S(2)}, u32[]{:S(2)}) async-start(f32[16,32,128]{2,1,0:T(8,128)} %exchange.4), calls=%async_computation | async-start | bytes 524288 | tf_op jit(solution)/shard_map/all_to_all | solution.py:313
  45.8 0.0 copy-start.1
  45.8 0.0 collective-permute-done.1.refs_0_
  45.8 0.4 collective-permute-done.2.refs_1_
  46.2 8.1 %collective-permute-done.3.refs_2_ = f32[1,640,256]{2,1,0:T(8,128)} collective-permute-done((f32[1,640,256]{2,1,0:T(8,128)}, f32[1,640,256]{2,1,0:T(8,128)}, u32[]{:S(2)}, u32[]{:S(2)}) %collective-permute-start.3) | collective-permute-done | bytes 655392 | tf_op jit(solution)/shard_map/ppermute | solution.py:298
  54.2 3.8 %collective-permute-done.4.refs_3_ = f32[1,640,256]{2,1,0:T(8,128)} collective-permute-done((f32[1,640,256]{2,1,0:T(8,128)}, f32[1,640,256]{2,1,0:T(8,128)}, u32[]{:S(2)}, u32[]{:S(2)}) %collective-permute-start.4) | collective-permute-done | bytes 655392 | tf_op jit(solution)/shard_map/ppermute | solution.py:298
  58.1 0.8 pick.5
  58.9 0.0 copy-start.13
  58.9 0.8 copy-done.13
  59.7 0.9 copy-done.14
  60.6 0.0 all-to-all-done.refs_4_
  60.6 2.6 %collective-permute-start.5 = (f32[1,640,256]{2,1,0:T(8,128)}, f32[1,640,256]{2,1,0:T(8,128)}, u32[]{:S(2)}, u32[]{:S(2)}) collective-permute-start(f32[1,640,256]{2,1,0:T(8,128)} %copy-done.14), channel_id=1, source_target_pairs={{0,256},{64,320},{128,384},{192,448},{256,0},{320,64},{384,128},{4... | collective-permute-start | bytes 1966088 | tf_op jit(solution)/shard_map/ppermute | solution.py:298
  63.2 4.9 %collective-permute-start.6 = (f32[1,640,256]{2,1,0:T(8,128)}, f32[1,640,256]{2,1,0:T(8,128)}, u32[]{:S(2)}, u32[]{:S(2)}) collective-permute-start(f32[1,640,256]{2,1,0:T(8,128)} %copy-done.13), channel_id=1, source_target_pairs={{0,320},{64,256},{128,448},{192,384},{256,64},{320,0},{384,192},{4... | collective-permute-start | bytes 1966088 | tf_op jit(solution)/shard_map/ppermute | solution.py:298
  68.1 0.2 broadcast_in_dim.27.refs_5_.refs_4_
  68.3 2.5 %exchange.5 = f32[16,96,128]{2,1,0:T(8,128)S(1)} custom-call(s32[2]{0:T(128)S(1)} %pad_add_fusion.ids_ref.refs_0_, s32[16]{0:T(128)S(1)} %reshape.19.refs_1_, f32[8]{0:T(128)S(1)} %copy-done.11, s32[8]{0:T(128)S(1)} %bitcast.33, f32[16,32,128]{2,1,0:T(8,128)S(1)} %all-to-all-done.refs_4_, f32[768,128]{1,0:T(8,128)S(1)} %broadcast_in_dim.27.refs_5_.refs_4_, ...), custom_call_target="tpu_custom_call" | custom-call | flops 671088640 | bytes 1572864 | tf_op jit(solution)/shard_map/exchange/pallas_call | solution.py:180
  70.8 0.0 copy-start.4
  70.9 0.9 copy-done.4
  71.7 8.7 %all-to-all-start.1 = ((f32[16,96,128]{2,1,0:T(8,128)}), f32[16,96,128]{2,1,0:T(8,128)S(1)}, u32[]{:S(2)}, u32[]{:S(2)}) async-start(f32[16,96,128]{2,1,0:T(8,128)} %copy-done.4), calls=%async_computation.1 | async-start | bytes 1572864 | tf_op jit(solution)/shard_map/all_to_all | solution.py:301
  80.5 1.4 collective-permute-done.5.refs_0_
  81.9 13.9 %collective-permute-done.6.refs_1_ = f32[1,640,256]{2,1,0:T(8,128)} collective-permute-done((f32[1,640,256]{2,1,0:T(8,128)}, f32[1,640,256]{2,1,0:T(8,128)}, u32[]{:S(2)}, u32[]{:S(2)}) %collective-permute-start.6) | collective-permute-done | bytes 655392 | tf_op jit(solution)/shard_map/ppermute | solution.py:298
  95.8 6.1 %all-to-all-done.1.refs_4_.refs_6_ = f32[16,96,128]{2,1,0:T(8,128)S(1)} async-done(((f32[16,96,128]{2,1,0:T(8,128)}), f32[16,96,128]{2,1,0:T(8,128)S(1)}, u32[]{:S(2)}, u32[]{:S(2)}) %all-to-all-start.1) | async-done | bytes 786464 | tf_op jit(solution)/shard_map/all_to_all | solution.py:301
  101.8 2.0 %exchange.6 = f32[16,96,128]{2,1,0:T(8,128)S(1)} custom-call(s32[2]{0:T(128)S(1)} %pad_add_fusion.ids_ref.refs_0_, s32[16]{0:T(128)S(1)} %reshape.19.refs_1_, f32[8]{0:T(128)S(1)} %copy-done.11, s32[8]{0:T(128)S(1)} %bitcast.34, f32[16,96,128]{2,1,0:T(8,128)S(1)} %all-to-all-done.1.refs_4_.refs_6_, f32[768,128]{1,0:T(8,128)S(1)} %broadcast_in_dim.27.refs_5_.refs_4_, ...), custom_call_target="tpu_custom_call" | custom-call | flops 335544320 | bytes 1572864 | tf_op jit(solution)/shard_map/exchange/pallas_call | solution.py:180
  103.8 27.1 %all_to_all.20.refs_4_.refs_7_ = f32[16,96,128]{2,1,0:T(8,128)S(1)} all-to-all(f32[16,96,128]{2,1,0:T(8,128)S(1)} %exchange.6), channel_id=1, replica_groups=mesh['occ'=8,'aux'=16,'vir'=4] {'aux'}, dimensions={0} | all-to-all | bytes 1572864 | tf_op jit(solution)/shard_map/all_to_all | solution.py:301
  130.9 1.3 exchange.7
  132.2 4.3 %all-to-all-start.3 = ((f32[16,32,128]{2,1,0:T(8,128)}), f32[16,32,128]{2,1,0:T(8,128)S(1)}, u32[]{:S(2)}, u32[]{:S(2)}) async-start(f32[16,32,128]{2,1,0:T(8,128)} %exchange.7), calls=%async_computation.3 | async-start | bytes 524288 | tf_op jit(solution)/shard_map/all_to_all | solution.py:301
  136.6 0.7 energy.2
  137.3 0.0 copy-done.6
  137.4 1.1 copy-done.9
  138.4 3.2 %gamma.2.refs_4_ = f32[632,768]{1,0:T(8,128)S(1)} custom-call(s32[2]{0:T(128)S(1)} %pad_add_fusion.ids_ref.refs_0_, s32[16]{0:T(128)S(1)} %reshape.19.refs_1_, f32[8]{0:T(128)S(1)} %copy-done.11, s32[8]{0:T(128)S(1)} %bitcast.37, f32[16,96,128]{2,1,0:T(8,128)S(1)} %all-to-all-done.1.refs_4_.refs_6_, f32[1,640,256]{2,1,0:T(8,128)} %collective-permute-done.refs_5_, ...), custom_call_target="tpu_custom_call" | custom-call | flops 994050048 | bytes 3883008 | tf_op jit(solution)/shard_map/gamma/pallas_call | solution.py:267
  141.7 0.0 copy-start.2
  141.7 1.3 copy-done.2
  142.9 4.0 %all-to-all-done.3.refs_6_.refs_5_ = f32[16,32,128]{2,1,0:T(8,128)S(1)} async-done(((f32[16,32,128]{2,1,0:T(8,128)}), f32[16,32,128]{2,1,0:T(8,128)S(1)}, u32[]{:S(2)}, u32[]{:S(2)}) %all-to-all-start.3) | async-done | bytes 262176 | tf_op jit(solution)/shard_map/all_to_all | solution.py:301
  146.9 0.6 energy.3
  147.5 0.1 maximum_reduce_fusion
  147.6 0.1 stack.47
  147.7 12.0 %psum.7 = f32[8]{0:T(128)S(1)} all-reduce(f32[8]{0:T(128)S(1)} %maximum_reduce_fusion), channel_id=1, replica_groups=mesh['occ'=8,'aux'=16,'vir'=4] {'vir'}, use_global_device_ids=true, to_apply=%region_1.0 | all-reduce | flops 8 | bytes 64 | tf_op jit(solution)/shard_map/psum | solution.py:329
  159.7 0.6 select_reduce_fusion
  160.3 1.5 copy-done.3
  161.8 3.2 %gamma.3 = f32[632,768]{1,0:T(8,128)} custom-call(s32[2]{0:T(128)S(1)} %pad_add_fusion.ids_ref.refs_0_, s32[16]{0:T(128)S(1)} %reshape.19.refs_1_, f32[8]{0:T(128)S(1)} %copy-done.11, s32[8]{0:T(128)S(1)} %bitcast.39, f32[632,768]{1,0:T(8,128)S(1)} %copy-done.3, f32[16,32,128]{2,1,0:T(8,128)S(1)} %all-to-all-done.3.refs_6_.refs_5_, ...), custom_call_target="tpu_custom_call" | custom-call | flops 331350016 | bytes 3883008 | tf_op jit(solution)/shard_map/gamma/pallas_call | solution.py:267
  (14 shorter events, 0.0 us)
Async XLA Ops:
  13.7 1.5 copy-start
  18.8 0.9 copy-start.7
  18.8 14.5 %copy-start.15 = (s32[1,8,1,2]{1,3,2,0:T(2,128)S(1)}, s32[1,8,1,2]{1,3,2,0:T(2,128)}, u32[]{:S(2)}) copy-start(s32[1,8,1,2]{1,3,2,0:T(2,128)} %param.8) | copy-start | bytes 196
  18.9 14.7 %copy-start.11 = (f32[8]{0:T(128)S(1)}, f32[8]{0:T(128)}, u32[]{:S(2)}) copy-start(f32[8]{0:T(128)} %refs_2_.15) | copy-start | bytes 100
  18.9 14.7 %copy-start.12 = (s32[1,8]{1,0:T(1,128)S(1)}, s32[1,8]{1,0:T(1,128)}, u32[]{:S(2)}) copy-start(s32[1,8]{1,0:T(1,128)} %param.9) | copy-start | bytes 100
  19.7 13.9 %collective-permute-start = (f32[1,640,256]{2,1,0:T(8,128)}, f32[1,640,256]{2,1,0:T(8,128)}, u32[]{:S(2)}, u32[]{:S(2)}) collective-permute-start(f32[1,640,256]{2,1,0:T(8,128)} %get-tuple-element.42), channel_id=1, source_target_pairs={{0,64},{64,0},{128,192},{192,128},{256,320},{320,256},{384,448},{4... | collective-permute-start | bytes 1966088 | tf_op jit(solution)/shard_map/ppermute | solution.py:298
  21.9 23.9 %collective-permute-start.1 = (f32[1,640,256]{2,1,0:T(8,128)}, f32[1,640,256]{2,1,0:T(8,128)S(1)}, u32[]{:S(2)}, u32[]{:S(2)}) collective-permute-start(f32[1,640,256]{2,1,0:T(8,128)} %get-tuple-element.48), channel_id=1, source_target_pairs={{0,128},{64,192},{128,256},{192,320},{256,384},{320,448},{384,0},{... | collective-permute-start | bytes 1966088 | tf_op jit(solution)/shard_map/ppermute | solution.py:298
  25.1 21.0 %collective-permute-start.2 = (f32[1,640,256]{2,1,0:T(8,128)}, f32[1,640,256]{2,1,0:T(8,128)}, u32[]{:S(2)}, u32[]{:S(2)}) collective-permute-start(f32[1,640,256]{2,1,0:T(8,128)} %get-tuple-element.49), channel_id=1, source_target_pairs={{0,384},{64,448},{128,0},{192,64},{256,128},{320,192},{384,256},{4... | collective-permute-start | bytes 1966088 | tf_op jit(solution)/shard_map/ppermute | solution.py:298
  27.8 26.5 %collective-permute-start.3 = (f32[1,640,256]{2,1,0:T(8,128)}, f32[1,640,256]{2,1,0:T(8,128)}, u32[]{:S(2)}, u32[]{:S(2)}) collective-permute-start(f32[1,640,256]{2,1,0:T(8,128)} %get-tuple-element.50), channel_id=1, source_target_pairs={{0,192},{64,128},{128,320},{192,256},{256,448},{320,384},{384,64},... | collective-permute-start | bytes 1966088 | tf_op jit(solution)/shard_map/ppermute | solution.py:298
  31.4 26.6 %collective-permute-start.4 = (f32[1,640,256]{2,1,0:T(8,128)}, f32[1,640,256]{2,1,0:T(8,128)}, u32[]{:S(2)}, u32[]{:S(2)}) collective-permute-start(f32[1,640,256]{2,1,0:T(8,128)} %get-tuple-element.51), channel_id=1, source_target_pairs={{0,448},{64,384},{128,64},{192,0},{256,192},{320,128},{384,320},{4... | collective-permute-start | bytes 1966088 | tf_op jit(solution)/shard_map/ppermute | solution.py:298
  33.6 1.1 copy-start.8
  37.1 23.5 %all-to-all-start = ((f32[16,32,128]{2,1,0:T(8,128)}), f32[16,32,128]{2,1,0:T(8,128)S(1)}, u32[]{:S(2)}, u32[]{:S(2)}) async-start(f32[16,32,128]{2,1,0:T(8,128)} %exchange.4), calls=%async_computation | async-start | bytes 524288 | tf_op jit(solution)/shard_map/all_to_all | solution.py:313
  45.8 12.3 %copy-start.1 = (f32[1,632,768]{2,1,0:T(8,128)S(1)}, f32[1,632,768]{2,1,0:T(8,128)}, u32[]{:S(2)}) copy-start(f32[1,632,768]{2,1,0:T(8,128)} %param.5) | copy-start | bytes 5824516
  58.1 12.8 %copy-start.5 = (f32[1,640,256]{2,1,0:T(8,128)}, f32[1,640,256]{2,1,0:T(8,128)S(1)}, u32[]{:S(2)}) copy-start(f32[1,640,256]{2,1,0:T(8,128)S(1)} %get-tuple-element.57.refs_8_) | copy-start | bytes 1966084
  58.1 10.1 %copy-start.10 = (f32[768]{0:T(1024)S(1)}, f32[768]{0:T(1024)}, u32[]{:S(2)}) copy-start(f32[768]{0:T(1024)} %param.7) | copy-start | bytes 9220
  58.9 0.8 copy-start.13
  59.7 0.9 copy-start.14
  60.6 21.3 %collective-permute-start.5 = (f32[1,640,256]{2,1,0:T(8,128)}, f32[1,640,256]{2,1,0:T(8,128)}, u32[]{:S(2)}, u32[]{:S(2)}) collective-permute-start(f32[1,640,256]{2,1,0:T(8,128)} %copy-done.14), channel_id=1, source_target_pairs={{0,256},{64,320},{128,384},{192,448},{256,0},{320,64},{384,128},{4... | collective-permute-start | bytes 1966088 | tf_op jit(solution)/shard_map/ppermute | solution.py:298
  63.2 32.5 %collective-permute-start.6 = (f32[1,640,256]{2,1,0:T(8,128)}, f32[1,640,256]{2,1,0:T(8,128)}, u32[]{:S(2)}, u32[]{:S(2)}) collective-permute-start(f32[1,640,256]{2,1,0:T(8,128)} %copy-done.13), channel_id=1, source_target_pairs={{0,320},{64,256},{128,448},{192,384},{256,64},{320,0},{384,192},{4... | collective-permute-start | bytes 1966088 | tf_op jit(solution)/shard_map/ppermute | solution.py:298
  70.8 0.9 copy-start.4
  71.7 30.1 %all-to-all-start.1 = ((f32[16,96,128]{2,1,0:T(8,128)}), f32[16,96,128]{2,1,0:T(8,128)S(1)}, u32[]{:S(2)}, u32[]{:S(2)}) async-start(f32[16,96,128]{2,1,0:T(8,128)} %copy-done.4), calls=%async_computation.1 | async-start | bytes 1572864 | tf_op jit(solution)/shard_map/all_to_all | solution.py:301
  130.9 6.4 %copy-start.6 = (f32[1,640,256]{2,1,0:T(8,128)S(1)}, f32[1,640,256]{2,1,0:T(8,128)}, u32[]{:S(2)}) copy-start(f32[1,640,256]{2,1,0:T(8,128)} %copy-done.5) | copy-start | bytes 1966084
  132.2 14.7 %all-to-all-start.3 = ((f32[16,32,128]{2,1,0:T(8,128)}), f32[16,32,128]{2,1,0:T(8,128)S(1)}, u32[]{:S(2)}, u32[]{:S(2)}) async-start(f32[16,32,128]{2,1,0:T(8,128)} %exchange.7), calls=%async_computation.3 | async-start | bytes 524288 | tf_op jit(solution)/shard_map/all_to_all | solution.py:301
  137.3 1.1 copy-start.9
  141.7 1.3 copy-start.2
  160.3 1.5 copy-start.3

commit v11 on v9

--- a/solution.py
+++ b/solution.py
@@ -301,11 +301,11 @@
         return lax.all_to_all(exchange(scalars, returned, group), "aux", 0, 0)
 
     near = pick(ids, all_pairs, block, NEAR, (1,) * 4, padded)
-    later_ids, *near = lax.optimization_barrier((ids, *near))
+    left_split = left(block, padded)
+    later_ids, left_split, *near = lax.optimization_barrier((ids, left_split, *near))
     near = held(70, *[moved(tiles, *shift) for tiles, shift in zip(near, NEAR)])
     mate, own, *far = pick(later_ids, all_pairs, block, EARLY + FAR, (1,) * 4, padded)
     early_rights = [(moved(mate, 0, 1), 0), (own, 0)]
-    left_split = left(block, padded)
 
     early = sent(None, (EARLY, left_split, early_rights))
     far[0], far[1], early, *near = lax.optimization_barrier((*far, early, *near))

time: 164 us -> 165 us (level)
  waiting for transfers between devices: 35.4 us -> 37.6 us
    ppermute x7, waiting for transfers between devices: 25.4 us -> 27.6 us  [moved(): return lax.ppermute(tiles, 'occ', route)]
    unnamed x33 -> x31, local copies, waits for them, and re-layouts: 9.87 us -> 9.38 us
  transfers between devices with their start and end apart: 10 -> 10, of which waited for: 6 -> 7; matrix products, arithmetic and copies ran while one was open for 0% -> 0% of each run, Pallas kernels for 6% -> 5%
where the time goes in v11:
time: 165 us; the launch traced here: 164 us
  blocking collectives  51.8 us (31%)
  starting transfers between devices  42.9 us (26%)
  waiting for transfers between devices  37.6 us (23%)
  Pallas kernels  20.4 us (12%)
  local copies, waits for them, and re-layouts  9.96 us (6%)
    ppermute x7, waiting for transfers between devices, moved(): return lax.ppermute(tiles, 'occ', route)  27.6 us
    all_to_all x1, blocking collectives, sent(): return lax.all_to_all(exchange(scalars, returned, group), 'aux', 0, 0)  27.1 us
    all_to_all x3, starting transfers between devices, sent(): return lax.all_to_all(exchange(scalars, returned, group), 'aux', 0, 0)  21.7 us
    ppermute x7, starting transfers between devices, moved(): return lax.ppermute(tiles, 'occ', route)  21.2 us
    all_gather x1, blocking collectives, per_device(): all_pairs = lax.all_gather(tile_pairs[0, :, 0, :], 'occ').reshape(-1)  12.7 us
    psum x1, blocking collectives, per_device(): energy, last = lax.optimization_barrier((lax.psum(energy, 'vir'), last))  12 us
    all_to_all x3, waiting for transfers between devices, sent(): return lax.all_to_all(exchange(scalars, returned, group), 'aux', 0, 0)  10 us
    unnamed x31, local copies, waits for them, and re-layouts  9.38 us
  transfers between devices with their start and end apart: 10, of which 7 were waited for; matrix products, arithmetic and copies ran while one was open for 0% of the time, Pallas kernels for 5%

profile of v11, /device:TPU:6, one launch (start us, length us, event | category | flops | bytes accessed | tf_op | source)
XLA Modules:
  0.0 164.4 jit_solution(3856467736519711293)
XLA Ops:
  0.6 12.7 %all-gather = s32[8,8,1,2]{1,3,2,0:T(2,128)S(1)} all-gather(s32[1,8,1,2]{1,3,2,0:T(2,128)} %param.8), channel_id=2, replica_groups=mesh['occ'=8,'aux'=16,'vir'=4] {'occ'}, dimensions={0}, use_global_device_ids=true | all-gather | bytes 576 | tf_op jit(solution)/shard_map/all_gather | solution.py:290
  13.3 0.1 copy.20
  13.4 0.1 reshape.21.pairs_ref
  13.6 0.0 copy-start
  13.6 1.5 copy-done
  15.1 0.6 left.1.refs_4_.refs_7_
  15.7 0.1 pad_add_fusion.ids_ref.refs_0_
  15.8 2.2 %pick.2 = (f32[1,640,256]{2,1,0:T(8,128)}, f32[1,640,256]{2,1,0:T(8,128)}, f32[1,640,256]{2,1,0:T(8,128)}, f32[1,640,256]{2,1,0:T(8,128)}) custom-call(s32[2]{0:T(128)S(1)} %pad_add_fusion.ids_ref.refs_0_, s32[128]{0:T(128)S(1)} %reshape.21.pairs_ref, f32[632,768]{1,0:T(8,128)S(1)} %bitcast.24), custom_call_target="tpu_custom_call" | custom-call | bytes 5242880 | tf_op jit(solution)/shard_map/pick/pallas_call | solution.py:60
  18.0 1.5 pick.3
  19.6 0.0 copy-start.6
  19.6 0.9 copy-done.6
  20.4 0.8 copy-done.12
  21.3 0.2 copy-done.13
  21.5 2.2 %collective-permute-start = (f32[1,640,256]{2,1,0:T(8,128)}, f32[1,640,256]{2,1,0:T(8,128)}, u32[]{:S(2)}, u32[]{:S(2)}) collective-permute-start(f32[1,640,256]{2,1,0:T(8,128)} %get-tuple-element.42), channel_id=1, source_target_pairs={{0,64},{64,0},{128,192},{192,128},{256,320},{320,256},{384,448},{4... | collective-permute-start | bytes 1966088 | tf_op jit(solution)/shard_map/ppermute | solution.py:298
  23.7 3.2 %collective-permute-start.1 = (f32[1,640,256]{2,1,0:T(8,128)}, f32[1,640,256]{2,1,0:T(8,128)S(1)}, u32[]{:S(2)}, u32[]{:S(2)}) collective-permute-start(f32[1,640,256]{2,1,0:T(8,128)} %get-tuple-element.44), channel_id=1, source_target_pairs={{0,128},{64,192},{128,256},{192,320},{256,384},{320,448},{384,0},{... | collective-permute-start | bytes 1966088 | tf_op jit(solution)/shard_map/ppermute | solution.py:298
  26.9 2.6 %collective-permute-start.2 = (f32[1,640,256]{2,1,0:T(8,128)}, f32[1,640,256]{2,1,0:T(8,128)}, u32[]{:S(2)}, u32[]{:S(2)}) collective-permute-start(f32[1,640,256]{2,1,0:T(8,128)} %get-tuple-element.45), channel_id=1, source_target_pairs={{0,384},{64,448},{128,0},{192,64},{256,128},{320,192},{384,256},{4... | collective-permute-start | bytes 1966088 | tf_op jit(solution)/shard_map/ppermute | solution.py:298
  29.6 3.7 %collective-permute-start.3 = (f32[1,640,256]{2,1,0:T(8,128)}, f32[1,640,256]{2,1,0:T(8,128)}, u32[]{:S(2)}, u32[]{:S(2)}) collective-permute-start(f32[1,640,256]{2,1,0:T(8,128)} %get-tuple-element.46), channel_id=1, source_target_pairs={{0,192},{64,128},{128,320},{192,256},{256,448},{320,384},{384,64},... | collective-permute-start | bytes 1966088 | tf_op jit(solution)/shard_map/ppermute | solution.py:298
  33.2 1.9 %collective-permute-start.4 = (f32[1,640,256]{2,1,0:T(8,128)}, f32[1,640,256]{2,1,0:T(8,128)}, u32[]{:S(2)}, u32[]{:S(2)}) collective-permute-start(f32[1,640,256]{2,1,0:T(8,128)} %get-tuple-element.47), channel_id=1, source_target_pairs={{0,448},{64,384},{128,64},{192,0},{256,192},{320,128},{384,320},{4... | collective-permute-start | bytes 1966088 | tf_op jit(solution)/shard_map/ppermute | solution.py:298
  35.2 0.0 copy-done.14
  35.2 0.1 copy.19
  35.2 0.1 reshape.19.refs_1_
  35.3 0.0 collective-permute-done.refs_5_
  35.3 0.0 copy-done.10
  35.3 0.0 copy-done.11
  35.4 0.0 copy-start.7
  35.4 1.1 copy-done.7
  36.4 2.4 %exchange.4 = f32[16,32,128]{2,1,0:T(8,128)} custom-call(s32[2]{0:T(128)S(1)} %pad_add_fusion.ids_ref.refs_0_, s32[16]{0:T(128)S(1)} %reshape.19.refs_1_, f32[8]{0:T(128)S(1)} %copy-done.10, s32[8]{0:T(128)S(1)} %bitcast.31, bf16[6,256,640]{2,1,0:T(8,128)(2,1)S(1)} %left.1.refs_4_.refs_7_, f32[1,640,256]{2,1,0:T(8,128)} %collective-permute-done.refs_5_, ...), custom_call_target="tpu_custom_call" | custom-call | flops 335544320 | bytes 524288 | tf_op jit(solution)/shard_map/exchange/pallas_call | solution.py:180
  38.8 8.7 %all-to-all-start = ((f32[16,32,128]{2,1,0:T(8,128)}), f32[16,32,128]{2,1,0:T(8,128)S(1)}, u32[]{:S(2)}, u32[]{:S(2)}) async-start(f32[16,32,128]{2,1,0:T(8,128)} %exchange.4), calls=%async_computation | async-start | bytes 524288 | tf_op jit(solution)/shard_map/all_to_all | solution.py:301
  47.6 0.0 copy-start.9
  47.6 0.0 collective-permute-done.1.refs_0_
  47.6 0.4 collective-permute-done.2.refs_1_
  48.0 8.1 %collective-permute-done.3.refs_2_ = f32[1,640,256]{2,1,0:T(8,128)} collective-permute-done((f32[1,640,256]{2,1,0:T(8,128)}, f32[1,640,256]{2,1,0:T(8,128)}, u32[]{:S(2)}, u32[]{:S(2)}) %collective-permute-start.3) | collective-permute-done | bytes 655392 | tf_op jit(solution)/shard_map/ppermute | solution.py:298
  56.0 3.8 %collective-permute-done.4.refs_3_ = f32[1,640,256]{2,1,0:T(8,128)} collective-permute-done((f32[1,640,256]{2,1,0:T(8,128)}, f32[1,640,256]{2,1,0:T(8,128)}, u32[]{:S(2)}, u32[]{:S(2)}) %collective-permute-start.4) | collective-permute-done | bytes 655392 | tf_op jit(solution)/shard_map/ppermute | solution.py:298
  59.9 0.0 all-to-all-done.refs_4_
  59.9 2.6 %collective-permute-start.5 = (f32[1,640,256]{2,1,0:T(8,128)}, f32[1,640,256]{2,1,0:T(8,128)}, u32[]{:S(2)}, u32[]{:S(2)}) collective-permute-start(f32[1,640,256]{2,1,0:T(8,128)} %copy-done.13), channel_id=1, source_target_pairs={{0,256},{64,320},{128,384},{192,448},{256,0},{320,64},{384,128},{4... | collective-permute-start | bytes 1966088 | tf_op jit(solution)/shard_map/ppermute | solution.py:298
  62.5 4.9 %collective-permute-start.6 = (f32[1,640,256]{2,1,0:T(8,128)}, f32[1,640,256]{2,1,0:T(8,128)}, u32[]{:S(2)}, u32[]{:S(2)}) collective-permute-start(f32[1,640,256]{2,1,0:T(8,128)} %copy-done.12), channel_id=1, source_target_pairs={{0,320},{64,256},{128,448},{192,384},{256,64},{320,0},{384,192},{4... | collective-permute-start | bytes 1966088 | tf_op jit(solution)/shard_map/ppermute | solution.py:298
  67.4 0.0 copy-done.9
  67.5 0.2 broadcast_in_dim.27.refs_5_.refs_4_
  67.6 2.5 %exchange.5 = f32[16,96,128]{2,1,0:T(8,128)S(1)} custom-call(s32[2]{0:T(128)S(1)} %pad_add_fusion.ids_ref.refs_0_, s32[16]{0:T(128)S(1)} %reshape.19.refs_1_, f32[8]{0:T(128)S(1)} %copy-done.10, s32[8]{0:T(128)S(1)} %bitcast.32, f32[16,32,128]{2,1,0:T(8,128)S(1)} %all-to-all-done.refs_4_, f32[768,128]{1,0:T(8,128)S(1)} %broadcast_in_dim.27.refs_5_.refs_4_, ...), custom_call_target="tpu_custom_call" | custom-call | flops 671088640 | bytes 1572864 | tf_op jit(solution)/shard_map/exchange/pallas_call | solution.py:180
  70.1 0.0 copy-done.4
  70.2 0.0 copy-start.3
  70.2 0.9 copy-done.3
  71.0 8.7 %all-to-all-start.1 = ((f32[16,96,128]{2,1,0:T(8,128)}), f32[16,96,128]{2,1,0:T(8,128)S(1)}, u32[]{:S(2)}, u32[]{:S(2)}) async-start(f32[16,96,128]{2,1,0:T(8,128)} %copy-done.3), calls=%async_computation.1 | async-start | bytes 1572864 | tf_op jit(solution)/shard_map/all_to_all | solution.py:301
  79.8 1.4 collective-permute-done.5.refs_0_
  81.2 13.9 %collective-permute-done.6.refs_1_ = f32[1,640,256]{2,1,0:T(8,128)} collective-permute-done((f32[1,640,256]{2,1,0:T(8,128)}, f32[1,640,256]{2,1,0:T(8,128)}, u32[]{:S(2)}, u32[]{:S(2)}) %collective-permute-start.6) | collective-permute-done | bytes 655392 | tf_op jit(solution)/shard_map/ppermute | solution.py:298
  95.1 6.1 %all-to-all-done.1.refs_4_.refs_6_ = f32[16,96,128]{2,1,0:T(8,128)S(1)} async-done(((f32[16,96,128]{2,1,0:T(8,128)}), f32[16,96,128]{2,1,0:T(8,128)S(1)}, u32[]{:S(2)}, u32[]{:S(2)}) %all-to-all-start.1) | async-done | bytes 786464 | tf_op jit(solution)/shard_map/all_to_all | solution.py:301
  101.1 2.0 %exchange.6 = f32[16,96,128]{2,1,0:T(8,128)S(1)} custom-call(s32[2]{0:T(128)S(1)} %pad_add_fusion.ids_ref.refs_0_, s32[16]{0:T(128)S(1)} %reshape.19.refs_1_, f32[8]{0:T(128)S(1)} %copy-done.10, s32[8]{0:T(128)S(1)} %bitcast.33, f32[16,96,128]{2,1,0:T(8,128)S(1)} %all-to-all-done.1.refs_4_.refs_6_, f32[768,128]{1,0:T(8,128)S(1)} %broadcast_in_dim.27.refs_5_.refs_4_, ...), custom_call_target="tpu_custom_call" | custom-call | flops 335544320 | bytes 1572864 | tf_op jit(solution)/shard_map/exchange/pallas_call | solution.py:180
  103.1 27.1 %all_to_all.20.refs_4_.refs_7_ = f32[16,96,128]{2,1,0:T(8,128)S(1)} all-to-all(f32[16,96,128]{2,1,0:T(8,128)S(1)} %exchange.6), channel_id=1, replica_groups=mesh['occ'=8,'aux'=16,'vir'=4] {'aux'}, dimensions={0} | all-to-all | bytes 1572864 | tf_op jit(solution)/shard_map/all_to_all | solution.py:301
  130.2 1.3 exchange.7
  131.6 4.3 %all-to-all-start.3 = ((f32[16,32,128]{2,1,0:T(8,128)}), f32[16,32,128]{2,1,0:T(8,128)S(1)}, u32[]{:S(2)}, u32[]{:S(2)}) async-start(f32[16,32,128]{2,1,0:T(8,128)} %exchange.7), calls=%async_computation.3 | async-start | bytes 524288 | tf_op jit(solution)/shard_map/all_to_all | solution.py:301
  135.9 0.7 energy.2
  136.7 0.0 copy-done.5
  136.7 1.1 copy-done.8
  137.8 3.2 %gamma.2.refs_4_ = f32[632,768]{1,0:T(8,128)S(1)} custom-call(s32[2]{0:T(128)S(1)} %pad_add_fusion.ids_ref.refs_0_, s32[16]{0:T(128)S(1)} %reshape.19.refs_1_, f32[8]{0:T(128)S(1)} %copy-done.10, s32[8]{0:T(128)S(1)} %bitcast.36, f32[16,96,128]{2,1,0:T(8,128)S(1)} %all-to-all-done.1.refs_4_.refs_6_, f32[1,640,256]{2,1,0:T(8,128)} %collective-permute-done.refs_5_, ...), custom_call_target="tpu_custom_call" | custom-call | flops 994050048 | bytes 3883008 | tf_op jit(solution)/shard_map/gamma/pallas_call | solution.py:267
  141.0 0.0 copy-start.1
  141.0 1.3 copy-done.1
  142.3 3.9 %all-to-all-done.3.refs_6_.refs_5_ = f32[16,32,128]{2,1,0:T(8,128)S(1)} async-done(((f32[16,32,128]{2,1,0:T(8,128)}), f32[16,32,128]{2,1,0:T(8,128)S(1)}, u32[]{:S(2)}, u32[]{:S(2)}) %all-to-all-start.3) | async-done | bytes 262176 | tf_op jit(solution)/shard_map/all_to_all | solution.py:301
  146.2 0.6 energy.3
  146.9 0.1 maximum_reduce_fusion
  147.0 0.1 stack.47
  147.1 12.0 %psum.7 = f32[8]{0:T(128)S(1)} all-reduce(f32[8]{0:T(128)S(1)} %maximum_reduce_fusion), channel_id=1, replica_groups=mesh['occ'=8,'aux'=16,'vir'=4] {'vir'}, use_global_device_ids=true, to_apply=%region_1.0 | all-reduce | flops 8 | bytes 64 | tf_op jit(solution)/shard_map/psum | solution.py:326
  159.0 0.6 select_reduce_fusion
  159.6 1.5 copy-done.2
  161.2 3.3 %gamma.3 = f32[632,768]{1,0:T(8,128)} custom-call(s32[2]{0:T(128)S(1)} %pad_add_fusion.ids_ref.refs_0_, s32[16]{0:T(128)S(1)} %reshape.19.refs_1_, f32[8]{0:T(128)S(1)} %copy-done.10, s32[8]{0:T(128)S(1)} %bitcast.38, f32[632,768]{1,0:T(8,128)S(1)} %copy-done.2, f32[16,32,128]{2,1,0:T(8,128)S(1)} %all-to-all-done.3.refs_6_.refs_5_, ...), custom_call_target="tpu_custom_call" | custom-call | flops 331350016 | bytes 3883008 | tf_op jit(solution)/shard_map/gamma/pallas_call | solution.py:267
  (11 shorter events, 0.0 us)
Async XLA Ops:
  13.6 1.5 copy-start
  15.8 19.4 %copy-start.14 = (s32[1,8,1,2]{1,3,2,0:T(2,128)S(1)}, s32[1,8,1,2]{1,3,2,0:T(2,128)}, u32[]{:S(2)}) copy-start(s32[1,8,1,2]{1,3,2,0:T(2,128)} %param.8) | copy-start | bytes 196
  15.8 19.5 %copy-start.10 = (f32[8]{0:T(128)S(1)}, f32[8]{0:T(128)}, u32[]{:S(2)}) copy-start(f32[8]{0:T(128)} %refs_2_.15) | copy-start | bytes 100
  15.8 19.6 %copy-start.11 = (s32[1,8]{1,0:T(1,128)S(1)}, s32[1,8]{1,0:T(1,128)}, u32[]{:S(2)}) copy-start(s32[1,8]{1,0:T(1,128)} %param.9) | copy-start | bytes 100
  19.6 0.9 copy-start.6
  20.4 0.8 copy-start.12
  20.4 1.0 copy-start.13
  21.5 13.9 %collective-permute-start = (f32[1,640,256]{2,1,0:T(8,128)}, f32[1,640,256]{2,1,0:T(8,128)}, u32[]{:S(2)}, u32[]{:S(2)}) collective-permute-start(f32[1,640,256]{2,1,0:T(8,128)} %get-tuple-element.42), channel_id=1, source_target_pairs={{0,64},{64,0},{128,192},{192,128},{256,320},{320,256},{384,448},{4... | collective-permute-start | bytes 1966088 | tf_op jit(solution)/shard_map/ppermute | solution.py:298
  23.7 23.9 %collective-permute-start.1 = (f32[1,640,256]{2,1,0:T(8,128)}, f32[1,640,256]{2,1,0:T(8,128)S(1)}, u32[]{:S(2)}, u32[]{:S(2)}) collective-permute-start(f32[1,640,256]{2,1,0:T(8,128)} %get-tuple-element.44), channel_id=1, source_target_pairs={{0,128},{64,192},{128,256},{192,320},{256,384},{320,448},{384,0},{... | collective-permute-start | bytes 1966088 | tf_op jit(solution)/shard_map/ppermute | solution.py:298
  26.9 21.0 %collective-permute-start.2 = (f32[1,640,256]{2,1,0:T(8,128)}, f32[1,640,256]{2,1,0:T(8,128)}, u32[]{:S(2)}, u32[]{:S(2)}) collective-permute-start(f32[1,640,256]{2,1,0:T(8,128)} %get-tuple-element.45), channel_id=1, source_target_pairs={{0,384},{64,448},{128,0},{192,64},{256,128},{320,192},{384,256},{4... | collective-permute-start | bytes 1966088 | tf_op jit(solution)/shard_map/ppermute | solution.py:298
  29.6 26.5 %collective-permute-start.3 = (f32[1,640,256]{2,1,0:T(8,128)}, f32[1,640,256]{2,1,0:T(8,128)}, u32[]{:S(2)}, u32[]{:S(2)}) collective-permute-start(f32[1,640,256]{2,1,0:T(8,128)} %get-tuple-element.46), channel_id=1, source_target_pairs={{0,192},{64,128},{128,320},{192,256},{256,448},{320,384},{384,64},... | collective-permute-start | bytes 1966088 | tf_op jit(solution)/shard_map/ppermute | solution.py:298
  33.2 26.6 %collective-permute-start.4 = (f32[1,640,256]{2,1,0:T(8,128)}, f32[1,640,256]{2,1,0:T(8,128)}, u32[]{:S(2)}, u32[]{:S(2)}) collective-permute-start(f32[1,640,256]{2,1,0:T(8,128)} %get-tuple-element.47), channel_id=1, source_target_pairs={{0,448},{64,384},{128,64},{192,0},{256,192},{320,128},{384,320},{4... | collective-permute-start | bytes 1966088 | tf_op jit(solution)/shard_map/ppermute | solution.py:298
  35.4 1.1 copy-start.7
  38.8 21.0 %all-to-all-start = ((f32[16,32,128]{2,1,0:T(8,128)}), f32[16,32,128]{2,1,0:T(8,128)S(1)}, u32[]{:S(2)}, u32[]{:S(2)}) async-start(f32[16,32,128]{2,1,0:T(8,128)} %exchange.4), calls=%async_computation | async-start | bytes 524288 | tf_op jit(solution)/shard_map/all_to_all | solution.py:301
  47.6 19.9 %copy-start.9 = (f32[768]{0:T(1024)S(1)}, f32[768]{0:T(1024)}, u32[]{:S(2)}) copy-start(f32[768]{0:T(1024)} %param.7) | copy-start | bytes 9220
  59.9 10.3 %copy-start.4 = (f32[1,640,256]{2,1,0:T(8,128)}, f32[1,640,256]{2,1,0:T(8,128)S(1)}, u32[]{:S(2)}) copy-start(f32[1,640,256]{2,1,0:T(8,128)S(1)} %get-tuple-element.53.refs_8_) | copy-start | bytes 1966084
  59.9 21.3 %collective-permute-start.5 = (f32[1,640,256]{2,1,0:T(8,128)}, f32[1,640,256]{2,1,0:T(8,128)}, u32[]{:S(2)}, u32[]{:S(2)}) collective-permute-start(f32[1,640,256]{2,1,0:T(8,128)} %copy-done.13), channel_id=1, source_target_pairs={{0,256},{64,320},{128,384},{192,448},{256,0},{320,64},{384,128},{4... | collective-permute-start | bytes 1966088 | tf_op jit(solution)/shard_map/ppermute | solution.py:298
  62.5 32.5 %collective-permute-start.6 = (f32[1,640,256]{2,1,0:T(8,128)}, f32[1,640,256]{2,1,0:T(8,128)}, u32[]{:S(2)}, u32[]{:S(2)}) collective-permute-start(f32[1,640,256]{2,1,0:T(8,128)} %copy-done.12), channel_id=1, source_target_pairs={{0,320},{64,256},{128,448},{192,384},{256,64},{320,0},{384,192},{4... | collective-permute-start | bytes 1966088 | tf_op jit(solution)/shard_map/ppermute | solution.py:298
  70.2 0.9 copy-start.3
  71.0 30.1 %all-to-all-start.1 = ((f32[16,96,128]{2,1,0:T(8,128)}), f32[16,96,128]{2,1,0:T(8,128)S(1)}, u32[]{:S(2)}, u32[]{:S(2)}) async-start(f32[16,96,128]{2,1,0:T(8,128)} %copy-done.3), calls=%async_computation.1 | async-start | bytes 1572864 | tf_op jit(solution)/shard_map/all_to_all | solution.py:301
  130.2 6.5 %copy-start.5 = (f32[1,640,256]{2,1,0:T(8,128)S(1)}, f32[1,640,256]{2,1,0:T(8,128)}, u32[]{:S(2)}) copy-start(f32[1,640,256]{2,1,0:T(8,128)} %copy-done.4) | copy-start | bytes 1966084
  131.6 14.7 %all-to-all-start.3 = ((f32[16,32,128]{2,1,0:T(8,128)}), f32[16,32,128]{2,1,0:T(8,128)S(1)}, u32[]{:S(2)}, u32[]{:S(2)}) async-start(f32[16,32,128]{2,1,0:T(8,128)} %exchange.7), calls=%async_computation.3 | async-start | bytes 524288 | tf_op jit(solution)/shard_map/all_to_all | solution.py:301
  136.7 1.1 copy-start.8
  141.0 1.3 copy-start.1
  159.6 1.5 copy-start.2
